TPU v7x, 32 devices: a whole 2x2x4 slice. The times are simulated.
32 devices in a mesh: groups: 2 (over y), space: 4 (over z), test: 4 (over x, core).
Axes of the slice: x: 2, y: 2, z: 4, core: 2. Of those that a mesh axis runs over, the one named last changes fastest.
Arguments:
- log_k: bfloat16 [384, 288, 128], P(('groups', 'space')), parts along dimension 0, may hold values from -1.5 to 1.5
- heads: bfloat16 [4, 384, 288, 128], P('test', ('groups', 'space')), parts along dimension 1, may hold values from -6 to 6
- warm_adjoint: bfloat16 [4, 384, 288, 128], P('test', ('groups', 'space')), parts along dimension 1, may hold values from -6 to 6
- obs_columns: int32 [4, 128], P('test', 'groups'), parts along dimension 1, may hold values from 0 to 55295
- obs_residuals: float32 [4, 128, 128], P('test', 'groups'), parts along dimension 1, may hold values from -18 to 18
- well_columns: int32 [8], P(('groups', 'test')), parts along dimension 0, may hold values from 0 to 55295
Outputs:
- prior_gradient: float32 [384, 288, 128], P(('groups', 'space'), 'test'), parts along dimension 0
There are 2 independent parts, one for each index of `groups`. A program takes and returns all parts, laid end to end along the dimension named above; each array names one. Nothing has to cross between parts.
Inputs may be any that keep to these rules, and one draw needn't show every extreme that they name: `obs_columns`: x * 288 + y of the borehole's cell column. `well_columns`: x * 288 + y of the well's cell column.
All inputs are finite; a program needn't handle non-finite values.
Results may differ from a plain program's by a relative error of at most 0.0003.
Values may be sent and summed in bfloat16 or wider, within the bound.
No kernel may reach another device: no remote copies, remote signals or barrier semaphores. Data moves between devices by JAX's collectives and lax.ppermute only.
A program may use at most 128 MiB of HBM per device.

v0:
```python
import jax
import jax.numpy as jnp
from jax import lax
from jax.sharding import PartitionSpec as P

ITERS = 2


prior_gain = 5.0
range_squared = 4.0


def with_halo(cells, sides, width):
    for axis, dim in sides:
        count = lax.axis_size(axis)
        ends = count - 1
        head = lax.slice_in_dim(cells, 0, width, axis=dim)
        tail = lax.slice_in_dim(cells, cells.shape[dim] - width, cells.shape[dim], axis=dim)
        cells = jnp.concatenate(
            [
                lax.ppermute(tail, axis, [(i, (i + 1) % count) for i in range(ends)]),
                cells,
                lax.ppermute(head, axis, [((i + 1) % count, i) for i in range(ends)]),
            ],
            axis=dim,
        )
    return cells


def neighbours(padded):
    return [
        padded[2:, 1:-1, 1:-1],
        padded[:-2, 1:-1, 1:-1],
        padded[1:-1, 2:, 1:-1],
        padded[1:-1, :-2, 1:-1],
        padded[1:-1, 1:-1, 2:],
        padded[1:-1, 1:-1, :-2],
    ]


def operate(values, padded, conduct):
    summed = jnp.zeros_like(values)
    for face_k, beside in zip(conduct, neighbours(padded)):
        summed = summed + face_k * (values - beside)
    return summed


def kappa_of(indices, length):
    return 4.0 * jnp.sin(jnp.pi * indices / length) ** 2


def pad_sides(padded):
    return jnp.pad(padded, ((0, 0), (1, 1), (1, 1)))


def with_faces(values):
    return pad_sides(with_halo(values, (("space", 0),), 1))


def squares(residual):
    return lax.psum(jnp.sum(residual * residual), "space")


def hartley(length):
    indices = jnp.arange(length, dtype=jnp.int32)
    products = indices[:, None] * indices[None, :] % length
    angles = products.astype(jnp.float32) * (2.0 * jnp.pi / length)
    return jnp.cos(angles) + jnp.sin(angles)


def on_device(log_k, heads, warm_adjoint, obs_columns, obs_residuals, well_columns):
    slab_rows, width_cells, depth_cells = log_k.shape
    space_count = lax.axis_size("space")
    first_row = lax.axis_index("space") * slab_rows
    logk_pad, head_pad = (
        with_halo(log_k, (("space", 0),), 1),
        with_halo(heads[0], (("space", 0),), 1),
    )
    logk_val = log_k.astype(jnp.float32)
    conduct = [
        jnp.exp(0.5 * (logk_val + beside))
        for beside in neighbours(pad_sides(logk_pad.astype(jnp.float32)))
    ]
    columns = obs_columns[0]
    row_local = columns // width_cells - first_row
    inside = (row_local >= 0) & (row_local < slab_rows)
    row_local = jnp.where(inside, row_local, slab_rows)
    source = jnp.zeros((slab_rows, width_cells, depth_cells), jnp.float32)
    source = source.at[row_local, columns % width_cells].add(obs_residuals[0], mode="drop")
    adjoint = warm_adjoint[0].astype(jnp.float32)
    lam_padded = with_faces(adjoint)
    residual = source - operate(adjoint, lam_padded, conduct)
    direction = residual
    norm_now = squares(residual)
    for iteration in range(ITERS):
        dir_padded = with_faces(direction)
        applied = operate(direction, dir_padded, conduct)
        step_length = norm_now / lax.psum(jnp.sum(direction * applied), "space")
        adjoint = adjoint + step_length * direction
        lam_padded = lam_padded + step_length * dir_padded
        if iteration + 1 < ITERS:
            residual = residual - step_length * applied
            norm_next = squares(residual)
            direction = residual + norm_next / norm_now * direction
            norm_now = norm_next
    lam_full = pad_sides(with_halo(adjoint, (("space", 0),), 1))
    head_val = heads[0].astype(jnp.float32)
    misfit_term = jnp.zeros_like(adjoint)
    for face_k, lam_side, head_side in zip(
        conduct, neighbours(lam_full), neighbours(pad_sides(head_pad.astype(jnp.float32)))
    ):
        misfit_term = misfit_term + face_k * (adjoint - lam_side) * (head_val - head_side)
    column_ids = (first_row + jnp.arange(slab_rows, dtype=jnp.int32))[
        :, None
    ] * width_cells + jnp.arange(width_cells, dtype=jnp.int32)[None, :]
    keep_mask = (column_ids != well_columns[0]).astype(jnp.float32)
    partial_value = -0.5 * misfit_term * keep_mask[:, :, None]
    highest = lax.Precision.HIGHEST
    cas_depth = hartley(depth_cells)
    cas_across = hartley(width_cells)
    along_cells = slab_rows * space_count
    cas_along = hartley(along_cells)
    summed = lax.psum_scatter(partial_value, "test", scatter_dimension=1, tiled=True)
    depth_freq = jnp.einsum("xyz,zk->xky", summed, cas_depth, precision=highest)
    pencil = lax.all_to_all(depth_freq, "test", split_axis=1, concat_axis=2, tiled=True)
    across_freq = jnp.einsum("xzy,yk->kzx", pencil, cas_across, precision=highest)
    column_block = lax.all_to_all(across_freq, "space", split_axis=0, concat_axis=2, tiled=True)
    along_freq = jnp.einsum("yzx,xk->yzk", column_block, cas_along, precision=highest)
    across_rows = column_block.shape[0]
    depth_rows = column_block.shape[1]
    kappa_x = kappa_of(jnp.arange(along_cells).astype(jnp.float32), along_cells)
    kappa_y = kappa_of(
        (lax.axis_index("space") * across_rows + jnp.arange(across_rows)).astype(jnp.float32),
        width_cells,
    )
    kappa_z = kappa_of(
        (lax.axis_index("test") * depth_rows + jnp.arange(depth_rows)).astype(jnp.float32),
        depth_cells,
    )
    spectrum = (
        prior_gain
        / (
            1.0
            + range_squared
            * (kappa_y[:, None, None] + kappa_z[None, :, None] + kappa_x[None, None, :])
        )
        ** 2
    )
    along_back = jnp.einsum("yzk,kx->yzx", along_freq * spectrum, cas_along, precision=highest)
    slab_block = lax.all_to_all(along_back, "space", split_axis=2, concat_axis=0, tiled=True)
    across_back = jnp.einsum("yzx,yk->xzk", slab_block, cas_across, precision=highest)
    depth_block = lax.all_to_all(across_back, "test", split_axis=2, concat_axis=1, tiled=True)
    result = jnp.einsum("xky,kz->xyz", depth_block, cas_depth, precision=highest)
    scale_back = 1.0 / (along_cells * width_cells * depth_cells)
    return result * scale_back


def solution(mesh):
    placed = (
        P(("groups", "space"), None, None),
        P("test", ("groups", "space"), None, None),
        P("test", ("groups", "space"), None, None),
        P("test", "groups"),
        P("test", "groups", None),
        P(("groups", "test")),
    )
    return jax.shard_map(
        on_device,
        mesh=mesh,
        in_specs=placed,
        out_specs=P(("groups", "space"), "test", None),
        check_vma=False,
    )
```

profile of v0, /device:TPU:0, one launch (start us, length us, event | category | flops | bytes accessed | tf_op | source)
XLA Modules:
  0.0 745.9 jit_solution(16803509805105050348)
XLA Ops:
  6.5 6.0 fusion.156
  14.6 6.2 collective-permute-start.3
  30.4 8.2 %scatter_fusion = f32[48,288,128]{2,1,0:T(8,128)} fusion(f32[48,288,128]{2,1,0:T(8,128)} %broadcast_in_dim.4, s32[64]{0:T(128)S(1)} %fusion.127, f32[64,128]{1,0:T(8,128)} %bitcast.94), kind=kCustom, calls=%fused_computation | custom fusion | flops 8192 | bytes 98816 | tf_op jit(solution)/shard_map/scatter-add | solution.py:89
  40.1 15.6 %select_maximum_fusion.6 = f32[50,290,130]{2,1,0:T(8,128)} fusion(f32[1,288,128]{2,1,0:T(8,128)} %collective-permute-done.2, f32[48,288,128]{2,1,0:T(8,128)} %get-tuple-element.21, f32[1,288,128]{2,1,0:T(8,128)} %collective-permute-done.3), kind=kLoop, calls=%fused_computation.31 | loop fusion | flops 28275000 | bytes 14912800 | tf_op jit(solution)/shard_map/concatenate | solution.py:19
  55.7 39.1 %fusion.65 = f32[48,288,128]{2,1,0:T(8,128)} fusion(f32[48,288,128]{2,1,0:T(8,128)} %scatter_fusion, f32[48,288,128]{2,1,0:T(8,128)} %get-tuple-element.21, f32[50,290,130]{2,1,0:T(8,128)} %select_maximum_fusion.6, f32[1,288,128]{2,1,0:T(8,128)} %collective-permute-done.3, f32[1,288,128]{2,1,0:T(8,128)} %collective-permute-done.2, ...), kind=kLoop, calls=%fused_computation.117 | loop fusion | flops 58392576 | bytes 74907648 | tf_op jit(solution)/shard_map/sub | solution.py:92
  97.1 5.9 collective-permute-start.5
  105.1 13.9 %select_maximum_fusion.4 = f32[50,290,130]{2,1,0:T(8,128)} fusion(f32[1,288,128]{2,1,0:T(8,128)S(1)} %collective-permute-done.4, f32[48,288,128]{2,1,0:T(8,128)} %fusion.65, f32[1,288,128]{2,1,0:T(8,128)S(1)} %collective-permute-done.5), kind=kLoop, calls=%fused_computation.29 | loop fusion | flops 28275000 | bytes 14912800 | tf_op jit(solution)/shard_map/concatenate | solution.py:19
  119.0 36.6 %multiply_reduce_fusion.1 = (f32[]{:T(128)}, f32[]{:T(128)}, f32[48,288,128]{2,1,0:T(8,128)}) fusion(f32[48,288,128]{2,1,0:T(8,128)} %fusion.65, f32[50,290,130]{2,1,0:T(8,128)} %select_maximum_fusion.4, f32[50,288,128]{2,1,0:T(8,128)S(1)} %maximum_convert_fusion, f32[1,288,128]{2,1,0:T(8,128)S(1)} %collective-permute-done.5, ...), kind=kLoop, calls=%fused_computation.138 | loop fusion | flops 63700992 | bytes 67829768 | tf_op jit(solution)/shard_map/reduce_sum | solution.py:98
  155.6 14.0 %all-reduce.6 = (f32[]{:T(128)}, f32[]{:T(128)}) all-reduce(f32[]{:T(128)} %get-tuple-element.6, f32[]{:T(128)} %get-tuple-element.5), channel_id=1, replica_groups=mesh['groups'=2,'space'=4,'test'=4] {'space'}, use_global_device_ids=true, to_apply=%region_2.3 | all-reduce | flops 2 | bytes 16 | tf_op jit(solution)/shard_map/psum | solution.py:61
  171.0 7.4 multiply_reduce_fusion
  178.5 9.0 %psum.30 = f32[]{:T(128)} all-reduce(f32[]{:T(128)} %multiply_reduce_fusion), channel_id=1, replica_groups=mesh['groups'=2,'space'=4,'test'=4] {'space'}, use_global_device_ids=true, to_apply=%region_6.7 | all-reduce | flops 1 | bytes 8 | tf_op jit(solution)/shard_map/psum | solution.py:61
  188.9 6.4 multiply_add_fusion.1
  211.4 10.4 %select_maximum_fusion.2 = f32[50,290,130]{2,1,0:T(8,128)} fusion(f32[1,288,128]{2,1,0:T(8,128)S(1)} %collective-permute-done.6, f32[48,288,128]{2,1,0:T(8,128)S(1)} %multiply_add_fusion.1, f32[1,288,128]{2,1,0:T(8,128)S(1)} %collective-permute-done.7), kind=kLoop, calls=%fused_computation.27 | loop fusion | flops 28275000 | bytes 14912800 | tf_op jit(solution)/shard_map/concatenate | solution.py:19
  221.8 51.6 %fusion.38 = f32[]{:T(128)} fusion(f32[48,288,128]{2,1,0:T(8,128)} %copy-done.3, f32[50,290,130]{2,1,0:T(8,128)} %select_maximum_fusion.2, f32[1,288,128]{2,1,0:T(8,128)} %copy-done.7, f32[1,288,128]{2,1,0:T(8,128)} %copy-done.5, f32[50,288,128]{2,1,0:T(8,128)} %copy-done, bf16[48,288,128]{2,1,0:T(8,128)(2,1)S(1)} %copy-done.1), kind=kLoop, calls=%fused_computation.78 | loop fusion | flops 60162048 | bytes 60751876 | tf_op jit(solution)/shard_map/reduce_sum | solution.py:98
  274.1 10.3 %psum.31 = f32[]{:T(128)} all-reduce(f32[]{:T(128)} %fusion.38), channel_id=1, replica_groups=mesh['groups'=2,'space'=4,'test'=4] {'space'}, use_global_device_ids=true, to_apply=%region_8.9 | all-reduce | flops 1 | bytes 8 | tf_op jit(solution)/shard_map/psum | solution.py:98
  285.8 7.3 multiply_add_fusion
  303.4 10.4 %select_maximum_fusion = f32[50,290,130]{2,1,0:T(8,128)} fusion(f32[1,288,128]{2,1,0:T(8,128)S(1)} %collective-permute-done.8, f32[48,288,128]{2,1,0:T(8,128)S(1)} %multiply_add_fusion, f32[1,288,128]{2,1,0:T(8,128)S(1)} %collective-permute-done.11), kind=kLoop, calls=%fused_computation.25 | loop fusion | flops 28275000 | bytes 14912800 | tf_op jit(solution)/shard_map/concatenate | solution.py:19
  313.8 70.3 %fusion.21 = f32[48,288,128]{2,1,0:T(8,128)} fusion(f32[50,288,128]{2,1,0:T(8,128)} %maximum_convert_fusion.1, f32[48,288,128]{2,1,0:T(8,128)} %copy-done.2, f32[50,290,130]{2,1,0:T(8,128)} %select_maximum_fusion, f32[1,288,128]{2,1,0:T(8,128)} %copy-done.6, f32[1,288,128]{2,1,0:T(8,128)} %copy-done.8, f32[48,288]{1,0:T(8,128)} %fusion.116, ...), kind=kLoop, calls=%fused_computation.54 | loop fusion | flops 81395712 | bytes 92971008 | tf_op jit(solution)/shard_map/mul | solution.py:117
  384.1 63.6 %reduce-scatter.2.cloned.1.call-done = f32[48,72,128]{2,1,0:T(8,128)} async-done(((f32[48,288,128]{2,1,0:T(8,128)}), f32[48,72,128]{2,1,0:T(8,128)}) %reduce-scatter.2.cloned.1.call-update) | async-done | bytes 1769488 | tf_op jit(solution)/shard_map/reduce_scatter | solution.py:123
  454.5 39.9 %all_to_all.72 = f32[48,128,72]{2,0,1:T(8,128)S(1)} all-to-all(f32[48,128,72]{2,0,1:T(8,128)S(1)} %copy.29), channel_id=1, replica_groups=mesh['groups'=2,'space'=4,'test'=4] {'test'}, dimensions={1} | all-to-all | bytes 3538944 | tf_op jit(solution)/shard_map/all_to_all | solution.py:125
  499.0 7.8 %convolution_bitcast_fusion = f32[288,32,48]{0,2,1:T(8,128)S(1)} fusion(f32[48,32,288]{2,0,1:T(8,128)} %all_to_all.55), kind=kOutput, calls=%fused_computation.150 | convolution fusion | flops 1529653248 | bytes 3538944 | tf_op jit(solution)/shard_map/xzy,yk->kzx/dot_general | solution.py:126
  506.8 5.5 copy.32
  512.3 6.9 reshape.202
  524.8 39.9 %all-to-all-done.1 = f32[4,1,110592]{2,1,0:T(1,128)S(1)} async-done(((f32[4,1,110592]{2,1,0:T(1,128)}), f32[4,1,110592]{2,1,0:T(1,128)S(1)}, u32[]{:S(2)}, u32[]{:S(2)}) %all-to-all-start.1) | async-done | bytes 1769504 | tf_op jit(solution)/shard_map/all_to_all | solution.py:127
  565.3 5.8 reduce
  595.0 73.1 %all_to_all.73 = f32[72,32,192]{0,1,2:T(8,128)S(1)} all-to-all(f32[72,32,192]{0,1,2:T(8,128)S(1)} %copy.35), channel_id=1, replica_groups=mesh['groups'=2,'space'=4,'test'=4] {'space'}, dimensions={2} | all-to-all | bytes 3538944 | tf_op jit(solution)/shard_map/all_to_all | solution.py:150
  672.8 7.8 %fusion.95 = f32[288,1536]{0,1:S(1)} fusion(f32[288,1536]{0,1:T(8,128)} %reshape.199), kind=kOutput, calls=%fused_computation.168 | convolution fusion | flops 1529653248 | bytes 3538944
  686.1 5.9 reshape.204
  692.0 24.8 %all_to_all.74 = f32[4,1,110592]{2,1,0:T(1,128)S(1)} all-to-all(f32[4,1,110592]{2,1,0:T(1,128)S(1)} %reshape.204), channel_id=1, replica_groups=mesh['groups'=2,'space'=4,'test'=4] {'test'}, dimensions={0} | all-to-all | bytes 3538944 | tf_op jit(solution)/shard_map/all_to_all | solution.py:152
  716.8 5.8 reduce.1
  726.9 5.5 copy.39
  732.5 6.3 convolution_multiply_fusion
  (78 shorter events, 99.7 us)
Async XLA Ops:
  6.5 14.2 %copy-start.1 = (bf16[48,288,128]{2,1,0:T(8,128)(2,1)S(1)}, bf16[48,288,128]{2,1,0:T(8,128)(2,1)}, u32[]{:S(2)}) copy-start(bf16[48,288,128]{2,1,0:T(8,128)(2,1)} %param.6) | copy-start | bytes 10616836
  6.5 20.1 %copy-start.10 = (s32[1,64]{1,0:T(1,128)S(1)}, s32[1,64]{1,0:T(1,128)}, u32[]{:S(2)}) copy-start(s32[1,64]{1,0:T(1,128)} %param.9) | copy-start | bytes 772
  6.5 441.1 %reduce-scatter.2.cloned.1.call-start = ((), (), s32[]{:S(2)}) async-start(), calls=%async_computation.5 | async-start | bytes 8847360 | tf_op jit(solution)/shard_map/reduce_scatter | solution.py:123
  13.3 26.8 %collective-permute-start.2 = (f32[1,288,128]{2,1,0:T(8,128)}, f32[1,288,128]{2,1,0:T(8,128)}, u32[]{:S(2)}, u32[]{:S(2)}) collective-permute-start(f32[1,288,128]{2,1,0:T(8,128)} %get-tuple-element.17), channel_id=1, source_target_pairs={{4,0},{8,4},{12,8},{5,1},{9,5},{13,9},{6,2},{10,6},{14,10},{7,3},{... | collective-permute-start | bytes 442376 | tf_op jit(solution)/shard_map/ppermute | solution.py:23
  14.6 25.6 %collective-permute-start.3 = (f32[1,288,128]{2,1,0:T(8,128)}, f32[1,288,128]{2,1,0:T(8,128)}, u32[]{:S(2)}, u32[]{:S(2)}) collective-permute-start(f32[1,288,128]{2,1,0:T(8,128)} %get-tuple-element.16), channel_id=1, source_target_pairs={{0,4},{4,8},{8,12},{1,5},{5,9},{9,13},{2,6},{6,10},{10,14},{3,7},{... | collective-permute-start | bytes 442376 | tf_op jit(solution)/shard_map/ppermute | solution.py:21
  21.4 17.2 %collective-permute-start = (bf16[1,288,128]{2,1,0:T(8,128)(2,1)}, bf16[1,288,128]{2,1,0:T(8,128)(2,1)}, u32[]{:S(2)}, u32[]{:S(2)}) collective-permute-start(bf16[1,288,128]{2,1,0:T(8,128)(2,1)} %get-tuple-element.18), channel_id=1, source_target_pairs={{0,4},{4,8},{8,12},{1,5},{5,9},{9,13},{2,6},{6,10},{10,14},{3,7},{... | collective-permute-start | bytes 221192 | tf_op jit(solution)/shard_map/ppermute | solution.py:21
  25.3 13.3 %collective-permute-start.1 = (bf16[1,288,128]{2,1,0:T(8,128)(2,1)}, bf16[1,288,128]{2,1,0:T(8,128)(2,1)}, u32[]{:S(2)}, u32[]{:S(2)}) collective-permute-start(bf16[1,288,128]{2,1,0:T(8,128)(2,1)} %get-tuple-element.19), channel_id=1, source_target_pairs={{4,0},{8,4},{12,8},{5,1},{9,5},{13,9},{6,2},{10,6},{14,10},{7,3},{... | collective-permute-start | bytes 221192 | tf_op jit(solution)/shard_map/ppermute | solution.py:23
  40.1 79.0 %copy-start = (f32[50,288,128]{2,1,0:T(8,128)}, f32[50,288,128]{2,1,0:T(8,128)S(1)}, u32[]{:S(2)}) copy-start(f32[50,288,128]{2,1,0:T(8,128)S(1)} %maximum_convert_fusion) | copy-start | bytes 22118404
  95.8 7.8 %collective-permute-start.4 = (f32[1,288,128]{2,1,0:T(8,128)S(1)}, f32[1,288,128]{2,1,0:T(8,128)S(1)}, u32[]{:S(2)}, u32[]{:S(2)}) collective-permute-start(f32[1,288,128]{2,1,0:T(8,128)S(1)} %get-tuple-element.15), channel_id=1, source_target_pairs={{4,0},{8,4},{12,8},{5,1},{9,5},{13,9},{6,2},{10,6},{14,10},{7,3},{... | collective-permute-start | bytes 442376 | tf_op jit(solution)/shard_map/ppermute | solution.py:23
  97.1 8.0 %collective-permute-start.5 = (f32[1,288,128]{2,1,0:T(8,128)S(1)}, f32[1,288,128]{2,1,0:T(8,128)S(1)}, u32[]{:S(2)}, u32[]{:S(2)}) collective-permute-start(f32[1,288,128]{2,1,0:T(8,128)S(1)} %get-tuple-element.14), channel_id=1, source_target_pairs={{0,4},{4,8},{8,12},{1,5},{5,9},{9,13},{2,6},{6,10},{10,14},{3,7},{... | collective-permute-start | bytes 442376 | tf_op jit(solution)/shard_map/ppermute | solution.py:21
  195.3 14.8 %copy-start.3 = (f32[48,288,128]{2,1,0:T(8,128)}, f32[48,288,128]{2,1,0:T(8,128)S(1)}, u32[]{:S(2)}) copy-start(f32[48,288,128]{2,1,0:T(8,128)S(1)} %multiply_add_fusion.1) | copy-start | bytes 21233668
  195.3 14.7 %collective-permute-start.6 = (f32[1,288,128]{2,1,0:T(8,128)S(1)}, f32[1,288,128]{2,1,0:T(8,128)S(1)}, u32[]{:S(2)}, u32[]{:S(2)}) collective-permute-start(f32[1,288,128]{2,1,0:T(8,128)S(1)} %get-tuple-element.13), channel_id=1, source_target_pairs={{4,0},{8,4},{12,8},{5,1},{9,5},{13,9},{6,2},{10,6},{14,10},{7,3},{... | collective-permute-start | bytes 442376 | tf_op jit(solution)/shard_map/ppermute | solution.py:23
  196.6 13.5 %collective-permute-start.7 = (f32[1,288,128]{2,1,0:T(8,128)S(1)}, f32[1,288,128]{2,1,0:T(8,128)S(1)}, u32[]{:S(2)}, u32[]{:S(2)}) collective-permute-start(f32[1,288,128]{2,1,0:T(8,128)S(1)} %get-tuple-element.12), channel_id=1, source_target_pairs={{0,4},{4,8},{8,12},{1,5},{5,9},{9,13},{2,6},{6,10},{10,14},{3,7},{... | collective-permute-start | bytes 442376 | tf_op jit(solution)/shard_map/ppermute | solution.py:21
  202.8 94.4 %collective-permute-start.10 = (bf16[1,288,128]{2,1,0:T(8,128)(2,1)}, bf16[1,288,128]{2,1,0:T(8,128)(2,1)}, u32[]{:S(2)}, u32[]{:S(2)}) collective-permute-start(bf16[1,288,128]{2,1,0:T(8,128)(2,1)} %get-tuple-element.23), channel_id=1, source_target_pairs={{4,0},{8,4},{12,8},{5,1},{9,5},{13,9},{6,2},{10,6},{14,10},{7,3},{... | collective-permute-start | bytes 221192 | tf_op jit(solution)/shard_map/ppermute | solution.py:23
  204.1 93.1 %collective-permute-start.9 = (bf16[1,288,128]{2,1,0:T(8,128)(2,1)}, bf16[1,288,128]{2,1,0:T(8,128)(2,1)}, u32[]{:S(2)}, u32[]{:S(2)}) collective-permute-start(bf16[1,288,128]{2,1,0:T(8,128)(2,1)} %get-tuple-element.22), channel_id=1, source_target_pairs={{0,4},{4,8},{8,12},{1,5},{5,9},{9,13},{2,6},{6,10},{10,14},{3,7},{... | collective-permute-start | bytes 221192 | tf_op jit(solution)/shard_map/ppermute | solution.py:21
  210.1 0.7 copy-start.5
  210.7 0.7 copy-start.7
  285.8 11.4 %copy-start.4 = (bf16[1,48,288,128]{3,2,1,0:T(8,128)(2,1)S(1)}, bf16[1,48,288,128]{3,2,1,0:T(8,128)(2,1)}, u32[]{:S(2)}) copy-start(bf16[1,48,288,128]{3,2,1,0:T(8,128)(2,1)} %param.7) | copy-start | bytes 10616836
  293.1 9.6 %copy-start.2 = (f32[48,288,128]{2,1,0:T(8,128)}, f32[48,288,128]{2,1,0:T(8,128)S(1)}, u32[]{:S(2)}) copy-start(f32[48,288,128]{2,1,0:T(8,128)S(1)} %multiply_add_fusion) | copy-start | bytes 21233668
  293.1 8.5 %collective-permute-start.11 = (f32[1,288,128]{2,1,0:T(8,128)S(1)}, f32[1,288,128]{2,1,0:T(8,128)S(1)}, u32[]{:S(2)}, u32[]{:S(2)}) collective-permute-start(f32[1,288,128]{2,1,0:T(8,128)S(1)} %get-tuple-element.10), channel_id=1, source_target_pairs={{0,4},{4,8},{8,12},{1,5},{5,9},{9,13},{2,6},{6,10},{10,14},{3,7},{... | collective-permute-start | bytes 442376 | tf_op jit(solution)/shard_map/ppermute | solution.py:21
  295.6 7.0 collective-permute-start.8
  301.6 1.1 copy-start.6
  302.7 0.7 copy-start.8
  519.2 45.6 %all-to-all-start.1 = ((f32[4,1,110592]{2,1,0:T(1,128)}), f32[4,1,110592]{2,1,0:T(1,128)S(1)}, u32[]{:S(2)}, u32[]{:S(2)}) async-start(f32[4,1,110592]{2,1,0:T(1,128)} %reshape.202), calls=%async_computation.2 | async-start | bytes 3538944 | tf_op jit(solution)/shard_map/all_to_all | solution.py:127
  579.1 7.6 %copy-start.9 = (f32[72,32]{1,0:T(8,128)S(1)}, f32[72,32]{1,0:T(8,128)}, u32[]{:S(2)}) copy-start(f32[72,32]{1,0:T(8,128)} %broadcast_add_fusion) | copy-start | bytes 27652
Sparse Core Ops, SparseCore 0:
  384.2 63.3 reduce-scatter.1
where the time goes:
time: 755 us; the launch traced here: 746 us
  other arithmetic  302 us (40%)
  blocking collectives  171 us (23%)
  waiting for transfers between devices  107 us (14%)
  local copies, waits for them, and re-layouts  70.3 us (9%)
  starting transfers between devices  41.1 us (5%)
  matrix products  35.6 us (5%)
  between operations  18.7 us (2%)
    reduce_sum x2, other arithmetic, on_device(): step_length = norm_now / lax.psum(jnp.sum(direction * applied), 'space')  88.2 us
    all_to_all x1, blocking collectives, on_device(): lax.all_to_all(along_back, 'space', split_axis=2, concat_axis=0, tiled=True)  73.1 us
    mul x2, other arithmetic, on_device(): partial_value = -0.5 * misfit_term * keep_mask[:, :, None]  71 us
    reduce_scatter x1, waiting for transfers between devices, on_device(): lax.psum_scatter(partial_value, 'test', scatter_dimension=1, tiled=True)  63.6 us
    concatenate x4, other arithmetic, with_halo(): jnp.concatenate([lax.ppermute(tail, axis, [(i, (i + 1) % count) for i in...  50.4 us
    all_to_all x1, waiting for transfers between devices, on_device(): lax.all_to_all(across_freq, 'space', split_axis=0, concat_axis=2, tiled=T...  39.9 us
    all_to_all x1, blocking collectives, on_device(): lax.all_to_all(depth_freq, 'test', split_axis=1, concat_axis=2, tiled=True)  39.9 us
    sub x1, other arithmetic, on_device(): residual = source - operate(adjoint, lam_padded, conduct)  39.1 us
  transfers between devices with their start and end apart: 14, of which 5 were waited for; matrix products, arithmetic and copies ran while one was open for 12% of the time, Pallas kernels for 0%

commit v1 on v0

v1 whole, which is shorter than its diff:
```python
import functools

import jax
import jax.numpy as jnp
import ml_dtypes
import numpy as np
from jax import lax
from jax.experimental import pallas as pl
from jax.experimental.pallas import tpu as pltpu
from jax.sharding import PartitionSpec as P

prior_gain = 5.0
range_squared = 4.0

HALO = 3
PAD = 8
F32 = jnp.float32
BF16 = jnp.bfloat16
VMEM_LIMIT = 60 * 1024 * 1024

SMEM_SPEC = pl.BlockSpec(memory_space=pltpu.SMEM)
VMEM_SPEC = pl.BlockSpec(memory_space=pltpu.VMEM)
ANY_SPEC = pl.BlockSpec(memory_space=pl.ANY)


def cas(length):
    index = np.arange(length)
    angle = 2.0 * np.pi * (index[:, None] * index[None, :] % length) / length
    return np.cos(angle) + np.sin(angle)


def halves(table):
    table = np.asarray(table, np.float32)
    high = table.astype(ml_dtypes.bfloat16)
    low = (table - high.astype(np.float32)).astype(ml_dtypes.bfloat16)
    return high, low


def kappa(length):
    return 4.0 * np.sin(np.pi * np.arange(length) / length) ** 2


def split(value):
    high = value.astype(BF16)
    low = (value - high.astype(F32)).astype(BF16)
    return high, low


def dot(left, right):
    return lax.dot_general(left, right, (((1,), (0,)), ((), ())), preferred_element_type=F32)


def dot3(left, right):
    return dot(left[0], right[0]) + (dot(left[0], right[1]) + dot(left[1], right[0]))


def block_rows(count):
    for rows in (48, 32, 16):
        if count % rows == 0:
            return rows
    return count


def lane_index(shape):
    return lax.broadcasted_iota(jnp.int32, shape, 1)


def window(ref, start, rows):
    return ref.at[pl.ds(pl.multiple_of(start - PAD, 8), rows + 2 * PAD)]


def neighbour_sum(ref, start, rows, plane, fill):
    near = window(ref, start, rows)
    here = near[PAD : PAD + rows]
    lanes = lane_index(here.shape)
    depth = here.shape[1]
    up = jnp.where(lanes == depth - 1, fill, pltpu.roll(here, depth - 1, 1))
    down = jnp.where(lanes == 0, fill, pltpu.roll(here, 1, 1))
    along = ref[pl.ds(pl.multiple_of(start - plane, 8), rows)] + ref[pl.ds(pl.multiple_of(start + plane, 8), rows)]
    across = near[PAD - 1 : PAD - 1 + rows] + near[PAD + 1 : PAD + 1 + rows]
    return along + across + (up + down), here


def fold(value):
    return jnp.sum(value.reshape(-1, 8, value.shape[1]), axis=0)


def moments_kernel(
    rows, ny, count_x,
    meta, columns, residuals, lk_low, lk, lk_high, w_low, w, w_high,
    v_out, q_out, mom_out,
    lk_buf, w_buf, e_ref, u_ref, v_ref, s_ref, r_ref, sems,
):
    depth = lk.shape[2]
    plane = ny + PAD
    planes = rows + 2 * HALO
    size = block_rows(ny)
    blocks = [i * size for i in range(ny // size)]
    first_row = meta[0]

    copies = []
    for index, (low, mid, high, buf) in enumerate(
        ((lk_low, lk, lk_high, lk_buf), (w_low, w, w_high, w_buf))
    ):
        copies += [
            pltpu.make_async_copy(low, buf.at[pl.ds(0, HALO)], sems.at[3 * index]),
            pltpu.make_async_copy(mid, buf.at[pl.ds(HALO, rows)], sems.at[3 * index + 1]),
            pltpu.make_async_copy(high, buf.at[pl.ds(HALO + rows, HALO)], sems.at[3 * index + 2]),
        ]
    for copy in copies:
        copy.start()

    ones = jnp.ones((PAD, depth), F32)
    zeros = jnp.zeros((PAD, depth), F32)

    def clear(p, carry):
        at = pl.ds(pl.multiple_of(p * plane, 8), PAD)
        e_ref[at] = ones
        u_ref[at] = zeros
        v_ref[at] = zeros
        return carry

    lax.fori_loop(0, planes, clear, 0)
    last = pl.ds(planes * plane, PAD)
    e_ref[last] = ones
    u_ref[last] = zeros
    v_ref[last] = zeros

    for copy in copies:
        copy.wait()

    def scale(p, carry):
        base = p * plane + PAD
        for b in blocks:
            e = jnp.exp(0.5 * lk_buf[p, b : b + size].astype(F32))
            at = pl.ds(pl.multiple_of(base + b, 8), size)
            e_ref[at] = e
            u_ref[at] = e * w_buf[p, b : b + size].astype(F32)
        return carry

    lax.fori_loop(0, planes, scale, 0)

    def inside(p):
        row = first_row + p - HALO
        return jnp.where((row >= 0) & (row < count_x), 1.0, 0.0).astype(F32)

    def residual(p, carry):
        base = p * plane + PAD
        valid = inside(p)
        for b in blocks:
            start = base + b
            at = pl.ds(pl.multiple_of(start, 8), size)
            flat = pl.ds(pl.multiple_of(p * ny + b, 8), size)
            s, e = neighbour_sum(e_ref, start, size, plane, 1.0)
            n, u = neighbour_sum(u_ref, start, size, plane, 0.0)
            r = (e * n - s * u) * valid
            s_ref[flat] = s
            r_ref[flat] = r
            v_ref[at] = e * r
        return carry

    lax.fori_loop(1, planes - 1, residual, 0)

    def plant(o, carry):
        column = columns[o]
        row = lax.div(column, ny)
        y = column - row * ny
        p = row - first_row + HALO

        @pl.when((p >= 1) & (p < planes - 1))
        def _():
            at = pl.ds(p * plane + PAD + y, 1)
            flat = pl.ds(p * ny + y, 1)
            added = residuals[pl.ds(o, 1)]
            r_ref[flat] = r_ref[flat] + added
            v_ref[at] = v_ref[at] + e_ref[at] * added

        return carry

    lax.fori_loop(0, columns.shape[0], plant, 0)
    extent = (rows + 2) * plane
    v_copy = pltpu.make_async_copy(v_ref.at[pl.ds(2 * plane, extent)], v_out, sems.at[6])
    v_copy.start()

    def image(p, sums, valid, summed):
        m0, m1, m2 = sums
        base = p * plane + PAD
        for b in blocks:
            start = base + b
            at = pl.ds(pl.multiple_of(start, 8), size)
            flat = pl.ds(pl.multiple_of(p * ny + b, 8), size)
            n, v = neighbour_sum(v_ref, start, size, plane, 0.0)
            e = e_ref[at]
            y = s_ref[flat] * v - e * n
            if valid is not None:
                y = y * valid
            u_ref[at] = e * y
            if summed:
                r = r_ref[flat]
                m0 = m0 + fold(r * r)
                m1 = m1 + fold(r * y)
                m2 = m2 + fold(y * y)
                r_ref[flat] = y
        return m0, m1, m2

    zero = jnp.zeros((8, depth), F32)
    sums = (zero, zero, zero)
    image(HALO - 1, sums, inside(HALO - 1), False)
    image(HALO + rows, sums, inside(HALO + rows), False)
    m0, m1, m2 = lax.fori_loop(HALO, HALO + rows, lambda p, c: image(p, c, None, True), sums)
    q_copy = pltpu.make_async_copy(u_ref.at[pl.ds(2 * plane, extent)], q_out, sems.at[7])
    q_copy.start()

    def second(p, m3):
        base = p * plane + PAD
        for b in blocks:
            start = base + b
            at = pl.ds(pl.multiple_of(start, 8), size)
            flat = pl.ds(pl.multiple_of(p * ny + b, 8), size)
            n, q = neighbour_sum(u_ref, start, size, plane, 0.0)
            m3 = m3 + fold(r_ref[flat] * (s_ref[flat] * q - e_ref[at] * n))
        return m3

    m3 = lax.fori_loop(HALO, HALO + rows, second, zero)
    for k, m in enumerate((m0, m1, m2, m3)):
        mom_out[k] = jnp.sum(m)
    v_copy.wait()
    q_copy.wait()


def moments(meta, columns, residuals, lk_parts, w_parts, count_x):
    rows, ny, depth = lk_parts[1].shape
    plane = ny + PAD
    planes = rows + 2 * HALO
    field = pltpu.VMEM((planes * plane + PAD, depth), F32)
    flat = pltpu.VMEM((planes * ny, depth), F32)
    out = jax.ShapeDtypeStruct(((rows + 2) * plane, depth), F32)
    cells = planes * ny * depth
    return pl.pallas_call(
        functools.partial(moments_kernel, rows, ny, count_x),
        out_shape=(out, out, jax.ShapeDtypeStruct((4,), F32)),
        in_specs=[SMEM_SPEC, SMEM_SPEC, VMEM_SPEC] + [ANY_SPEC] * 6,
        out_specs=(ANY_SPEC, ANY_SPEC, SMEM_SPEC),
        scratch_shapes=[
            pltpu.VMEM((planes, ny, depth), BF16),
            pltpu.VMEM((planes, ny, depth), BF16),
            field, field, field, flat, flat,
            pltpu.SemaphoreType.DMA((8,)),
        ],
        compiler_params=pltpu.CompilerParams(vmem_limit_bytes=VMEM_LIMIT),
        cost_estimate=pl.CostEstimate(flops=60 * cells, bytes_accessed=12 * cells, transcendentals=cells),
        name="moments",
    )(meta, columns, residuals, *lk_parts, *w_parts)


def misfit_kernel(
    rows, ny, first, size, parts, tests,
    meta, coeffs, lk_low, lk, lk_high, w_low, w, w_high, h_low, h, h_high, v, q, bd_high, bd_low,
    mine_out, other_out,
    lk_buf, w_buf, h_buf, v_buf, q_buf, e_ref, a_ref, h_ref, x_ref, t_high, t_low, f_ref, sems,
):
    depth = lk.shape[2]
    length = rows // parts
    edge = 16
    low = edge if first > 0 else 0
    high = edge if first + size < ny else 0
    wide = size + 2 * edge
    from_row, span = first - low, low + size + high
    v_low = PAD
    v_span = PAD + size + (PAD if high else 0)
    block = block_rows(size)
    blocks = [i * block for i in range(size // block)]
    first_row, well = meta[0], meta[1]

    copies = []
    sem = iter(range(5 * parts + 6 + tests))

    def start(source, target, chunk):
        copy = pltpu.make_async_copy(source, target, sems.at[next(sem)])
        copy.start()
        copies[chunk].append(copy)

    for chunk in range(parts):
        copies.append([])
        begin = chunk * length
        for lo, mid, hi, buf in (
            (lk_low, lk, lk_high, lk_buf),
            (w_low, w, w_high, w_buf),
            (h_low, h, h_high, h_buf),
        ):
            ys, yt = pl.ds(from_row, span), pl.ds(edge - low, span)
            if chunk == 0:
                start(lo.at[pl.ds(lo.shape[0] - 1, 1), ys], buf.at[pl.ds(0, 1), yt], chunk)
                start(mid.at[pl.ds(0, length + (1 if parts > 1 else 0)), ys], buf.at[pl.ds(1, length + (1 if parts > 1 else 0)), yt], chunk)
            else:
                more = 1 if chunk < parts - 1 else 0
                start(mid.at[pl.ds(begin + 1, length - 1 + more), ys], buf.at[pl.ds(begin + 2, length - 1 + more), yt], chunk)
            if chunk == parts - 1:
                start(hi.at[pl.ds(0, 1), ys], buf.at[pl.ds(rows + 1, 1), yt], chunk)
        for source, buf in ((v, v_buf), (q, q_buf)):
            zs = pl.ds(first, v_span)
            lo_p = 0 if chunk == 0 else begin + 2
            hi_p = begin + length + 2
            start(source.at[pl.ds(lo_p, hi_p - lo_p), zs], buf.at[pl.ds(lo_p, hi_p - lo_p), pl.ds(0, v_span)], chunk)

    c0, c1 = coeffs[0], coeffs[1]
    slot_rows = wide
    ones = jnp.ones((PAD, depth), F32)
    zeros = jnp.zeros((PAD, depth), F32)
    for s in range(4):
        base = s * slot_rows
        for at in (pl.ds(base + edge - PAD, PAD), pl.ds(base + edge + size, PAD)):
            e_ref[at] = ones
            a_ref[at] = zeros
            h_ref[at] = zeros

    def slot(p):
        return lax.rem(p, 4) * slot_rows

    spans = [(edge + b, block) for b in blocks]
    if low:
        spans.insert(0, (0, edge))
    if high:
        spans.append((edge + size, edge))

    def prepare(p):
        base = slot(p)
        for at, count in spans:
            e = jnp.exp(0.5 * lk_buf[p, at : at + count].astype(F32))
            a = e * w_buf[p, at : at + count].astype(F32)
            hh = h_buf[p, at : at + count].astype(F32)
            if at == 0:
                e, a, hh = e[8:], a[8:], hh[8:]
                at, count = 8, 8
            elif at == edge + size:
                e, a, hh = e[:8], a[:8], hh[:8]
                count = 8
            zat = at - edge + PAD
            a = a + c0 * v_buf[p, zat : zat + count] + c1 * q_buf[p, zat : zat + count]
            to = pl.ds(pl.multiple_of(base + at, 8), count)
            e_ref[to] = e
            a_ref[to] = a
            h_ref[to] = hh

    def along(p):
        here, there = slot(p), slot(p + 1)
        for b in blocks:
            at = pl.ds(pl.multiple_of(here + edge + b, 8), block)
            to = pl.ds(pl.multiple_of(there + edge + b, 8), block)
            x_ref[b : b + block] = (e_ref[to] * a_ref[at] - e_ref[at] * a_ref[to]) * (h_ref[at] - h_ref[to])

    def centre(p, x, part):
        here, there = slot(p), slot(p + 1)
        column = (first_row + x) * ny + first
        for b in blocks:
            begin = here + edge + b
            to = pl.ds(pl.multiple_of(there + edge + b, 8), block)
            e_near, a_near, h_near = (window(ref, begin, block) for ref in (e_ref, a_ref, h_ref))
            mid = slice(PAD, PAD + block)
            e, a, hh = e_near[mid], a_near[mid], h_near[mid]
            en, an, hn = e_ref[to], a_ref[to], h_ref[to]
            before = x_ref[b : b + block]
            after = (en * a - e * an) * (hh - hn)
            x_ref[b : b + block] = after
            total = before + after
            for shift in (-1, 1):
                at = slice(PAD + shift, PAD + shift + block)
                en, an, hn = e_near[at], a_near[at], h_near[at]
                total = total + (en * a - e * an) * (hh - hn)
            lanes = lane_index(e.shape)
            end = lanes == depth - 1
            en = jnp.where(end, 1.0, pltpu.roll(e, depth - 1, 1))
            an = jnp.where(end, 0.0, pltpu.roll(a, depth - 1, 1))
            hn = jnp.where(end, 0.0, pltpu.roll(hh, depth - 1, 1))
            up = (en * a - e * an) * (hh - hn)
            down = jnp.where(lanes == 0, a * hh, pltpu.roll(up, 1, 1))
            total = -0.5 * (total + up + down)
            row = lax.broadcasted_iota(jnp.int32, e.shape, 0) + (column + b)
            total = jnp.where(row == well, 0.0, total)
            high_part, low_part = split(total)
            to = pl.ds(pl.multiple_of((x - part * length) * size + b, 16), block)
            t_high[to, part * depth : (part + 1) * depth] = high_part
            t_low[to, part * depth : (part + 1) * depth] = low_part

    for part in range(parts):
        for copy in copies[part]:
            copy.wait()
        if part == 0:
            prepare(0)
            prepare(1)
            along(0)

        def step(x, carry):
            prepare(x + 2)
            centre(x + 1, x, part)
            return carry

        lax.fori_loop(part * length, (part + 1) * length, step, 0)

    chunk = size
    lanes_out = f_ref.shape[2]

    def transform(i, carry):
        at = pl.ds(pl.multiple_of(i * chunk, 16), chunk)
        value = dot3((t_high[at], t_low[at]), (bd_high[...], bd_low[...]))
        for t in range(tests):
            f_ref[t, at] = value[:, t * lanes_out : (t + 1) * lanes_out]
        return carry

    lax.fori_loop(0, length, transform, 0)
    chips = tests // 2
    outs = []
    for k in range(chips):
        outs.append(pltpu.make_async_copy(f_ref.at[meta[4 + k]], mine_out.at[k], sems.at[next(sem)]))
        outs.append(pltpu.make_async_copy(f_ref.at[meta[4 + chips + k]], other_out.at[k], sems.at[next(sem)]))
    for copy in outs:
        copy.start()
    for copy in outs:
        copy.wait()


def misfit(meta, coeffs, lk_parts, w_parts, h_parts, v, q, tables, first, size, parts, tests):
    rows, ny, depth = lk_parts[1].shape
    length = rows // parts
    lanes = tables[0].shape[1] // tests
    plane = ny + PAD
    v, q = (a.reshape(rows + 2, plane, depth) for a in (v, q))
    wide = size + 32
    out = jax.ShapeDtypeStruct((tests // 2, length * size, lanes), F32)
    half = pltpu.VMEM((rows + 2, wide, depth), BF16)
    full = pltpu.VMEM((rows + 2, size + 2 * PAD, depth), F32)
    ring = pltpu.VMEM((4 * wide, depth), F32)
    cells = rows * size * depth
    return pl.pallas_call(
        functools.partial(misfit_kernel, rows, ny, first, size, parts, tests),
        out_shape=(out, out),
        in_specs=[SMEM_SPEC, SMEM_SPEC] + [ANY_SPEC] * 11 + [VMEM_SPEC] * 2,
        out_specs=(ANY_SPEC, ANY_SPEC),
        scratch_shapes=[
            half, half, half, full, full, ring, ring, ring,
            pltpu.VMEM((size, depth), F32),
            pltpu.VMEM((length * size, parts * depth), BF16),
            pltpu.VMEM((length * size, parts * depth), BF16),
            pltpu.VMEM((tests, length * size, lanes), F32),
            pltpu.SemaphoreType.DMA((5 * parts + 6 + tests,)),
        ],
        compiler_params=pltpu.CompilerParams(vmem_limit_bytes=VMEM_LIMIT),
        cost_estimate=pl.CostEstimate(flops=60 * cells, bytes_accessed=18 * cells, transcendentals=cells),
        name="misfit",
    )(meta, coeffs, *lk_parts, *w_parts, *h_parts, v, q, *tables)


def power(value, exponent):
    result = None
    while exponent:
        if exponent & 1:
            result = value if result is None else result * value
        exponent >>= 1
        if exponent:
            value = value * value
    return result


def ratio_of(across, deep):
    half = (1.0 + range_squared * (across + deep) + 2.0 * range_squared) / (2.0 * range_squared)
    return 1.0 / (half + jnp.sqrt(half * half - 1.0))


def by_block(values, lanes, width):
    result = values[-1]
    for j in range(len(values) - 2, -1, -1):
        result = jnp.where(lanes < (j + 1) * width, values[j], result)
    return result


def powers(value, length, count):
    step = power(value, length)
    result = [jnp.ones_like(value)]
    for _ in range(count - 1):
        result.append(result[-1] * step)
    return result


def everywhere(value, width):
    lanes = value.shape[1]
    shift = width
    while shift < lanes:
        value = value + pltpu.roll(value, shift, 1)
        shift *= 2
    return value


def solve_kernel(length, parts, width, chunks, meta, across, deep, *refs):
    groups = refs[:chunks]
    tables = refs[chunks : 3 * chunks]
    local_out, state_out, packed_out, h_ref = refs[3 * chunks :]
    ny, lanes_count = across.shape
    size = groups[0].shape[0] // length
    pair = 2 if length % 2 == 0 else 1
    for g in range(0, length, pair):
        total = None
        for c in range(chunks):
            value = jnp.concatenate([groups[c][(g + k) * size : (g + k + 1) * size] for k in range(pair)], axis=1)
            product = dot3((tables[2 * c][...], tables[2 * c + 1][...]), split(value))
            total = product if total is None else total + product
        for k in range(pair):
            h_ref[g + k] = total[:, k * lanes_count : (k + 1) * lanes_count]

    block = block_rows(ny)
    qz = deep[pl.ds(meta[2], 1)]

    def solve(i, carry):
        at = pl.ds(pl.multiple_of(i * block, 16), block)
        rho = ratio_of(across[at], qz)
        square = rho * rho
        tilt = (1.0 + square) / (1.0 - square)
        p1 = jnp.zeros_like(rho)
        p2 = jnp.zeros_like(rho)
        for x in range(length):
            p2 = rho * (p2 + p1)
            p1 = h_ref[x, at] + rho * p1
            local_out[x, at] = p2 + tilt * p1
        n1 = jnp.zeros_like(rho)
        n2 = jnp.zeros_like(rho)
        for x in range(length - 1, -1, -1):
            local_out[x, at] = local_out[x, at] + (n2 + tilt * n1)
            n1 = rho * (n1 + h_ref[x, at])
            n2 = rho * n2 + n1
        if parts == 1:
            for k, value in enumerate((p1, p2, n1, n2)):
                state_out[k, at] = jnp.zeros_like(rho)
                packed_out[k, at] = value
            return carry
        lanes = lane_index(rho.shape)
        steps = powers(rho, length, parts)
        zero = jnp.zeros_like(rho)
        into = [zero] * 4
        for s in range(1, parts):
            weight = jnp.where(lanes >= s * width, steps[s - 1], 0.0)
            far = float(length * (s - 1))
            one, two = (pltpu.roll(value, s * width, 1) for value in (p1, p2))
            into[0] = into[0] + weight * one
            into[1] = into[1] + weight * (two + far * one)
            weight = jnp.where(lanes < (parts - s) * width, steps[s - 1], 0.0)
            one, two = (pltpu.roll(value, lanes_count - s * width, 1) for value in (n1, n2))
            into[2] = into[2] + weight * one
            into[3] = into[3] + weight * (two + far * one)
        for k in range(4):
            state_out[k, at] = into[k]
        place = lanes // width
        weight = by_block(steps[::-1], lanes, width)
        far = ((parts - 1 - place) * length).astype(F32)
        d1 = everywhere(weight * p1, width)
        d2 = everywhere(weight * (p2 + far * p1), width)
        weight = by_block(steps, lanes, width)
        far = (place * length).astype(F32)
        e1 = everywhere(weight * n1, width)
        e2 = everywhere(weight * (n2 + far * n1), width)
        packed_out[at] = by_block([d1, d2, e1, e2], lanes, width)
        return carry

    lax.fori_loop(0, ny // block, solve, 0)


def solve(meta, across, deep, groups, tables, length, parts, width):
    ny, lanes = across.shape
    chunks = len(groups)
    packed = (ny, lanes) if parts == 4 else (4, ny, lanes)
    cells = length * ny * lanes
    return pl.pallas_call(
        functools.partial(solve_kernel, length, parts, width, chunks),
        out_shape=(
            jax.ShapeDtypeStruct((length, ny, lanes), F32),
            jax.ShapeDtypeStruct((4, ny, lanes), F32),
            jax.ShapeDtypeStruct(packed, F32),
        ),
        in_specs=[SMEM_SPEC] + [VMEM_SPEC] * (2 + 3 * chunks),
        out_specs=(VMEM_SPEC,) * 3,
        scratch_shapes=[pltpu.VMEM((length, ny, lanes), F32)],
        compiler_params=pltpu.CompilerParams(vmem_limit_bytes=VMEM_LIMIT),
        cost_estimate=pl.CostEstimate(flops=6 * cells * ny, bytes_accessed=16 * cells, transcendentals=0),
        name="solve",
    )(meta, across, deep, *groups, *tables)


def finish_kernel(
    length, parts, width, spaces, tests, scale,
    meta, across, deep, local, state, packed, c_high, c_low, out, v_ref, v_high, v_low,
):
    ny, lanes_count = across.shape
    block = block_rows(ny)
    qz = deep[pl.ds(meta[2], 1)]
    rank = meta[3]
    slab = length * parts

    def correct(i, carry):
        at = pl.ds(pl.multiple_of(i * block, 16), block)
        rho = ratio_of(across[at], qz)
        square = rho * rho
        tilt = (1.0 + square) / (1.0 - square)
        gain = rho / (2.0 * range_squared * 0.5 * (1.0 - square))
        gain = (prior_gain * scale) * gain * gain
        lanes = lane_index(rho.shape)
        step = power(rho, slab)
        weight = jnp.ones_like(rho)
        if parts > 1:
            near = far = jnp.zeros_like(rho)
            for k in range(1, spaces + 1):
                left = packed[lax.rem(rank + spaces - k, spaces), at]
                right = packed[lax.rem(rank + k, spaces), at]
                value = weight * jnp.where(lanes < 2 * width, left, right)
                near = near + value
                far = far + float(slab * (k - 1)) * value
                weight = weight * step

            def pick(value, s):
                return everywhere(jnp.where((lanes >= s * width) & (lanes < (s + 1) * width), value, 0.0), width)

            one, two, far_one = pick(near, 0), pick(near, 1), pick(far, 0)
            back_one, back_two, back_far = pick(near, 2), pick(near, 3), pick(far, 2)
        else:
            one = two = far_one = back_one = back_two = back_far = jnp.zeros_like(rho)
            for k in range(1, spaces + 1):
                left = lax.rem(rank + spaces - k, spaces)
                right = lax.rem(rank + k, spaces)
                first = weight * packed[left, 0, at]
                one = one + first
                two = two + weight * packed[left, 1, at]
                far_one = far_one + float(slab * (k - 1)) * first
                first = weight * packed[right, 2, at]
                back_one = back_one + first
                back_two = back_two + weight * packed[right, 3, at]
                back_far = back_far + float(slab * (k - 1)) * first
                weight = weight * step
        around = 1.0 / (1.0 - weight)
        again = float(slab * spaces) * weight * around * around
        two = around * (two + far_one) + again * one
        one = around * one
        back_two = around * (back_two + back_far) + again * back_one
        back_one = around * back_one
        if parts > 1:
            steps = powers(rho, length, parts)
            place = lanes // width
            weight = by_block(steps, lanes, width)
            two = weight * (two + (place * length).astype(F32) * one)
            one = weight * one
            weight = by_block(steps[::-1], lanes, width)
            back_two = weight * (back_two + ((parts - 1 - place) * length).astype(F32) * back_one)
            back_one = weight * back_one
        one = one + state[0, at]
        two = two + state[1, at]
        back_one = back_one + state[2, at]
        back_two = back_two + state[3, at]
        for x in range(length):
            two = rho * (two + one)
            one = rho * one
            v_ref[x, at] = local[x, at] + (two + tilt * one)
        for x in range(length - 1, -1, -1):
            value = gain * (v_ref[x, at] + (back_two + tilt * back_one))
            v_high[x, at], v_low[x, at] = split(value)
            back_one = rho * back_one
            back_two = rho * back_two + back_one
        return carry

    lax.fori_loop(0, ny // block, correct, 0)
    pair = 2 if length % 2 == 0 else 1
    rows = ny // tests
    for g in range(0, length, pair):
        right = tuple(jnp.concatenate([ref[g + k] for k in range(pair)], axis=1) for ref in (v_high, v_low))
        total = dot3((c_high[...], c_low[...]), right)
        for k in range(pair):
            for t in range(tests):
                out[t, g + k] = total[t * rows : (t + 1) * rows, k * lanes_count : (k + 1) * lanes_count]


def finish(meta, across, deep, local, state, packed, tables, parts, width, tests, scale):
    length, ny, lanes = local.shape
    spaces = packed.shape[0]
    cells = length * ny * lanes
    return pl.pallas_call(
        functools.partial(finish_kernel, length, parts, width, spaces, tests, scale),
        out_shape=jax.ShapeDtypeStruct((tests, length, ny // tests, lanes), F32),
        in_specs=[SMEM_SPEC] + [VMEM_SPEC] * 7,
        out_specs=VMEM_SPEC,
        scratch_shapes=[
            pltpu.VMEM((length, ny, lanes), F32),
            pltpu.VMEM((length, ny, lanes), BF16),
            pltpu.VMEM((length, ny, lanes), BF16),
        ],
        compiler_params=pltpu.CompilerParams(vmem_limit_bytes=VMEM_LIMIT),
        cost_estimate=pl.CostEstimate(flops=6 * cells * ny, bytes_accessed=16 * cells, transcendentals=0),
        name="finish",
    )(meta, across, deep, local, state, packed, *tables)


def depth_kernel(tests, parts, depth, pieces, bd_high, bd_low, out):
    rows = pieces.shape[1]
    value = jnp.concatenate([pieces[t] for t in range(tests)], axis=1)
    result = dot3(split(value), (bd_high[...], bd_low[...]))
    for j in range(parts):
        out[j] = result[:, j * depth : (j + 1) * depth]


def depth_cells(pieces, tables, parts, depth):
    tests, rows, lanes = pieces.shape
    steps = 3 if rows % 24 == 0 else 1
    return pl.pallas_call(
        functools.partial(depth_kernel, tests, parts, depth),
        out_shape=jax.ShapeDtypeStruct((parts, rows, depth), F32),
        grid=(steps,),
        in_specs=[
            pl.BlockSpec((tests, rows // steps, lanes), lambda i: (0, i, 0)),
            pl.BlockSpec(tables[0].shape, lambda i: (0, 0)),
            pl.BlockSpec(tables[1].shape, lambda i: (0, 0)),
        ],
        out_specs=pl.BlockSpec((parts, rows // steps, depth), lambda i: (0, i, 0)),
        compiler_params=pltpu.CompilerParams(vmem_limit_bytes=VMEM_LIMIT),
        cost_estimate=pl.CostEstimate(
            flops=6 * tests * rows * lanes * parts * depth, bytes_accessed=8 * tests * rows * lanes, transcendentals=0
        ),
        name="depth_cells",
    )(pieces, *tables)


def on_device(log_k, heads, warm_adjoint, obs_columns, obs_residuals, well_columns):
    rows, ny, depth = log_k.shape
    spaces = lax.axis_size("space")
    tests = lax.axis_size("test")
    rank = lax.axis_index("space")
    test = lax.axis_index("test")
    chips = tests // 2
    width = depth // tests
    parts = depth // width if depth // width == 4 and rows % 4 == 0 else 1
    length = rows // parts
    lanes = depth
    count_x = rows * spaces

    forward = [(i, i + 1) for i in range(spaces - 1)]
    backward = [(i + 1, i) for i in range(spaces - 1)]

    def with_halo(field, count):
        low = lax.ppermute(field[rows - count :], "space", forward)
        high = lax.ppermute(field[:count], "space", backward)
        return low, field, high

    w_parts = with_halo(warm_adjoint[0], HALO)
    lk_parts = with_halo(log_k, HALO)
    h_parts = with_halo(heads[0], 1)

    chip, core = test // 2, test % 2
    order = [2 * ((chip + k) % chips) + core for k in range(chips)]
    order += [2 * ((chip + k) % chips) + 1 - core for k in range(chips)]
    meta = jnp.stack([rank * rows, well_columns[0], test, rank] + order).astype(jnp.int32)

    v, q, sums = moments(meta, obs_columns[0], obs_residuals[0], lk_parts, w_parts, count_x)
    m0, m1, m2, m3 = lax.psum(sums, "space")
    alpha = m0 / m1
    new = alpha * alpha * m2 - 2.0 * alpha * m1 + m0
    beta = new / m0
    bent = 1.0 + beta
    second = new / (bent * bent * m1 - 2.0 * bent * alpha * m2 + alpha * alpha * m3)
    coeffs = jnp.stack([alpha + second * bent, -second * alpha])

    cas_z = cas(depth)
    forward_z = np.zeros((parts, depth, tests, lanes))
    inverse_z = np.zeros((tests, lanes, parts, depth))
    kappa_z = np.zeros((tests, lanes))
    for t in range(tests):
        chosen = np.arange(t * width, (t + 1) * width)
        for j in range(parts):
            at = slice(j * width, (j + 1) * width)
            forward_z[j, :, t, at] = cas_z[:, chosen]
            inverse_z[t, at, j, :] = cas_z[chosen, :]
            kappa_z[t, at] = kappa(depth)[chosen]
    forward_z = halves(forward_z.reshape(parts * depth, tests * lanes))
    inverse_z = halves(inverse_z.reshape(tests * lanes, parts * depth))
    deep = kappa_z.astype(np.float32)
    across = np.repeat(kappa(ny)[:, None], lanes, axis=1).astype(np.float32)
    cas_y = cas(ny)

    chunks = 2 if (ny // 2) % 48 == 0 else 1
    size = ny // chunks
    other_core = [(i, i ^ 1) for i in range(tests)]
    groups, tables = [], []
    for c in range(chunks):
        mine, other = misfit(
            meta, coeffs, lk_parts, w_parts, h_parts, v, q, forward_z, c * size, size, parts, tests
        )
        summed = mine + lax.ppermute(other, "test", other_core)
        total = summed[0]
        for k in range(1, chips):
            total = total + lax.ppermute(
                summed[k], "test", [(i, (i + 2 * k) % tests) for i in range(tests)]
            )
        groups.append(total)
        tables += halves(cas_y[:, c * size : (c + 1) * size])

    local, state, packed = solve(meta, across, deep, groups, tables, length, parts, width)
    gathered = lax.all_gather(packed, "space")
    pieces = finish(
        meta, across, deep, local, state, gathered, halves(cas_y), parts, width, tests, 1.0 / (ny * depth)
    )
    pieces = pieces.reshape(tests, length * (ny // tests), lanes)
    pieces = lax.all_to_all(pieces, "test", split_axis=0, concat_axis=0, tiled=True)
    return depth_cells(pieces, inverse_z, parts, depth).reshape(rows, ny // tests, depth)


def solution(mesh):
    placed = (
        P(("groups", "space"), None, None),
        P("test", ("groups", "space"), None, None),
        P("test", ("groups", "space"), None, None),
        P("test", "groups"),
        P("test", "groups", None),
        P(("groups", "test")),
    )
    return jax.shard_map(
        on_device,
        mesh=mesh,
        in_specs=placed,
        out_specs=P(("groups", "space"), "test", None),
        check_vma=False,
    )
```

time: 755 us -> 230 us (0.30); the launches traced: 746 us -> 229 us
  other arithmetic: 302 us -> 3.02 us
  blocking collectives: 171 us -> 56.6 us
  Pallas kernels: 0 us -> 99.5 us
  waiting for transfers between devices: 107 us -> 36.3 us
  local copies, waits for them, and re-layouts: 70.3 us -> 5.92 us
  matrix products: 35.6 us -> 0 us
  starting transfers between devices: 41.1 us -> 21.6 us
  between operations: 18.7 us -> 6.14 us
    all_to_all x3 -> x1, blocking collectives: 138 us -> 26.6 us  [on_device(): lax.all_to_all(pieces, 'test', split_axis=0, concat_axis=0, tiled=True)]
    pallas_call x0 -> x6, Pallas kernels: none -> 99.5 us  [the longest x2 44.4 us: misfit(): pl.pallas_call(functools.partial(misfit_kernel, rows, ny, first, size, pa...]
    reduce_sum x3 -> x0, other arithmetic: 95.6 us -> none  [the longest x2 88.2 us: on_device(): step_length = norm_now / lax.psum(jnp.sum(direction * applied), 'space')]
    mul x6 -> x0, other arithmetic: 71.2 us -> none  [the longest x2 71 us: on_device(): partial_value = -0.5 * misfit_term * keep_mask[:, :, None]]
    reduce_scatter x1 -> x0, waiting for transfers between devices: 63.6 us -> none  [on_device(): lax.psum_scatter(partial_value, 'test', scatter_dimension=1, tiled=True)]
    concatenate x5 -> x0, other arithmetic: 50.4 us -> none  [the longest x4 50.4 us: with_halo(): jnp.concatenate([lax.ppermute(tail, axis, [(i, (i + 1) % count) for i in...]
    all_to_all x1 -> x0, waiting for transfers between devices: 39.9 us -> none  [on_device(): lax.all_to_all(across_freq, 'space', split_axis=0, concat_axis=2, tiled=T...]
    sub x1 -> x0, other arithmetic: 39.1 us -> none  [on_device(): residual = source - operate(adjoint, lam_padded, conduct)]
  transfers between devices with their start and end apart: 14 -> 10, of which waited for: 5 -> 3; matrix products, arithmetic and copies ran while one was open for 12% -> 2% of each run, Pallas kernels for 0% -> 26%
where the time goes in v1:
time: 230 us; the launch traced here: 229 us
  Pallas kernels  99.5 us (43%)
  blocking collectives  56.6 us (25%)
  waiting for transfers between devices  36.3 us (16%)
  starting transfers between devices  21.6 us (9%)
  between operations  6.14 us (3%)
  local copies, waits for them, and re-layouts  5.92 us (3%)
  other arithmetic  3.02 us (1%)
    pallas_call x2, Pallas kernels, misfit(): pl.pallas_call(functools.partial(misfit_kernel, rows, ny, first, size, pa...  44.4 us
    pallas_call x1, Pallas kernels, moments(): pl.pallas_call(functools.partial(moments_kernel, rows, ny, count_x), out_...  36.5 us
    ppermute x2, waiting for transfers between devices, on_device(): lax.ppermute(summed[k], 'test', [(i, (i + 2 * k) % tests) for i in range(...  34.6 us
    all_to_all x1, blocking collectives, on_device(): lax.all_to_all(pieces, 'test', split_axis=0, concat_axis=0, tiled=True)  26.6 us
    all_gather x1, blocking collectives, on_device(): gathered = lax.all_gather(packed, 'space')  16.9 us
    ppermute x3, starting transfers between devices, with_halo(): low = lax.ppermute(field[rows - count:], 'space', forward)  14.1 us
    psum x1, blocking collectives, on_device(): m0, m1, m2, m3 = lax.psum(sums, 'space')  13.2 us
    pallas_call x1, Pallas kernels, finish(): pl.pallas_call(functools.partial(finish_kernel, length, parts, width, spa...  7.19 us
  transfers between devices with their start and end apart: 10, of which 3 were waited for; matrix products, arithmetic and copies ran while one was open for 2% of the time, Pallas kernels for 26%

profile of v1, /device:TPU:0, one launch (start us, length us, event | category | flops | bytes accessed | tf_op | source)
XLA Modules:
  0.0 229.1 jit_solution(18342382806540533407)
XLA Ops:
  0.0 1.1 fusion.2
  1.1 4.9 %collective-permute-start = (bf16[3,288,128]{2,1,0:T(8,128)(2,1)S(1)}, bf16[3,288,128]{2,1,0:T(8,128)(2,1)S(1)}, u32[]{:S(2)}, u32[]{:S(2)}) collective-permute-start(bf16[3,288,128]{2,1,0:T(8,128)(2,1)S(1)} %get-tuple-element.30), channel_id=1, source_target_pairs={{0,4},{4,8},{8,12},{1,5},{5,9},{9,13},{2,6},{6,10},{10,14},{3,7},{... | collective-permute-start | bytes 663560 | tf_op jit(solution)/shard_map/ppermute | solution.py:742
  6.0 1.3 collective-permute-start.1
  7.3 1.1 slice_bitcast_fusion.4
  8.4 4.6 %collective-permute-start.2 = (bf16[3,288,128]{2,1,0:T(8,128)(2,1)S(1)}, bf16[3,288,128]{2,1,0:T(8,128)(2,1)S(1)}, u32[]{:S(2)}, u32[]{:S(2)}) collective-permute-start(bf16[3,288,128]{2,1,0:T(8,128)(2,1)S(1)} %get-tuple-element.28), channel_id=1, source_target_pairs={{0,4},{4,8},{8,12},{1,5},{5,9},{9,13},{2,6},{6,10},{10,14},{3,7},{... | collective-permute-start | bytes 663560 | tf_op jit(solution)/shard_map/ppermute | solution.py:742
  13.0 1.3 collective-permute-start.3
  14.3 0.9 slice_bitcast_fusion.6
  15.2 4.5 %collective-permute-start.4 = (bf16[1,288,128]{2,1,0:T(8,128)(2,1)S(1)}, bf16[1,288,128]{2,1,0:T(8,128)(2,1)S(1)}, u32[]{:S(2)}, u32[]{:S(2)}) collective-permute-start(bf16[1,288,128]{2,1,0:T(8,128)(2,1)S(1)} %get-tuple-element.26), channel_id=1, source_target_pairs={{0,4},{4,8},{8,12},{1,5},{5,9},{9,13},{2,6},{6,10},{10,14},{3,7},{... | collective-permute-start | bytes 221192 | tf_op jit(solution)/shard_map/ppermute | solution.py:742
  20.5 0.7 stack.40.meta
  21.1 1.3 collective-permute-start.5
  22.5 0.6 copy-done.1
  23.3 36.5 %moments.1 = (f32[14800,128]{1,0:T(8,128)}, f32[14800,128]{1,0:T(8,128)}, f32[4]{0:T(128)}) custom-call(s32[8]{0:T(128)} %stack.40.meta, s32[64]{0:T(128)} %bitcast.54, f32[64,128]{1,0:T(8,128)} %bitcast.53, bf16[3,288,128]{2,1,0:T(8,128)(2,1)} %copy-done, bf16[48,288,128]{2,1,0:T(8,128)(2,1)} %lk.5, bf16[3,288,128]{2,1,0:T(8,128)(2,1)} %copy-done.1, ...), custom_call_target="tpu_custom_call" | custom-call | flops 119439360 | bytes 23887872 | tf_op jit(solution)/shard_map/moments/pallas_call | solution.py:239
  59.8 13.2 %psum.7 = f32[4]{0:T(128)S(1)} all-reduce(f32[4]{0:T(128)} %get-tuple-element.15), channel_id=1, replica_groups=mesh['groups'=2,'space'=4,'test'=4] {'space'}, use_global_device_ids=true, to_apply=%region_0.1 | all-reduce | flops 4 | bytes 32 | tf_op jit(solution)/shard_map/psum | solution.py:756
  72.9 0.6 fusion.3
  78.8 0.6 pad_maximum_fusion.coeffs
  79.4 0.6 copy-done.6
  80.0 22.3 %misfit.2 = (f32[2,1728,128]{2,1,0:T(8,128)}, f32[2,1728,128]{2,1,0:T(8,128)}) custom-call(s32[8]{0:T(128)} %stack.40.meta, f32[2]{0:T(128)} %pad_maximum_fusion.coeffs, bf16[3,288,128]{2,1,0:T(8,128)(2,1)} %copy-done, bf16[48,288,128]{2,1,0:T(8,128)(2,1)} %lk.5, bf16[3,288,128]{2,1,0:T(8,128)(2,1)} %copy-done.1, bf16[3,288,128]{2,1,0:T(8,128)(2,1)} %copy-done.2, ...), custom_call_target="tpu_custom_call" | custom-call | flops 53084160 | bytes 15925248 | tf_op jit(solution)/shard_map/misfit/pallas_call | solution.py:434
  102.4 22.2 %misfit.3 = (f32[2,1728,128]{2,1,0:T(8,128)}, f32[2,1728,128]{2,1,0:T(8,128)}) custom-call(s32[8]{0:T(128)} %stack.40.meta, f32[2]{0:T(128)} %pad_maximum_fusion.coeffs, bf16[3,288,128]{2,1,0:T(8,128)(2,1)} %copy-done, bf16[48,288,128]{2,1,0:T(8,128)(2,1)} %lk.5, bf16[3,288,128]{2,1,0:T(8,128)(2,1)} %copy-done.1, bf16[3,288,128]{2,1,0:T(8,128)(2,1)} %copy-done.2, ...), custom_call_target="tpu_custom_call" | custom-call | flops 53084160 | bytes 15925248 | tf_op jit(solution)/shard_map/misfit/pallas_call | solution.py:434
  124.6 0.4 collective-permute-start.8
  125.3 1.6 collective-permute-start.7
  126.9 1.7 collective-permute-done.8
  128.6 0.2 add.65
  128.8 1.6 collective-permute-start.9
  130.4 17.4 %collective-permute-done.7 = f32[1728,128]{1,0:T(8,128)S(1)} collective-permute-done((f32[1728,128]{1,0:T(8,128)S(1)}, f32[1728,128]{1,0:T(8,128)S(1)}, u32[]{:S(2)}, u32[]{:S(2)}) %collective-permute-start.7) | collective-permute-done | bytes 884768 | tf_op jit(solution)/shard_map/ppermute | solution.py:792
  147.8 1.0 fusion.1.refs_0_
  148.8 17.2 %collective-permute-done.9 = f32[1728,128]{1,0:T(8,128)S(1)} collective-permute-done((f32[1728,128]{1,0:T(8,128)S(1)}, f32[1728,128]{1,0:T(8,128)S(1)}, u32[]{:S(2)}, u32[]{:S(2)}) %collective-permute-start.9) | collective-permute-done | bytes 884768 | tf_op jit(solution)/shard_map/ppermute | solution.py:792
  166.0 1.0 fusion.refs_1_
  167.1 6.6 %solve.1 = (f32[12,288,128]{2,1,0:T(8,128)}, f32[4,288,128]{2,1,0:T(8,128)}, f32[288,128]{1,0:T(8,128)}) custom-call(s32[8]{0:T(128)} %stack.40.meta, f32[288,128]{1,0:T(8,128)} %constant.76.clone.across, f32[4,128]{1,0:T(4,128)} %constant.77.clone.deep, f32[1728,128]{1,0:T(8,128)} %fusion.1.refs_0_, f32[1728,128]{1,0:T(8,128)} %fusion.refs_1_, ...), custom_call_target="tpu_custom_call" | custom-call | flops 764411904 | bytes 7077888 | tf_op jit(solution)/shard_map/solve/pallas_call | solution.py:570
  173.6 16.9 %all-gather = f32[1152,128]{1,0:T(8,128)} all-gather(f32[288,128]{1,0:T(8,128)} %get-tuple-element.24), channel_id=2, replica_groups=mesh['groups'=2,'space'=4,'test'=4] {'space'}, dimensions={0}, use_global_device_ids=true | all-gather | bytes 737280 | tf_op jit(solution)/shard_map/all_gather | solution.py:799
  190.5 7.2 %finish.1 = f32[4,12,72,128]{3,2,1,0:T(8,128)} custom-call(s32[8]{0:T(128)} %stack.40.meta, f32[288,128]{1,0:T(8,128)} %constant.76.clone.across, f32[4,128]{1,0:T(4,128)} %constant.77.clone.deep, f32[12,288,128]{2,1,0:T(8,128)} %get-tuple-element.22.local, f32[4,288,128]{2,1,0:T(8,128)} %get-tuple-element.23.state, f32[4,288,128]{2,1,0:T(8,128)} %bitcast.52, ...), custom_call_target="tpu_custom_call" | custom-call | flops 764411904 | bytes 7077888 | tf_op jit(solution)/shard_map/finish/pallas_call | solution.py:680
  197.7 26.6 %all_to_all.5.pieces = f32[4,864,128]{2,1,0:T(8,128)} all-to-all(f32[4,864,128]{2,1,0:T(8,128)} %bitcast.51), channel_id=1, replica_groups=mesh['groups'=2,'space'=4,'test'=4] {'test'}, dimensions={0} | all-to-all | bytes 3538944 | tf_op jit(solution)/shard_map/all_to_all | solution.py:804
  224.3 4.8 %depth_cells.1 = f32[4,864,128]{2,1,0:T(8,128)} custom-call(f32[4,864,128]{2,1,0:T(8,128)} %all_to_all.5.pieces, bf16[512,512]{1,0:T(8,128)(2,1)} %constant.84.clone.bd_high, bf16[512,512]{1,0:T(8,128)(2,1)} %constant.85.clone.bd_low), custom_call_target="tpu_custom_call" | custom-call | flops 1358954496 | bytes 3538944 | tf_op jit(solution)/shard_map/depth_cells/pallas_call | solution.py:707
  (25 shorter events, 0.6 us)
Async XLA Ops:
  1.1 20.1 %collective-permute-start = (bf16[3,288,128]{2,1,0:T(8,128)(2,1)S(1)}, bf16[3,288,128]{2,1,0:T(8,128)(2,1)S(1)}, u32[]{:S(2)}, u32[]{:S(2)}) collective-permute-start(bf16[3,288,128]{2,1,0:T(8,128)(2,1)S(1)} %get-tuple-element.30), channel_id=1, source_target_pairs={{0,4},{4,8},{8,12},{1,5},{5,9},{9,13},{2,6},{6,10},{10,14},{3,7},{... | collective-permute-start | bytes 663560 | tf_op jit(solution)/shard_map/ppermute | solution.py:742
  6.0 16.4 %collective-permute-start.1 = (bf16[3,288,128]{2,1,0:T(8,128)(2,1)S(1)}, bf16[3,288,128]{2,1,0:T(8,128)(2,1)S(1)}, u32[]{:S(2)}, u32[]{:S(2)}) collective-permute-start(bf16[3,288,128]{2,1,0:T(8,128)(2,1)S(1)} %get-tuple-element.29), channel_id=1, source_target_pairs={{4,0},{8,4},{12,8},{5,1},{9,5},{13,9},{6,2},{10,6},{14,10},{7,3},{... | collective-permute-start | bytes 663560 | tf_op jit(solution)/shard_map/ppermute | solution.py:743
  8.4 14.0 %collective-permute-start.2 = (bf16[3,288,128]{2,1,0:T(8,128)(2,1)S(1)}, bf16[3,288,128]{2,1,0:T(8,128)(2,1)S(1)}, u32[]{:S(2)}, u32[]{:S(2)}) collective-permute-start(bf16[3,288,128]{2,1,0:T(8,128)(2,1)S(1)} %get-tuple-element.28), channel_id=1, source_target_pairs={{0,4},{4,8},{8,12},{1,5},{5,9},{9,13},{2,6},{6,10},{10,14},{3,7},{... | collective-permute-start | bytes 663560 | tf_op jit(solution)/shard_map/ppermute | solution.py:742
  13.0 9.5 %collective-permute-start.3 = (bf16[3,288,128]{2,1,0:T(8,128)(2,1)S(1)}, bf16[3,288,128]{2,1,0:T(8,128)(2,1)S(1)}, u32[]{:S(2)}, u32[]{:S(2)}) collective-permute-start(bf16[3,288,128]{2,1,0:T(8,128)(2,1)S(1)} %get-tuple-element.27), channel_id=1, source_target_pairs={{4,0},{8,4},{12,8},{5,1},{9,5},{13,9},{6,2},{10,6},{14,10},{7,3},{... | collective-permute-start | bytes 663560 | tf_op jit(solution)/shard_map/ppermute | solution.py:743
  15.2 64.2 %collective-permute-start.4 = (bf16[1,288,128]{2,1,0:T(8,128)(2,1)S(1)}, bf16[1,288,128]{2,1,0:T(8,128)(2,1)S(1)}, u32[]{:S(2)}, u32[]{:S(2)}) collective-permute-start(bf16[1,288,128]{2,1,0:T(8,128)(2,1)S(1)} %get-tuple-element.26), channel_id=1, source_target_pairs={{0,4},{4,8},{8,12},{1,5},{5,9},{9,13},{2,6},{6,10},{10,14},{3,7},{... | collective-permute-start | bytes 221192 | tf_op jit(solution)/shard_map/ppermute | solution.py:742
  21.1 1.4 copy-start
  21.1 58.2 %collective-permute-start.5 = (bf16[1,288,128]{2,1,0:T(8,128)(2,1)S(1)}, bf16[1,288,128]{2,1,0:T(8,128)(2,1)S(1)}, u32[]{:S(2)}, u32[]{:S(2)}) collective-permute-start(bf16[1,288,128]{2,1,0:T(8,128)(2,1)S(1)} %get-tuple-element.25), channel_id=1, source_target_pairs={{4,0},{8,4},{12,8},{5,1},{9,5},{13,9},{6,2},{10,6},{14,10},{7,3},{... | collective-permute-start | bytes 221192 | tf_op jit(solution)/shard_map/ppermute | solution.py:743
  22.4 0.7 copy-start.1
  22.5 0.7 copy-start.2
  22.5 0.8 copy-start.3
  79.4 0.6 copy-start.6
  79.4 0.7 copy-start.7
  102.3 22.7 %copy-start.5 = (f32[2,1728,128]{2,1,0:T(8,128)S(1)}, f32[2,1728,128]{2,1,0:T(8,128)}, u32[]{:S(2)}) copy-start(f32[2,1728,128]{2,1,0:T(8,128)} %get-tuple-element.18) | copy-start | bytes 5308420
  102.3 22.7 %collective-permute-start.6 = (f32[2,1728,128]{2,1,0:T(8,128)}, f32[2,1728,128]{2,1,0:T(8,128)S(1)}, u32[]{:S(2)}, u32[]{:S(2)}) collective-permute-start(f32[2,1728,128]{2,1,0:T(8,128)} %get-tuple-element.19), channel_id=1, source_target_pairs={{0,1},{1,0},{2,3},{3,2},{4,5},{5,4},{6,7},{7,6},{8,9},{9,8},{10,11... | collective-permute-start | bytes 5308424 | tf_op jit(solution)/shard_map/ppermute | solution.py:789
  124.6 4.0 %collective-permute-start.8 = (f32[2,1728,128]{2,1,0:T(8,128)}, f32[2,1728,128]{2,1,0:T(8,128)S(1)}, u32[]{:S(2)}, u32[]{:S(2)}) collective-permute-start(f32[2,1728,128]{2,1,0:T(8,128)} %get-tuple-element.21), channel_id=1, source_target_pairs={{0,1},{1,0},{2,3},{3,2},{4,5},{5,4},{6,7},{7,6},{8,9},{9,8},{10,11... | collective-permute-start | bytes 5308424 | tf_op jit(solution)/shard_map/ppermute | solution.py:789
  125.2 3.4 %copy-start.4 = (f32[2,1728,128]{2,1,0:T(8,128)S(1)}, f32[2,1728,128]{2,1,0:T(8,128)}, u32[]{:S(2)}) copy-start(f32[2,1728,128]{2,1,0:T(8,128)} %get-tuple-element.20) | copy-start | bytes 5308420
  125.3 22.6 %collective-permute-start.7 = (f32[1728,128]{1,0:T(8,128)S(1)}, f32[1728,128]{1,0:T(8,128)S(1)}, u32[]{:S(2)}, u32[]{:S(2)}) collective-permute-start(f32[1728,128]{1,0:T(8,128)S(1)} %slice_bitcast_fusion.2), channel_id=1, source_target_pairs={{0,2},{1,3},{2,0},{3,1},{4,6},{5,7},{6,4},{7,5},{8,10},{9,11},{10,... | collective-permute-start | bytes 2654216 | tf_op jit(solution)/shard_map/ppermute | solution.py:792
  128.8 37.2 %collective-permute-start.9 = (f32[1728,128]{1,0:T(8,128)S(1)}, f32[1728,128]{1,0:T(8,128)S(1)}, u32[]{:S(2)}, u32[]{:S(2)}) collective-permute-start(f32[1728,128]{1,0:T(8,128)S(1)} %slice_bitcast_fusion), channel_id=1, source_target_pairs={{0,2},{1,3},{2,0},{3,1},{4,6},{5,7},{6,4},{7,5},{8,10},{9,11},{10,... | collective-permute-start | bytes 2654216 | tf_op jit(solution)/shard_map/ppermute | solution.py:792

commit v2 on v1

v2 whole, which is shorter than its diff:
```python
import functools

import jax
import jax.numpy as jnp
import ml_dtypes
import numpy as np
from jax import lax
from jax.experimental import pallas as pl
from jax.experimental.pallas import tpu as pltpu
from jax.sharding import PartitionSpec as P

prior_gain = 5.0
range_squared = 4.0

HALO = 3
PAD = 8
F32 = jnp.float32
BF16 = jnp.bfloat16
VMEM_LIMIT = 32 * 1024 * 1024
SMALL_LIMIT = 20 * 1024 * 1024
MISFIT_LIMIT = 40 * 1024 * 1024

SMEM_SPEC = pl.BlockSpec(memory_space=pltpu.SMEM)
VMEM_SPEC = pl.BlockSpec(memory_space=pltpu.VMEM)
ANY_SPEC = pl.BlockSpec(memory_space=pl.ANY)


def in_vmem(array):
    return pltpu.with_memory_space_constraint(array, pltpu.VMEM)


def in_hbm(array):
    return pltpu.with_memory_space_constraint(array, pltpu.HBM)


def cas(length):
    index = np.arange(length)
    angle = 2.0 * np.pi * (index[:, None] * index[None, :] % length) / length
    return np.cos(angle) + np.sin(angle)


def halves(table):
    table = np.asarray(table, np.float32)
    high = table.astype(ml_dtypes.bfloat16)
    low = (table - high.astype(np.float32)).astype(ml_dtypes.bfloat16)
    return high, low


def kappa(length):
    return 4.0 * np.sin(np.pi * np.arange(length) / length) ** 2


def split(value):
    high = value.astype(BF16)
    low = (value - high.astype(F32)).astype(BF16)
    return high, low


def dot(left, right):
    return lax.dot_general(left, right, (((1,), (0,)), ((), ())), preferred_element_type=F32)


def dot3(left, right):
    return dot(left[0], right[0]) + (dot(left[0], right[1]) + dot(left[1], right[0]))


def block_rows(count):
    for rows in (48, 32, 16):
        if count % rows == 0:
            return rows
    return count


def unrolled(start, stop, body, carry, most=4):
    count = stop - start
    factor = next(f for f in range(most, 0, -1) if count % f == 0)
    return lax.fori_loop(start, stop, body, carry, unroll=factor)


def lane_index(shape):
    return lax.broadcasted_iota(jnp.int32, shape, 1)


def window(ref, start, rows):
    return ref.at[pl.ds(pl.multiple_of(start - PAD, 8), rows + 2 * PAD)]


def neighbour_sum(ref, start, rows, plane, fill):
    near = window(ref, start, rows)
    here = near[PAD : PAD + rows]
    lanes = lane_index(here.shape)
    depth = here.shape[1]
    up = jnp.where(lanes == depth - 1, fill, pltpu.roll(here, depth - 1, 1))
    down = jnp.where(lanes == 0, fill, pltpu.roll(here, 1, 1))
    along = ref[pl.ds(pl.multiple_of(start - plane, 8), rows)] + ref[pl.ds(pl.multiple_of(start + plane, 8), rows)]
    across = near[PAD - 1 : PAD - 1 + rows] + near[PAD + 1 : PAD + 1 + rows]
    return along + across + (up + down), here


def fold(value):
    return jnp.sum(value.reshape(-1, 8, value.shape[1]), axis=0)


def field_rows(rows, ny):
    return (rows + 2 * HALO) * (ny + PAD) + PAD


def scale_plane(e_ref, u_ref, p, ny, size, lk_of, w_of):
    base = p * (ny + PAD) + PAD
    for b in range(0, ny, size):
        e = jnp.exp(0.5 * lk_of(b).astype(F32))
        at = pl.ds(pl.multiple_of(base + b, 8), size)
        e_ref[at] = e
        u_ref[at] = e * w_of(b).astype(F32)


def residual_plane(e_ref, u_ref, s_ref, r_ref, v_ref, p, ny, size, valid):
    plane = ny + PAD
    for b in range(0, ny, size):
        start = p * plane + PAD + b
        at = pl.ds(pl.multiple_of(start, 8), size)
        flat = pl.ds(pl.multiple_of(p * ny + b, 8), size)
        s, e = neighbour_sum(e_ref, start, size, plane, 1.0)
        n, u = neighbour_sum(u_ref, start, size, plane, 0.0)
        r = e * n - s * u
        if valid is not None:
            r = r * valid
        s_ref[flat] = s
        r_ref[flat] = r
        v_ref[at] = e * r


def thirds(ref):
    count = ref.shape[0] // 3
    return tuple(ref.at[pl.ds(k * count, count)] for k in range(3))


def halved(ref):
    count = ref.shape[0] // 2
    return tuple(ref.at[pl.ds(k * count, count)] for k in range(2))


def interior_kernel(rows, ny, pieces, meta, lk_in, w_in, fields, flats, lk, w, sems):
    e_ref, u_ref, v_ref = thirds(fields)
    s_ref, r_ref = halved(flats)
    depth = lk.shape[2]
    plane = ny + PAD
    planes = rows + 2 * HALO
    size = block_rows(ny)
    count = rows // pieces
    copies = []
    for piece in range(pieces):
        at = pl.ds(piece * count, count)
        for k, (source, target) in enumerate(((lk_in, lk), (w_in, w))):
            copies.append(pltpu.make_async_copy(source.at[at], target.at[at], sems.at[2 * piece + k]))
    for copy in copies:
        copy.start()
    ones = jnp.ones((PAD, depth), F32)
    zeros = jnp.zeros((PAD, depth), F32)

    def clear(p, carry):
        at = pl.ds(pl.multiple_of(p * plane, 8), PAD)
        e_ref[at] = ones
        u_ref[at] = zeros
        v_ref[at] = zeros
        return carry

    lax.fori_loop(0, planes + 1, clear, 0)

    def scale(x, carry):
        scale_plane(
            e_ref, u_ref, x + HALO, ny, size, lambda b: lk[x, b : b + size], lambda b: w[x, b : b + size]
        )
        return carry

    for piece in range(pieces):
        copies[2 * piece].wait()
        copies[2 * piece + 1].wait()
        unrolled(piece * count, (piece + 1) * count, scale, 0)

    def residual(p, carry):
        residual_plane(e_ref, u_ref, s_ref, r_ref, v_ref, p, ny, size, None)
        return carry

    unrolled(HALO + 1, HALO + rows - 1, residual, 0)


def interior(meta, lk, w):
    rows, ny, depth = lk.shape
    fields = pltpu.VMEM((3 * field_rows(rows, ny), depth), F32)
    flats = pltpu.VMEM((2 * (rows + 2 * HALO) * ny, depth), F32)
    cells = rows * ny * depth
    pieces = next(k for k in (4, 3, 2, 1) if rows % k == 0)
    return pl.pallas_call(
        functools.partial(interior_kernel, rows, ny, pieces),
        out_shape=(fields, flats),
        in_specs=[SMEM_SPEC] + [ANY_SPEC] * 2,
        out_specs=(VMEM_SPEC,) * 2,
        scratch_shapes=[
            pltpu.VMEM((rows, ny, depth), BF16),
            pltpu.VMEM((rows, ny, depth), BF16),
            pltpu.SemaphoreType.DMA((2 * pieces,)),
        ],
        compiler_params=pltpu.CompilerParams(vmem_limit_bytes=SMALL_LIMIT),
        cost_estimate=pl.CostEstimate(flops=5000 * cells, bytes_accessed=4 * cells, transcendentals=cells),
        name="interior",
    )(meta, in_hbm(lk), in_hbm(w))


def moments_kernel(
    rows, ny, count_x,
    meta, columns, residuals, ends_low, ends_high, fields_in, flats_in,
    fields, flats, held_out, mom_out, sems,
):
    e_ref, u_ref, v_ref = thirds(fields)
    s_ref, r_ref = halved(flats)
    holds = [
        pltpu.make_async_copy(ref.at[pl.ds(0, held_out.shape[1])], held_out.at[k], sems.at[k])
        for k, ref in enumerate((e_ref, u_ref, v_ref))
    ]
    depth = residuals.shape[1]
    plane = ny + PAD
    planes = rows + 2 * HALO
    size = block_rows(ny)
    blocks = range(0, ny, size)
    first_row = meta[0]

    for ends, begin in ((ends_low, 0), (ends_high, HALO + rows)):

        def scale(p, carry):
            scale_plane(
                e_ref, u_ref, p + begin, ny, size,
                lambda b: ends[HALO + p, b : b + size], lambda b: ends[p, b : b + size],
            )
            return carry

        unrolled(0, HALO, scale, 0)

    def inside(p):
        row = first_row + p - HALO
        return jnp.where((row >= 0) & (row < count_x), 1.0, 0.0).astype(F32)

    def residual(p, carry):
        residual_plane(e_ref, u_ref, s_ref, r_ref, v_ref, p, ny, size, inside(p))
        return carry

    unrolled(1, HALO + 1, residual, 0)
    unrolled(HALO + rows - 1, planes - 1, residual, 0)

    def plant(o, carry):
        column = columns[o]
        row = lax.div(column, ny)
        y = column - row * ny
        p = row - first_row + HALO

        @pl.when((p >= 1) & (p < planes - 1))
        def _():
            at = pl.ds(p * plane + PAD + y, 1)
            flat = pl.ds(p * ny + y, 1)
            added = residuals[pl.ds(o, 1)]
            r_ref[flat] = r_ref[flat] + added
            v_ref[at] = v_ref[at] + e_ref[at] * added

        return carry

    holds[0].start()
    lax.fori_loop(0, columns.shape[0], plant, 0)
    holds[2].start()

    def image(p, sums, valid, summed):
        m0, m1, m2 = sums
        base = p * plane + PAD
        for b in blocks:
            start = base + b
            at = pl.ds(pl.multiple_of(start, 8), size)
            flat = pl.ds(pl.multiple_of(p * ny + b, 8), size)
            n, v = neighbour_sum(v_ref, start, size, plane, 0.0)
            e = e_ref[at]
            y = s_ref[flat] * v - e * n
            if valid is not None:
                y = y * valid
            u_ref[at] = e * y
            if summed:
                r = r_ref[flat]
                m0 = m0 + fold(r * r)
                m1 = m1 + fold(r * y)
                m2 = m2 + fold(y * y)
                r_ref[flat] = y
        return m0, m1, m2

    zero = jnp.zeros((8, depth), F32)
    sums = (zero, zero, zero)
    image(HALO - 1, sums, inside(HALO - 1), False)
    image(HALO + rows, sums, inside(HALO + rows), False)
    m0, m1, m2 = unrolled(HALO, HALO + rows, lambda p, c: image(p, c, None, True), sums)

    holds[1].start()

    def second(p, m3):
        base = p * plane + PAD
        for b in blocks:
            start = base + b
            flat = pl.ds(pl.multiple_of(p * ny + b, 8), size)
            near = window(u_ref, start, size)
            q = near[PAD : PAD + size]
            up = jnp.where(lane_index(q.shape) == depth - 1, 0.0, pltpu.roll(q, depth - 1, 1))
            ahead = u_ref[pl.ds(pl.multiple_of(start + plane, 8), size)] + near[PAD + 1 : PAD + 1 + size] + up
            m3 = m3 + fold(q * (s_ref[flat] * r_ref[flat] - 2.0 * ahead))
        return m3

    m3 = unrolled(HALO, HALO + rows, second, zero)
    for k, m in enumerate((m0, m1, m2, m3)):
        mom_out[k] = jnp.sum(m)
    for hold in holds:
        hold.wait()


def moments(meta, columns, residuals, ends, fields, flats, rows, ny, count_x):
    depth = residuals.shape[1]
    cells = rows * ny * depth
    return pl.pallas_call(
        functools.partial(moments_kernel, rows, ny, count_x),
        out_shape=(
            pltpu.VMEM(fields.shape, F32), pltpu.VMEM(flats.shape, F32),
            jax.ShapeDtypeStruct((3, fields.shape[0] // 3 - PAD, depth), F32), jax.ShapeDtypeStruct((4,), F32),
        ),
        in_specs=[SMEM_SPEC, SMEM_SPEC] + [VMEM_SPEC] * 5,
        out_specs=(VMEM_SPEC,) * 2 + (ANY_SPEC, SMEM_SPEC),
        input_output_aliases={5: 0, 6: 1},
        scratch_shapes=[pltpu.SemaphoreType.DMA((3,))],
        compiler_params=pltpu.CompilerParams(vmem_limit_bytes=SMALL_LIMIT),
        cost_estimate=pl.CostEstimate(flops=5000 * cells, bytes_accessed=4 * cells, transcendentals=cells),
        name="moments",
    )(meta, columns, residuals, *ends, in_vmem(fields), in_vmem(flats))


def step_lengths(sums):
    m0, m1, m2, m3 = (sum(ref[k] for ref in sums) for k in range(4))
    alpha = m0 / m1
    new = alpha * alpha * m2 - 2.0 * alpha * m1 + m0
    bent = 1.0 + new / m0
    second = new / (bent * bent * m1 - 2.0 * bent * alpha * m2 + alpha * alpha * m3)
    return alpha + second * bent, -second * alpha


def misfit_kernel(rows, ny, first, size, parts, tests, terms, meta, *refs):
    sums = refs[:terms]
    (
        fields, w, h, ends_low, ends_high, bd_high, bd_low,
        mine_out, other_out, e_ref, q_ref, v_ref, w_ref, h_bf, a_ref, h_ref, x_ref, t_high, t_low, sems,
    ) = refs[terms:]
    depth = w.shape[2]
    length = rows // parts
    plane = ny + PAD
    slot_rows = size + 2 * PAD
    edge = 16
    low = edge if first > 0 else 0
    high = edge if first + size < ny else 0
    held = PAD + size + (PAD if high else 0)
    early = min(4, length)
    sem = iter(range(sems.shape[0]))
    waits = ([], [])

    def bring(source, target, group):
        copy = pltpu.make_async_copy(source, target, sems.at[next(sem)])
        copy.start()
        waits[group].append(copy)

    def bring_rows(group, begin, end):
        count = end - begin
        for k, ref in enumerate((e_ref, q_ref, v_ref)):
            bring(
                fields.at[k, pl.ds(begin + HALO - 1, count), pl.ds(first, held)],
                ref.at[pl.ds(begin, count), pl.ds(0, held)],
                group,
            )
        ys, yt = pl.ds(first - low, low + size + high), pl.ds(edge - low, low + size + high)
        for source, below, above, ref in ((w, HALO - 1, 0, w_ref), (h, 2 * HALO, 2 * HALO, h_bf)):
            lo, hi = begin, end
            if lo == 0:
                bring(ends_low.at[pl.ds(below, 1), ys], ref.at[pl.ds(0, 1), yt], group)
                lo = 1
            if hi == rows + 2:
                bring(ends_high.at[pl.ds(above, 1), ys], ref.at[pl.ds(rows + 1, 1), yt], group)
                hi = rows + 1
            if hi > lo:
                bring(source.at[pl.ds(lo - 1, hi - lo), ys], ref.at[pl.ds(lo, hi - lo), yt], group)

    for part in range(parts):
        bring_rows(0, part * length, part * length + early)
    for part in range(parts):
        end = rows + 2 if part == parts - 1 else (part + 1) * length
        if end > part * length + early:
            bring_rows(1, part * length + early, end)
    block = block_rows(size)
    blocks = range(0, size, block)
    first_row, well = meta[0], meta[1]
    c0, c1 = step_lengths(sums)
    lanes_out = mine_out.shape[2]
    chips = tests // 2
    chip, core = meta[2] // 2, meta[2] % 2

    if first + size == ny:
        beyond = jnp.ones((PAD, depth), F32)

        def fill(p, carry):
            e_ref[p, pl.ds(PAD + size, PAD)] = beyond
            return carry

        lax.fori_loop(0, rows + 2, fill, 0)
    zeros = jnp.zeros((PAD, depth), F32)
    for s in range(4 * parts):
        for at in (pl.ds(s * slot_rows, PAD), pl.ds(s * slot_rows + PAD + size, PAD)):
            a_ref[at] = zeros
            h_ref[at] = zeros

    def slot(part, i):
        return (4 * part + lax.rem(i, 4)) * slot_rows

    spans = [(b, block, 0, block) for b in blocks]
    if low:
        spans.append((-edge, edge, PAD, PAD))
    if high:
        spans.append((size, edge, 0, PAD))

    def prepare(part, i):
        base = slot(part, i)
        p = part * length + i
        for y, count, skip, keep in spans:
            at = slice(PAD + y + skip, PAD + y + skip + keep)
            to = pl.ds(pl.multiple_of(base + PAD + y + skip, 8), keep)
            wide = w_ref[p, edge + y : edge + y + count].astype(F32)[skip : skip + keep]
            a_ref[to] = e_ref[p, at] * wide + c0 * v_ref[p, at] + c1 * q_ref[p, at]
            h_ref[to] = h_bf[p, edge + y : edge + y + count].astype(F32)[skip : skip + keep]

    def rows_at(start, count):
        return pl.ds(pl.multiple_of(start, 8), count)

    def along(part):
        for b in blocks:
            at = rows_at(slot(part, 0) + PAD + b, block)
            to = rows_at(slot(part, 1) + PAD + b, block)
            e = e_ref[part * length, PAD + b : PAD + b + block]
            en = e_ref[part * length + 1, PAD + b : PAD + b + block]
            x_ref[part, b : b + block] = (en * a_ref[at] - e * a_ref[to]) * (h_ref[at] - h_ref[to])

    def centre(part, x, buffer):
        here, there = slot(part, x + 1), slot(part, x + 2)
        p = part * length + x + 1
        column = (first_row + part * length + x) * ny + first
        for b in blocks:
            to = rows_at(there + PAD + b, block)
            e_near = e_ref.at[p, b : b + block + 2 * PAD]
            a_near, h_near = (window(ref, here + PAD + b, block) for ref in (a_ref, h_ref))
            mid = slice(PAD, PAD + block)
            e, a, hh = e_near[mid], a_near[mid], h_near[mid]
            en, an, hn = e_ref[p + 1, PAD + b : PAD + b + block], a_ref[to], h_ref[to]
            before = x_ref[part, b : b + block]
            after = (en * a - e * an) * (hh - hn)
            x_ref[part, b : b + block] = after
            total = before + after
            for shift in (-1, 1):
                at = slice(PAD + shift, PAD + shift + block)
                en, an, hn = e_near[at], a_near[at], h_near[at]
                total = total + (en * a - e * an) * (hh - hn)
            lanes = lane_index(e.shape)
            end = lanes == depth - 1
            en = jnp.where(end, 1.0, pltpu.roll(e, depth - 1, 1))
            an = jnp.where(end, 0.0, pltpu.roll(a, depth - 1, 1))
            hn = jnp.where(end, 0.0, pltpu.roll(hh, depth - 1, 1))
            up = (en * a - e * an) * (hh - hn)
            down = jnp.where(lanes == 0, a * hh, pltpu.roll(up, 1, 1))
            total = -0.5 * (total + up + down)
            row = lax.broadcasted_iota(jnp.int32, e.shape, 0) + (column + b)
            total = jnp.where(row == well, 0.0, total)
            high_part, low_part = split(total)
            t_high[buffer, b : b + block, part * depth : (part + 1) * depth] = high_part
            t_low[buffer, b : b + block, part * depth : (part + 1) * depth] = low_part

    def transform(x, buffer):
        value = dot3((t_high[buffer], t_low[buffer]), (bd_high[...], bd_low[...]))
        at = rows_at(x * size, size)
        for c in range(chips):
            even, odd = (value[:, (2 * c + k) * lanes_out : (2 * c + k + 1) * lanes_out] for k in range(2))
            k = lax.rem(c + chips - chip, chips)
            mine_out[k, at] = jnp.where(core == 0, even, odd)
            other_out[k, at] = jnp.where(core == 0, odd, even)

    def step(x):
        for part in range(parts):
            prepare(part, x + 2)
        for part in range(parts):
            centre(part, x, lax.rem(x, 2))

    def loop(x, carry):
        transform(x - 1, lax.rem(x + 1, 2))
        step(x)
        return carry

    for copy in waits[0]:
        copy.wait()
    for part in range(parts):
        prepare(part, 0)
        prepare(part, 1)
        along(part)
    if parts == 1 or length <= early:
        for copy in waits[1]:
            copy.wait()
        step(0)
        lax.fori_loop(1, length, loop, 0)
    else:
        step(0)
        lax.fori_loop(1, early - 2, loop, 0)
        for copy in waits[1]:
            copy.wait()
        lax.fori_loop(early - 2, length, loop, 0)
    transform(length - 1, (length - 1) % 2)


def misfit(meta, sums, fields, w, h, ends, tables, first, size, parts, tests):
    rows, ny, depth = w.shape
    length = rows // parts
    lanes = tables[0].shape[1] // tests
    out = jax.ShapeDtypeStruct((tests // 2, length * size, lanes), F32)
    ring = pltpu.VMEM((4 * parts * (size + 2 * PAD), depth), F32)
    full = pltpu.VMEM((rows + 2, size + 2 * PAD, depth), F32)
    half = pltpu.VMEM((rows + 2, size + 32, depth), BF16)
    cells = rows * size * depth
    return pl.pallas_call(
        functools.partial(misfit_kernel, rows, ny, first, size, parts, tests, len(sums)),
        out_shape=(out, out),
        in_specs=[SMEM_SPEC] * (1 + len(sums)) + [ANY_SPEC] * 5 + [VMEM_SPEC] * 2,
        out_specs=(VMEM_SPEC, VMEM_SPEC),
        scratch_shapes=[
            full, full, full, half, half, ring, ring,
            pltpu.VMEM((parts, size, depth), F32),
            pltpu.VMEM((2, size, parts * depth), BF16),
            pltpu.VMEM((2, size, parts * depth), BF16),
            pltpu.SemaphoreType.DMA((10 * parts + 4,)),
        ],
        compiler_params=pltpu.CompilerParams(vmem_limit_bytes=MISFIT_LIMIT),
        cost_estimate=pl.CostEstimate(flops=8000 * cells, bytes_accessed=4 * cells, transcendentals=cells),
        name="misfit",
    )(meta, *sums, in_hbm(fields), in_hbm(w), in_hbm(h), *ends, *tables)


def pack_rest(rests, width, kept):
    lanes = lane_index(rests[0].shape) % width
    result = rests[0]
    for m in range(1, len(rests)):
        moved = pltpu.roll(rests[m], m * kept, 1)
        result = jnp.where((lanes >= m * kept) & (lanes < (m + 1) * kept), moved, result)
    return result


def unpack_rest(packed, count, width, kept):
    near = lane_index(packed.shape) % width < kept
    depth = packed.shape[1]
    return [
        jnp.where(near, packed if m == 0 else pltpu.roll(packed, depth - m * kept, 1), 0.0) for m in range(count)
    ]


def join_kernel(length, width, kept, mine, other, own_out, far_out):
    far_count, rows = mine.shape[0] - 1, mine.shape[1]
    size = rows // length
    share = width // kept
    block = block_rows(size)

    def add(i, carry):
        at = pl.ds(pl.multiple_of(i * size, 16), size)
        own_out[at] = mine[0, at] + other[0, at]
        return carry

    lax.fori_loop(0, length, add, 0)
    for f in range(far_count):

        def code(i, carry):
            for b in range(0, size, block):
                rests = []
                for m in range(share):
                    at = pl.ds(pl.multiple_of((i * share + m) * size + b, 16), block)
                    value = mine[1 + f, at] + other[1 + f, at]
                    high = value.astype(BF16)
                    far_out[f, at] = high
                    rests.append(value - high.astype(F32))
                at = pl.ds(pl.multiple_of(rows + i * size + b, 16), block)
                far_out[f, at] = pack_rest(rests, width, kept).astype(BF16)
            return carry

        lax.fori_loop(0, length // share, code, 0)


def join(mine, other, length, width, kept):
    chips, rows, lanes = mine.shape
    return pl.pallas_call(
        functools.partial(join_kernel, length, width, kept),
        out_shape=(
            jax.ShapeDtypeStruct((rows, lanes), F32),
            jax.ShapeDtypeStruct((chips - 1, rows + rows * kept // width, lanes), BF16),
        ),
        in_specs=[VMEM_SPEC] * 2,
        out_specs=(VMEM_SPEC,) * 2,
        compiler_params=pltpu.CompilerParams(vmem_limit_bytes=VMEM_LIMIT),
        cost_estimate=pl.CostEstimate(flops=4 * rows * lanes, bytes_accessed=16 * rows * lanes, transcendentals=0),
        name="join",
    )(mine, other)


def power(value, exponent):
    result = None
    while exponent:
        if exponent & 1:
            result = value if result is None else result * value
        exponent >>= 1
        if exponent:
            value = value * value
    return result


def ratio_of(across, deep):
    half = (1.0 + range_squared * (across + deep) + 2.0 * range_squared) / (2.0 * range_squared)
    return 1.0 / (half + jnp.sqrt(half * half - 1.0))


def by_block(values, lanes, width):
    result = values[-1]
    for j in range(len(values) - 2, -1, -1):
        result = jnp.where(lanes < (j + 1) * width, values[j], result)
    return result


def powers(value, length, count):
    step = power(value, length)
    result = [jnp.ones_like(value)]
    for _ in range(count - 1):
        result.append(result[-1] * step)
    return result


def everywhere(value, width):
    lanes = value.shape[1]
    shift = width
    while shift < lanes:
        value = value + pltpu.roll(value, shift, 1)
        shift *= 2
    return value


def solve_kernel(length, parts, width, kept, chunks, fars, meta, across, deep, *refs):
    groups = refs[:chunks]
    far_refs = refs[chunks : chunks * (1 + fars)]
    tables = refs[chunks * (1 + fars) : chunks * (3 + fars)]
    local_out, state_out, packed_out, h_ref = refs[chunks * (3 + fars) :]
    ny, lanes_count = across.shape
    size = groups[0].shape[0] // length
    pair = 2 if length % 2 == 0 else 1
    share = width // kept
    rests = {}

    def gathered(c, x):
        at = slice(x * size, (x + 1) * size)
        value = groups[c][at]
        for f in range(fars):
            ref = far_refs[c * fars + f]
            g = x // share
            if (c, f, g) not in rests:
                start = length * size + g * size
                rests[c, f, g] = unpack_rest(ref[start : start + size].astype(F32), share, width, kept)
            value = value + (ref[at].astype(F32) + rests[c, f, g][x % share])
        return value

    for g in range(0, length, pair):
        total = None
        for c in range(chunks):
            value = jnp.concatenate([gathered(c, g + k) for k in range(pair)], axis=1)
            product = dot3((tables[2 * c][...], tables[2 * c + 1][...]), split(value))
            total = product if total is None else total + product
        for k in range(pair):
            h_ref[g + k] = total[:, k * lanes_count : (k + 1) * lanes_count]

    block = block_rows(ny)
    qz = deep[pl.ds(meta[2], 1)]

    def solve(i, carry):
        at = pl.ds(pl.multiple_of(i * block, 16), block)
        rho = ratio_of(across[at], qz)
        square = rho * rho
        tilt = (1.0 + square) / (1.0 - square)
        p1 = jnp.zeros_like(rho)
        p2 = jnp.zeros_like(rho)
        for x in range(length):
            p2 = rho * (p2 + p1)
            p1 = h_ref[x, at] + rho * p1
            local_out[x, at] = p2 + tilt * p1
        n1 = jnp.zeros_like(rho)
        n2 = jnp.zeros_like(rho)
        for x in range(length - 1, -1, -1):
            local_out[x, at] = local_out[x, at] + (n2 + tilt * n1)
            n1 = rho * (n1 + h_ref[x, at])
            n2 = rho * n2 + n1
        if parts == 1:
            for k, value in enumerate((p1, p2, n1, n2)):
                state_out[k, at] = jnp.zeros_like(rho)
                packed_out[k, at] = value
            return carry
        lanes = lane_index(rho.shape)
        steps = powers(rho, length, parts)
        zero = jnp.zeros_like(rho)
        into = [zero] * 4
        for s in range(1, parts):
            weight = jnp.where(lanes >= s * width, steps[s - 1], 0.0)
            far = float(length * (s - 1))
            one, two = (pltpu.roll(value, s * width, 1) for value in (p1, p2))
            into[0] = into[0] + weight * one
            into[1] = into[1] + weight * (two + far * one)
            weight = jnp.where(lanes < (parts - s) * width, steps[s - 1], 0.0)
            one, two = (pltpu.roll(value, lanes_count - s * width, 1) for value in (n1, n2))
            into[2] = into[2] + weight * one
            into[3] = into[3] + weight * (two + far * one)
        for k in range(4):
            state_out[k, at] = into[k]
        place = lanes // width
        weight = by_block(steps[::-1], lanes, width)
        far = ((parts - 1 - place) * length).astype(F32)
        d1 = everywhere(weight * p1, width)
        d2 = everywhere(weight * (p2 + far * p1), width)
        weight = by_block(steps, lanes, width)
        far = (place * length).astype(F32)
        e1 = everywhere(weight * n1, width)
        e2 = everywhere(weight * (n2 + far * n1), width)
        packed_out[at] = by_block([d1, d2, e1, e2], lanes, width)
        return carry

    lax.fori_loop(0, ny // block, solve, 0)


def solve(meta, across, deep, groups, fars, tables, length, parts, width, kept):
    ny, lanes = across.shape
    chunks = len(groups)
    packed = (ny, lanes) if parts == 4 else (4, ny, lanes)
    cells = length * ny * lanes
    return pl.pallas_call(
        functools.partial(solve_kernel, length, parts, width, kept, chunks, len(fars) // chunks),
        out_shape=(
            jax.ShapeDtypeStruct((length, ny, lanes), F32),
            jax.ShapeDtypeStruct((4, ny, lanes), F32),
            jax.ShapeDtypeStruct(packed, F32),
        ),
        in_specs=[SMEM_SPEC] + [VMEM_SPEC] * (2 + 3 * chunks + len(fars)),
        out_specs=(VMEM_SPEC,) * 3,
        scratch_shapes=[pltpu.VMEM((length, ny, lanes), F32)],
        compiler_params=pltpu.CompilerParams(vmem_limit_bytes=VMEM_LIMIT),
        cost_estimate=pl.CostEstimate(flops=6 * cells * ny, bytes_accessed=16 * cells, transcendentals=0),
        name="solve",
    )(meta, across, deep, *groups, *fars, *tables)


def peer(test, chips, hop, which):
    return 2 * lax.rem(test // 2 + hop, chips) + lax.rem(test % 2 + which, 2)


def finish_kernel(length, parts, width, kept, spaces, tests, scale, meta, across, deep, local, state, *refs):
    packed = refs[:spaces]
    c_high, c_low, *outs = refs[spaces : -4]
    v_ref, v_high, v_low, total_ref = refs[-4:]
    ny, lanes_count = across.shape
    block = block_rows(ny)
    qz = deep[pl.ds(meta[2], 1)]
    slab = length * parts

    def correct(i, carry):
        at = pl.ds(pl.multiple_of(i * block, 16), block)
        rho = ratio_of(across[at], qz)
        square = rho * rho
        tilt = (1.0 + square) / (1.0 - square)
        gain = rho / (2.0 * range_squared * 0.5 * (1.0 - square))
        gain = (prior_gain * scale) * gain * gain
        lanes = lane_index(rho.shape)
        step = power(rho, slab)
        weight = jnp.ones_like(rho)
        if parts > 1:
            near = far = jnp.zeros_like(rho)
            for k in range(1, spaces + 1):
                left = packed[k % spaces][at].astype(F32)
                right = packed[(spaces - k) % spaces][at].astype(F32)
                value = weight * jnp.where(lanes < 2 * width, left, right)
                near = near + value
                far = far + float(slab * (k - 1)) * value
                weight = weight * step

            def pick(value, s):
                return everywhere(jnp.where((lanes >= s * width) & (lanes < (s + 1) * width), value, 0.0), width)

            one, two, far_one = pick(near, 0), pick(near, 1), pick(far, 0)
            back_one, back_two, back_far = pick(near, 2), pick(near, 3), pick(far, 2)
        else:
            one = two = far_one = back_one = back_two = back_far = jnp.zeros_like(rho)
            for k in range(1, spaces + 1):
                left, right = packed[k % spaces], packed[(spaces - k) % spaces]
                first = weight * left[0, at]
                one = one + first
                two = two + weight * left[1, at]
                far_one = far_one + float(slab * (k - 1)) * first
                first = weight * right[2, at]
                back_one = back_one + first
                back_two = back_two + weight * right[3, at]
                back_far = back_far + float(slab * (k - 1)) * first
                weight = weight * step
        around = 1.0 / (1.0 - weight)
        again = float(slab * spaces) * weight * around * around
        two = around * (two + far_one) + again * one
        one = around * one
        back_two = around * (back_two + back_far) + again * back_one
        back_one = around * back_one
        if parts > 1:
            steps = powers(rho, length, parts)
            place = lanes // width
            weight = by_block(steps, lanes, width)
            two = weight * (two + (place * length).astype(F32) * one)
            one = weight * one
            weight = by_block(steps[::-1], lanes, width)
            back_two = weight * (back_two + ((parts - 1 - place) * length).astype(F32) * back_one)
            back_one = weight * back_one
        one = one + state[0, at]
        two = two + state[1, at]
        back_one = back_one + state[2, at]
        back_two = back_two + state[3, at]
        for x in range(length):
            two = rho * (two + one)
            one = rho * one
            v_ref[x, at] = local[x, at] + (two + tilt * one)
        for x in range(length - 1, -1, -1):
            value = gain * (v_ref[x, at] + (back_two + tilt * back_one))
            v_high[x, at], v_low[x, at] = split(value)
            back_one = rho * back_one
            back_two = rho * back_two + back_one
        return carry

    lax.fori_loop(0, ny // block, correct, 0)
    pair = 2 if length % 2 == 0 else 1
    rows = ny // tests
    four = total_ref.shape[0]
    for start in range(0, length, four):
        for g in range(0, four, pair):
            right = tuple(
                jnp.concatenate([ref[start + g + k] for k in range(pair)], axis=1) for ref in (v_high, v_low)
            )
            total = dot3((c_high[...], c_low[...]), right)
            for k in range(pair):
                total_ref[g + k] = total[:, k * lanes_count : (k + 1) * lanes_count]
        if not kept:
            for g in range(four):
                for t in range(tests):
                    outs[0][t, start + g] = total_ref[g, t * rows : (t + 1) * rows]
            continue
        chips = tests // 2
        for hop in range(chips):
            for which in range(2):
                out = outs[2 * hop + which]
                at = pl.ds(pl.multiple_of(peer(meta[2], chips, hop, which) * rows, 8), rows)
                values = [total_ref[g, at] for g in range(four)]
                if hop == 0:
                    for g in range(four):
                        out[(start + g) * rows : (start + g + 1) * rows] = values[g]
                    continue
                highs = [value.astype(BF16).astype(F32) for value in values]
                rests = [value - high for value, high in zip(values, highs)]
                for g in range(0, four, 2):
                    place = (start + g) * rows
                    out[place : place + 2 * rows] = jnp.concatenate(highs[g : g + 2], axis=0).astype(BF16)
                share = width // kept
                packs = [pack_rest(rests[g : g + share], width, kept) for g in range(0, four, share)]
                place = length * rows + start * rows // share
                out[place : place + four * rows // share] = jnp.concatenate(packs, axis=0).astype(BF16)


def finish(meta, across, deep, local, state, packed, tables, parts, width, kept, tests, scale):
    length, ny, lanes = local.shape
    spaces = len(packed)
    cells = length * ny * lanes
    rows = length * (ny // tests)
    if kept:
        out = [jax.ShapeDtypeStruct((rows, lanes), F32)] * 2
        out += [jax.ShapeDtypeStruct((rows + rows * kept // width, lanes), BF16)] * (tests - 2)
    else:
        out = [jax.ShapeDtypeStruct((tests, length, ny // tests, lanes), F32)]
    return pl.pallas_call(
        functools.partial(finish_kernel, length, parts, width, kept, spaces, tests, scale),
        out_shape=tuple(out),
        in_specs=[SMEM_SPEC] + [VMEM_SPEC] * (6 + spaces),
        out_specs=(VMEM_SPEC,) * len(out),
        scratch_shapes=[
            pltpu.VMEM((length, ny, lanes), F32),
            pltpu.VMEM((length, ny, lanes), BF16),
            pltpu.VMEM((length, ny, lanes), BF16),
            pltpu.VMEM((4 if length % 4 == 0 else length, ny, lanes), F32),
        ],
        compiler_params=pltpu.CompilerParams(vmem_limit_bytes=VMEM_LIMIT),
        cost_estimate=pl.CostEstimate(flops=6 * cells * ny, bytes_accessed=16 * cells, transcendentals=0),
        name="finish",
    )(meta, across, deep, local, state, *packed, *tables)


def depth_kernel(tests, parts, depth, pieces, bd_high, bd_low, out):
    rows = pieces.shape[1]
    value = jnp.concatenate([pieces[t] for t in range(tests)], axis=1)
    result = dot3(split(value), (bd_high[...], bd_low[...]))
    for j in range(parts):
        out[j] = result[:, j * depth : (j + 1) * depth]


def depth_cells(pieces, tables, parts, depth):
    tests, rows, lanes = pieces.shape
    steps = 3 if rows % 24 == 0 else 1
    return pl.pallas_call(
        functools.partial(depth_kernel, tests, parts, depth),
        out_shape=jax.ShapeDtypeStruct((parts, rows, depth), F32),
        grid=(steps,),
        in_specs=[
            pl.BlockSpec((tests, rows // steps, lanes), lambda i: (0, i, 0)),
            pl.BlockSpec(tables[0].shape, lambda i: (0, 0)),
            pl.BlockSpec(tables[1].shape, lambda i: (0, 0)),
        ],
        out_specs=pl.BlockSpec((parts, rows // steps, depth), lambda i: (0, i, 0)),
        compiler_params=pltpu.CompilerParams(vmem_limit_bytes=VMEM_LIMIT),
        cost_estimate=pl.CostEstimate(
            flops=6 * tests * rows * lanes * parts * depth, bytes_accessed=8 * tests * rows * lanes, transcendentals=0
        ),
        name="depth_cells",
    )(pieces, *tables)


def depth_coded_kernel(tests, parts, depth, width, kept, meta, *refs):
    out = refs[-1]
    bd_high, bd_low = refs[-3:-1]
    pieces = refs[:-3]
    chips = tests // 2
    share = width // kept
    values, places = [pieces[0][...], pieces[1][...]], [meta[2], peer(meta[2], chips, 0, 1)]
    for hop in range(1, chips):
        for which in range(2):
            k = 2 + 2 * (2 * (hop - 1) + which)
            high, rest = pieces[k], pieces[k + 1]
            rows = high.shape[0] // 4
            packed = rest[...].astype(F32)
            rests = []
            for g in range(4 // share):
                rests += unpack_rest(packed[g * rows : (g + 1) * rows], share, width, kept)
            values.append(high[...].astype(F32) + jnp.concatenate(rests, axis=0))
            places.append(peer(meta[2], chips, chips - hop, which))
    lanes = values[0].shape[1]
    high, low = (
        jnp.concatenate([ref[pl.ds(pl.multiple_of(place * lanes, lanes), lanes)] for place in places], axis=0)
        for ref in (bd_high, bd_low)
    )
    result = dot3(split(jnp.concatenate(values, axis=1)), (high, low))
    for j in range(parts):
        out[j] = result[:, j * depth : (j + 1) * depth]


def depth_coded(meta, pieces, tables, tests, parts, depth, width, kept, length):
    rows, lanes = pieces[0].shape
    steps = length // 4
    block = rows // steps
    share = width // kept
    specs = [pl.BlockSpec((block, lanes), lambda i: (i, 0))] * 2
    args = list(pieces[:2])
    for piece in pieces[2:]:
        specs.append(pl.BlockSpec((block, lanes), lambda i: (i, 0)))
        specs.append(pl.BlockSpec((block // share, lanes), lambda i: (share * steps + i, 0)))
        args += [piece, piece]
    whole = pl.BlockSpec(tables[0].shape, lambda i: (0, 0))
    return pl.pallas_call(
        functools.partial(depth_coded_kernel, tests, parts, depth, width, kept),
        out_shape=jax.ShapeDtypeStruct((parts, rows, depth), F32),
        grid=(steps,),
        in_specs=[SMEM_SPEC] + specs + [whole, whole],
        out_specs=pl.BlockSpec((parts, block, depth), lambda i: (0, i, 0)),
        compiler_params=pltpu.CompilerParams(vmem_limit_bytes=VMEM_LIMIT),
        cost_estimate=pl.CostEstimate(
            flops=6 * tests * rows * lanes * parts * depth, bytes_accessed=8 * tests * rows * lanes, transcendentals=0
        ),
        name="depth_cells",
    )(meta, *args, *tables)


def on_device(log_k, heads, warm_adjoint, obs_columns, obs_residuals, well_columns):
    rows, ny, depth = log_k.shape
    spaces = lax.axis_size("space")
    tests = lax.axis_size("test")
    rank = lax.axis_index("space")
    test = lax.axis_index("test")
    chips = tests // 2
    width = depth // tests
    parts = depth // width if depth // width == 4 and rows % 4 == 0 else 1
    length = rows // parts
    lanes = depth
    count_x = rows * spaces

    w, h = warm_adjoint[0], heads[0]
    ends = (
        lax.ppermute(
            jnp.concatenate([w[rows - HALO :], log_k[rows - HALO :], h[rows - 1 :]]),
            "space", [(i, i + 1) for i in range(spaces - 1)],
        ),
        lax.ppermute(
            jnp.concatenate([w[:HALO], log_k[:HALO], h[:1]]),
            "space", [(i + 1, i) for i in range(spaces - 1)],
        ),
    )

    meta = jnp.stack([rank * rows, well_columns[0], test, rank]).astype(jnp.int32)

    fields, flats = interior(meta, log_k, w)
    _, _, fields, sums = moments(
        meta, obs_columns[0], obs_residuals[0], ends, fields, flats, rows, ny, count_x
    )
    if spaces <= 8:
        turns = [[(i, (i + k) % spaces) for i in range(spaces)] for k in range(1, spaces)]
        sums = [sums] + [lax.ppermute(sums, "space", turn) for turn in turns]
    else:
        sums = [lax.psum(sums, "space")]

    fields = fields.reshape(3, rows + 2 * HALO, ny + PAD, depth)

    cas_z = cas(depth)
    order = np.argsort(np.minimum(np.arange(depth), depth - np.arange(depth)), kind="stable")
    forward_z = np.zeros((parts, depth, tests, lanes))
    inverse_z = np.zeros((tests, lanes, parts, depth))
    kappa_z = np.zeros((tests, lanes))
    for t in range(tests):
        chosen = order[t::tests]
        for j in range(parts):
            at = slice(j * width, (j + 1) * width)
            forward_z[j, :, t, at] = cas_z[:, chosen]
            inverse_z[t, at, j, :] = cas_z[chosen, :]
            kappa_z[t, at] = kappa(depth)[chosen]
    forward_z = halves(forward_z.reshape(parts * depth, tests * lanes))
    inverse_z = halves(inverse_z.reshape(tests * lanes, parts * depth))
    deep = kappa_z.astype(np.float32)
    across = np.repeat(kappa(ny)[:, None], lanes, axis=1).astype(np.float32)
    cas_y = cas(ny)

    chunks = 2 if (ny // 2) % 48 == 0 else 1
    size = ny // chunks
    other_core = [(i, i ^ 1) for i in range(tests)]
    coded = parts > 1 and length % 4 == 0 and size % 16 == 0
    groups, fars, tables = [], [], []
    for c in range(chunks):
        mine, other = misfit(meta, sums, fields, w, h, ends, forward_z, c * size, size, parts, tests)
        if fars:
            other, fars[-1] = lax.optimization_barrier((other, fars[-1]))
        other = lax.ppermute(other, "test", other_core)
        hops = [[(i, (i + 2 * k) % tests) for i in range(tests)] for k in range(1, chips)]
        if coded:
            total, far = join(mine, other, length, width, width // 4)
            fars += [lax.ppermute(far[k], "test", hop) for k, hop in enumerate(hops)]
            far, *sums = lax.optimization_barrier((far, *sums))
        else:
            summed = mine + other
            total = summed[0]
            for k, hop in enumerate(hops, 1):
                total = total + lax.ppermute(summed[k], "test", hop)
        groups.append(total)
        tables += halves(cas_y[:, c * size : (c + 1) * size])

    local, state, packed = solve(
        meta, across, deep, groups, fars, tables, length, parts, width, width // 4
    )
    if spaces <= 8:
        wide = 0.61**rows > 1e-4
        gathered = [packed]
        for k, turn in enumerate(turns, 1):
            near = wide or k in (1, spaces - 1)
            gathered.append(lax.ppermute(packed if near else packed.astype(BF16), "space", turn))
    else:
        gathered = jnp.take(lax.all_gather(packed, "space"), (rank - jnp.arange(spaces)) % spaces, axis=0)
        gathered = [gathered[k] for k in range(spaces)]
    kept = width // 2 if coded and (ny // tests) % 8 == 0 else 0
    pieces = finish(
        meta, across, deep, local, state, gathered, halves(cas_y), parts, width, kept, tests, 1.0 / (ny * depth)
    )
    if kept:
        arrived = [pieces[0]]
        for k in range(1, tests):
            hop, which = divmod(k, 2)
            turn = [(i, 2 * ((i // 2 + hop) % chips) + (i % 2 + which) % 2) for i in range(tests)]
            arrived.append(lax.ppermute(pieces[k], "test", turn))
        result = depth_coded(meta, arrived, inverse_z, tests, parts, depth, width, kept, length)
    else:
        pieces = pieces[0].reshape(tests, length * (ny // tests), lanes)
        pieces = lax.all_to_all(pieces, "test", split_axis=0, concat_axis=0, tiled=True)
        result = depth_cells(pieces, inverse_z, parts, depth)
    return result.reshape(rows, ny // tests, depth)


def solution(mesh):
    placed = (
        P(("groups", "space"), None, None),
        P("test", ("groups", "space"), None, None),
        P("test", ("groups", "space"), None, None),
        P("test", "groups"),
        P("test", "groups", None),
        P(("groups", "test")),
    )
    return jax.shard_map(
        on_device,
        mesh=mesh,
        in_specs=placed,
        out_specs=P(("groups", "space"), "test", None),
        check_vma=False,
    )
```

time: 230 us -> 151 us (0.66)
  blocking collectives: 56.6 us -> 0 us
  Pallas kernels: 99.5 us -> 73.8 us
  waiting for transfers between devices: 36.3 us -> 48.5 us
  between operations: 6.14 us -> 0.95 us
    all_to_all x1 -> x0, blocking collectives: 26.6 us -> none  [on_device(): lax.all_to_all(pieces, 'test', split_axis=0, concat_axis=0, tiled=True)]
    pallas_call x1, Pallas kernels: 36.5 us -> 13.9 us  [moments(): pl.pallas_call(functools.partial(moments_kernel, rows, ny, count_x), out_...]
    all_gather x1 -> x0, blocking collectives: 16.9 us -> none  [on_device(): gathered = lax.all_gather(packed, 'space')]
    psum x1 -> x0, blocking collectives: 13.2 us -> none  [on_device(): m0, m1, m2, m3 = lax.psum(sums, 'space')]
    ppermute x10 -> x15, waiting for transfers between devices: 36.3 us -> 48.5 us  [the longest x3 15 us: on_device(): arrived.append(lax.ppermute(pieces[k], 'test', turn))]
    pallas_call x2, Pallas kernels: 44.4 us -> 33.6 us  [misfit(): pl.pallas_call(functools.partial(misfit_kernel, rows, ny, first, size, pa...]
    pallas_call x3 -> x6, Pallas kernels: 18.5 us -> 26.4 us  [the longest x1 12.8 us: interior(): pl.pallas_call(functools.partial(interior_kernel, rows, ny, pieces), out_...]
    add x4 -> x0, other arithmetic: 2.41 us -> none  [the longest x2 2.06 us: on_device(): total + lax.ppermute(summed[k], 'test', [(i, (i + 2 * k) % tests) for i i...]
  transfers between devices with their start and end apart: 10 -> 15, of which waited for: 3 -> 9; matrix products, arithmetic and copies ran while one was open for 2% -> 0% of each run, Pallas kernels for 26% -> 20%
where the time goes in v2:
time: 151 us; the launch traced here: 150 us
  Pallas kernels  73.8 us (49%)
  waiting for transfers between devices  48.5 us (32%)
  starting transfers between devices  19.5 us (13%)
  local copies, waits for them, and re-layouts  6.8 us (5%)
    pallas_call x2, Pallas kernels, misfit(): pl.pallas_call(functools.partial(misfit_kernel, rows, ny, first, size, pa...  33.6 us
    ppermute x3, waiting for transfers between devices, on_device(): arrived.append(lax.ppermute(pieces[k], 'test', turn))  15 us
    ppermute x2, waiting for transfers between devices, on_device(): fars += [lax.ppermute(far[k], 'test', hop) for k, hop in enumerate(hops)]  14 us
    pallas_call x1, Pallas kernels, moments(): pl.pallas_call(functools.partial(moments_kernel, rows, ny, count_x), out_...  13.9 us
    pallas_call x1, Pallas kernels, interior(): pl.pallas_call(functools.partial(interior_kernel, rows, ny, pieces), out_...  12.8 us
    ppermute x3, waiting for transfers between devices, on_device(): lax.ppermute(packed if near else packed.astype(BF16), 'space', turn)  7.54 us
    ppermute x2, waiting for transfers between devices, on_device(): other = lax.ppermute(other, 'test', other_core)  7.36 us
    ppermute x3, starting transfers between devices, on_device(): sums = [sums] + [lax.ppermute(sums, 'space', turn) for turn in turns]  5.7 us
  transfers between devices with their start and end apart: 15, of which 9 were waited for; matrix products, arithmetic and copies ran while one was open for 0% of the time, Pallas kernels for 20%

profile of v2, /device:TPU:0, one launch (start us, length us, event | category | flops | bytes accessed | tf_op | source)
XLA Modules:
  0.0 150.3 jit_solution(16136144895363530942)
XLA Ops:
  0.0 0.9 slice_bitcast_fusion.2
  0.9 1.1 fusion
  2.0 1.1 slice_bitcast_fusion
  3.2 5.0 %collective-permute-start = (bf16[7,288,128]{2,1,0:T(8,128)(2,1)S(1)}, bf16[7,288,128]{2,1,0:T(8,128)(2,1)S(1)}, u32[]{:S(2)}, u32[]{:S(2)}) collective-permute-start(bf16[7,288,128]{2,1,0:T(8,128)(2,1)S(1)} %pad_maximum_fusion), channel_id=1, source_target_pairs={{0,4},{4,8},{8,12},{1,5},{5,9},{9,13},{2,6},{6,10},{10,14},{3,7},{... | collective-permute-start | bytes 1548296 | tf_op jit(solution)/shard_map/ppermute | solution.py:1003
  8.2 1.3 collective-permute-start.1
  10.7 12.8 %interior.1 = (f32[47976,128]{1,0:T(8,128)S(1)}, f32[31104,128]{1,0:T(8,128)S(1)}) custom-call(s32[4]{0:T(128)} %pad_add_fusion.meta, bf16[48,288,128]{2,1,0:T(8,128)(2,1)} %lk_in.1, bf16[48,288,128]{2,1,0:T(8,128)(2,1)} %bitcast.23), custom_call_target="tpu_custom_call" | custom-call | flops 8847360000 | bytes 7077888 | tf_op jit(solution)/shard_map/interior/pallas_call | solution.py:194
  23.6 0.8 copy-done
  24.6 13.9 %moments.1 = (f32[47976,128]{1,0:T(8,128)S(1)}, f32[31104,128]{1,0:T(8,128)S(1)}, f32[3,15984,128]{2,1,0:T(8,128)}, f32[4]{0:T(128)}) custom-call(s32[4]{0:T(128)} %pad_add_fusion.meta, s32[64]{0:T(128)} %bitcast.29, f32[64,128]{1,0:T(8,128)} %bitcast.28, bf16[7,288,128]{2,1,0:T(8,128)(2,1)} %copy-done, ...), custom_call_target="tpu_custom_call", output_to_operand_aliasing={{0}: (5, {}), {1}: (6, {})} | custom-call | flops 8847360000 | bytes 7077888 | tf_op jit(solution)/shard_map/moments/pallas_call | solution.py:321
  38.5 4.7 %collective-permute-start.4 = (f32[4]{0:T(128)}, f32[4]{0:T(128)S(1)}, u32[]{:S(2)}, u32[]{:S(2)}) collective-permute-start(f32[4]{0:T(128)} %get-tuple-element.38.refs_0_), channel_id=1, source_target_pairs={{0,12},{4,0},{8,4},{12,8},{1,13},{5,1},{9,5},{13,9},{2,14},{6,2},{... | collective-permute-start | bytes 56 | tf_op jit(solution)/shard_map/ppermute | solution.py:1021
  43.2 1.0 collective-permute-start.2
  44.7 3.1 %collective-permute-done.3.refs_2_ = f32[4]{0:T(128)S(1)} collective-permute-done((f32[4]{0:T(128)}, f32[4]{0:T(128)S(1)}, u32[]{:S(2)}, u32[]{:S(2)}) %collective-permute-start.3) | collective-permute-done | bytes 48 | tf_op jit(solution)/shard_map/ppermute | solution.py:1021
  47.8 0.9 collective-permute-done.2.refs_1_
  48.8 1.0 copy-done.1
  49.8 1.0 copy-done.3
  51.4 16.9 %misfit.2 = (f32[2,1728,128]{2,1,0:T(8,128)S(1)}, f32[2,1728,128]{2,1,0:T(8,128)S(1)}) custom-call(s32[4]{0:T(128)S(1)} %copy-done.15, f32[4]{0:T(128)S(1)} %copy-done.17, f32[4]{0:T(128)S(1)} %collective-permute-done.2.refs_1_, f32[4]{0:T(128)S(1)} %collective-permute-done.3.refs_2_, f32[4]{0:T(128)S(1)} %collective-permute-done.4.refs_3_, ...), custom_call_target="tpu_custom_call" | custom-call | flops 7077888000 | bytes 3538944 | tf_op jit(solution)/shard_map/misfit/pallas_call | solution.py:529
  68.4 3.7 %collective-permute-done.5.other = f32[2,1728,128]{2,1,0:T(8,128)S(1)} collective-permute-done((f32[2,1728,128]{2,1,0:T(8,128)S(1)}, f32[2,1728,128]{2,1,0:T(8,128)S(1)}, u32[]{:S(2)}, u32[]{:S(2)}) %collective-permute-start.5) | collective-permute-done | bytes 1769504 | tf_op jit(solution)/shard_map/ppermute | solution.py:1054
  72.6 1.6 %collective-permute-start.6 = (bf16[2160,128]{1,0:T(8,128)(2,1)S(1)}, bf16[2160,128]{1,0:T(8,128)(2,1)S(1)}, u32[]{:S(2)}, u32[]{:S(2)}) collective-permute-start(bf16[2160,128]{1,0:T(8,128)(2,1)S(1)} %bitcast.19), channel_id=1, source_target_pairs={{0,2},{1,3},{2,0},{3,1},{4,6},{5,7},{6,4},{7,5},{8,10},{9,11},{10,... | collective-permute-start | bytes 1658888 | tf_op jit(solution)/shard_map/ppermute | solution.py:1058
  74.1 16.6 %misfit.3 = (f32[2,1728,128]{2,1,0:T(8,128)S(1)}, f32[2,1728,128]{2,1,0:T(8,128)S(1)}) custom-call(s32[4]{0:T(128)S(1)} %copy-done.15, f32[4]{0:T(128)S(1)} %copy-done.17, f32[4]{0:T(128)S(1)} %collective-permute-done.2.refs_1_, f32[4]{0:T(128)S(1)} %collective-permute-done.3.refs_2_, f32[4]{0:T(128)S(1)} %collective-permute-done.4.refs_3_, ...), custom_call_target="tpu_custom_call" | custom-call | flops 7077888000 | bytes 3538944 | tf_op jit(solution)/shard_map/misfit/pallas_call | solution.py:529
  90.9 3.7 %collective-permute-done.7.other = f32[2,1728,128]{2,1,0:T(8,128)S(1)} collective-permute-done((f32[2,1728,128]{2,1,0:T(8,128)S(1)}, f32[2,1728,128]{2,1,0:T(8,128)S(1)}, u32[]{:S(2)}, u32[]{:S(2)}) %collective-permute-start.7) | collective-permute-done | bytes 1769504 | tf_op jit(solution)/shard_map/ppermute | solution.py:1054
  95.1 0.6 collective-permute-start.8
  95.7 14.0 %collective-permute-done.8.refs_3_ = bf16[2160,128]{1,0:T(8,128)(2,1)S(1)} collective-permute-done((bf16[2160,128]{1,0:T(8,128)(2,1)S(1)}, bf16[2160,128]{1,0:T(8,128)(2,1)S(1)}, u32[]{:S(2)}, u32[]{:S(2)}) %collective-permute-start.8) | collective-permute-done | bytes 552992 | tf_op jit(solution)/shard_map/ppermute | solution.py:1058
  109.8 4.4 %solve.1 = (f32[12,288,128]{2,1,0:T(8,128)S(1)}, f32[4,288,128]{2,1,0:T(8,128)S(1)}, f32[288,128]{1,0:T(8,128)S(1)}) custom-call(s32[4]{0:T(128)S(1)} %copy-done.15, f32[288,128]{1,0:T(8,128)S(1)} %copy-done.6, f32[4,128]{1,0:T(4,128)S(1)} %copy-done.16, f32[1728,128]{1,0:T(8,128)S(1)} %get-tuple-element.36.refs_0_, ...), custom_call_target="tpu_custom_call" | custom-call | flops 764411904 | bytes 7077888 | tf_op jit(solution)/shard_map/solve/pallas_call | solution.py:743
  114.2 0.7 collective-permute-start.11
  114.8 1.4 collective-permute-start.9
  116.3 1.2 collective-permute-start.10
  117.4 7.5 %collective-permute-done.10.refs_2_ = bf16[288,128]{1,0:T(8,128)(2,1)S(1)} collective-permute-done((bf16[288,128]{1,0:T(8,128)(2,1)S(1)}, bf16[288,128]{1,0:T(8,128)(2,1)S(1)}, u32[]{:S(2)}, u32[]{:S(2)}) %collective-permute-start.10) | collective-permute-done | bytes 73760 | tf_op jit(solution)/shard_map/ppermute | solution.py:1076
  125.0 4.8 %finish.1 = (f32[864,128]{1,0:T(8,128)S(1)}, f32[864,128]{1,0:T(8,128)S(1)}, bf16[1296,128]{1,0:T(8,128)(2,1)S(1)}, bf16[1296,128]{1,0:T(8,128)(2,1)S(1)}) custom-call(s32[4]{0:T(128)S(1)} %copy-done.15, f32[288,128]{1,0:T(8,128)S(1)} %copy-done.6, f32[4,128]{1,0:T(4,128)S(1)} %copy-done.16, f32[12,288,128]{2,1,0:T(8,128)S(1)} %get-tuple-element.48.local, ...), custom_call_target="tpu_custom_call" | custom-call | flops 764411904 | bytes 7077888 | tf_op jit(solution)/shard_map/finish/pallas_call | solution.py:888
  129.9 0.6 collective-permute-start.13
  130.5 1.3 collective-permute-start.14
  131.8 8.8 %collective-permute-done.13.refs_2_.refs_3_ = bf16[1296,128]{1,0:T(8,128)(2,1)S(1)} collective-permute-done((bf16[1296,128]{1,0:T(8,128)(2,1)S(1)}, bf16[1296,128]{1,0:T(8,128)(2,1)S(1)}, u32[]{:S(2)}, u32[]{:S(2)}) %collective-permute-start.13) | collective-permute-done | bytes 331808 | tf_op jit(solution)/shard_map/ppermute | solution.py:1089
  140.6 6.2 %collective-permute-done.14.refs_4_.refs_5_ = bf16[1296,128]{1,0:T(8,128)(2,1)S(1)} collective-permute-done((bf16[1296,128]{1,0:T(8,128)(2,1)S(1)}, bf16[1296,128]{1,0:T(8,128)(2,1)S(1)}, u32[]{:S(2)}, u32[]{:S(2)}) %collective-permute-start.14) | collective-permute-done | bytes 331808 | tf_op jit(solution)/shard_map/ppermute | solution.py:1089
  146.8 3.5 %depth_cells.1 = f32[4,864,128]{2,1,0:T(8,128)} custom-call(s32[4]{0:T(128)S(1)} %copy-done.15, f32[864,128]{1,0:T(8,128)S(1)} %get-tuple-element.51.refs_0_, f32[864,128]{1,0:T(8,128)S(1)} %collective-permute-done.12.refs_1_, bf16[1296,128]{1,0:T(8,128)(2,1)S(1)} %collective-permute-done.13.refs_2_.refs_3_, ...), custom_call_target="tpu_custom_call" | custom-call | flops 1358954496 | bytes 3538944 | tf_op jit(solution)/shard_map/depth_cells/pallas_call | solution.py:974
  (50 shorter events, 3.3 us)
Async XLA Ops:
  3.2 20.4 %collective-permute-start = (bf16[7,288,128]{2,1,0:T(8,128)(2,1)S(1)}, bf16[7,288,128]{2,1,0:T(8,128)(2,1)S(1)}, u32[]{:S(2)}, u32[]{:S(2)}) collective-permute-start(bf16[7,288,128]{2,1,0:T(8,128)(2,1)S(1)} %pad_maximum_fusion), channel_id=1, source_target_pairs={{0,4},{4,8},{8,12},{1,5},{5,9},{9,13},{2,6},{6,10},{10,14},{3,7},{... | collective-permute-start | bytes 1548296 | tf_op jit(solution)/shard_map/ppermute | solution.py:1003
  8.2 15.4 %collective-permute-start.1 = (bf16[7,288,128]{2,1,0:T(8,128)(2,1)S(1)}, bf16[7,288,128]{2,1,0:T(8,128)(2,1)S(1)}, u32[]{:S(2)}, u32[]{:S(2)}) collective-permute-start(bf16[7,288,128]{2,1,0:T(8,128)(2,1)S(1)} %pad_maximum_fusion.1), channel_id=1, source_target_pairs={{4,0},{8,4},{12,8},{5,1},{9,5},{13,9},{6,2},{10,6},{14,10},{7,3},{... | collective-permute-start | bytes 1548296 | tf_op jit(solution)/shard_map/ppermute | solution.py:1007
  23.6 0.8 copy-start
  23.6 1.0 copy-start.2
  24.6 24.2 %copy-start.4 = (bf16[512,512]{1,0:T(8,128)(2,1)S(1)}, bf16[512,512]{1,0:T(8,128)(2,1)}, u32[]{:S(2)}) copy-start(bf16[512,512]{1,0:T(8,128)(2,1)} %constant.34.clone.refs_10_) | copy-start | bytes 1572868
  24.6 24.2 %copy-start.5 = (bf16[512,512]{1,0:T(8,128)(2,1)S(1)}, bf16[512,512]{1,0:T(8,128)(2,1)}, u32[]{:S(2)}) copy-start(bf16[512,512]{1,0:T(8,128)(2,1)} %constant.33.clone.refs_9_) | copy-start | bytes 1572868
  24.6 24.2 %copy-start.15 = (s32[4]{0:T(128)S(1)}, s32[4]{0:T(128)}, u32[]{:S(2)}) copy-start(s32[4]{0:T(128)} %pad_add_fusion.meta) | copy-start | bytes 52
  38.5 6.2 %collective-permute-start.4 = (f32[4]{0:T(128)}, f32[4]{0:T(128)S(1)}, u32[]{:S(2)}, u32[]{:S(2)}) collective-permute-start(f32[4]{0:T(128)} %get-tuple-element.38.refs_0_), channel_id=1, source_target_pairs={{0,12},{4,0},{8,4},{12,8},{1,13},{5,1},{9,5},{13,9},{2,14},{6,2},{... | collective-permute-start | bytes 56 | tf_op jit(solution)/shard_map/ppermute | solution.py:1021
  43.2 4.7 %collective-permute-start.3 = (f32[4]{0:T(128)}, f32[4]{0:T(128)S(1)}, u32[]{:S(2)}, u32[]{:S(2)}) collective-permute-start(f32[4]{0:T(128)} %get-tuple-element.38.refs_0_), channel_id=1, source_target_pairs={{0,8},{4,12},{8,0},{12,4},{1,9},{5,13},{9,1},{13,5},{2,10},{6,14},... | collective-permute-start | bytes 56 | tf_op jit(solution)/shard_map/ppermute | solution.py:1021
  43.2 5.5 %collective-permute-start.2 = (f32[4]{0:T(128)}, f32[4]{0:T(128)S(1)}, u32[]{:S(2)}, u32[]{:S(2)}) collective-permute-start(f32[4]{0:T(128)} %get-tuple-element.38.refs_0_), channel_id=1, source_target_pairs={{0,4},{4,8},{8,12},{12,0},{1,5},{5,9},{9,13},{13,1},{2,6},{6,10},{... | collective-permute-start | bytes 56 | tf_op jit(solution)/shard_map/ppermute | solution.py:1021
  48.7 1.0 copy-start.1
  49.8 1.0 copy-start.3
  68.4 3.8 %collective-permute-start.5 = (f32[2,1728,128]{2,1,0:T(8,128)S(1)}, f32[2,1728,128]{2,1,0:T(8,128)S(1)}, u32[]{:S(2)}, u32[]{:S(2)}) collective-permute-start(f32[2,1728,128]{2,1,0:T(8,128)S(1)} %get-tuple-element.35), channel_id=1, source_target_pairs={{0,1},{1,0},{2,3},{3,2},{4,5},{5,4},{6,7},{7,6},{8,9},{9,8},{10,11... | collective-permute-start | bytes 5308424 | tf_op jit(solution)/shard_map/ppermute | solution.py:1054
  72.6 18.3 %collective-permute-start.6 = (bf16[2160,128]{1,0:T(8,128)(2,1)S(1)}, bf16[2160,128]{1,0:T(8,128)(2,1)S(1)}, u32[]{:S(2)}, u32[]{:S(2)}) collective-permute-start(bf16[2160,128]{1,0:T(8,128)(2,1)S(1)} %bitcast.19), channel_id=1, source_target_pairs={{0,2},{1,3},{2,0},{3,1},{4,6},{5,7},{6,4},{7,5},{8,10},{9,11},{10,... | collective-permute-start | bytes 1658888 | tf_op jit(solution)/shard_map/ppermute | solution.py:1058
  90.8 19.0 %copy-start.6 = (f32[288,128]{1,0:T(8,128)S(1)}, f32[288,128]{1,0:T(8,128)}, u32[]{:S(2)}) copy-start(f32[288,128]{1,0:T(8,128)} %constant.35.clone.across) | copy-start | bytes 442372
  90.8 18.9 %copy-start.11 = (bf16[288,144]{1,0:T(8,128)(2,1)S(1)}, bf16[288,144]{1,0:T(8,128)(2,1)}, u32[]{:S(2)}) copy-start(bf16[288,144]{1,0:T(8,128)(2,1)} %constant.40.clone.refs_7_) | copy-start | bytes 248836
  90.8 18.9 %copy-start.12 = (bf16[288,144]{1,0:T(8,128)(2,1)S(1)}, bf16[288,144]{1,0:T(8,128)(2,1)}, u32[]{:S(2)}) copy-start(bf16[288,144]{1,0:T(8,128)(2,1)} %constant.39.clone.refs_6_) | copy-start | bytes 248836
  90.8 18.9 %copy-start.13 = (bf16[288,144]{1,0:T(8,128)(2,1)S(1)}, bf16[288,144]{1,0:T(8,128)(2,1)}, u32[]{:S(2)}) copy-start(bf16[288,144]{1,0:T(8,128)(2,1)} %constant.38.clone.refs_5_) | copy-start | bytes 248836
  90.8 18.9 %copy-start.14 = (bf16[288,144]{1,0:T(8,128)(2,1)S(1)}, bf16[288,144]{1,0:T(8,128)(2,1)}, u32[]{:S(2)}) copy-start(bf16[288,144]{1,0:T(8,128)(2,1)} %constant.37.clone.refs_4_) | copy-start | bytes 248836
  90.8 18.9 %copy-start.16 = (f32[4,128]{1,0:T(4,128)S(1)}, f32[4,128]{1,0:T(4,128)}, u32[]{:S(2)}) copy-start(f32[4,128]{1,0:T(4,128)} %constant.36.clone.deep) | copy-start | bytes 6148
  90.9 3.8 %collective-permute-start.7 = (f32[2,1728,128]{2,1,0:T(8,128)S(1)}, f32[2,1728,128]{2,1,0:T(8,128)S(1)}, u32[]{:S(2)}, u32[]{:S(2)}) collective-permute-start(f32[2,1728,128]{2,1,0:T(8,128)S(1)} %get-tuple-element.44), channel_id=1, source_target_pairs={{0,1},{1,0},{2,3},{3,2},{4,5},{5,4},{6,7},{7,6},{8,9},{9,8},{10,11... | collective-permute-start | bytes 5308424 | tf_op jit(solution)/shard_map/ppermute | solution.py:1054
  94.6 30.4 %copy-start.9 = (bf16[288,288]{1,0:T(8,128)(2,1)S(1)}, bf16[288,288]{1,0:T(8,128)(2,1)}, u32[]{:S(2)}) copy-start(bf16[288,288]{1,0:T(8,128)(2,1)} %constant.42.clone.refs_5_) | copy-start | bytes 497668
  94.6 30.4 %copy-start.10 = (bf16[288,288]{1,0:T(8,128)(2,1)S(1)}, bf16[288,288]{1,0:T(8,128)(2,1)}, u32[]{:S(2)}) copy-start(bf16[288,288]{1,0:T(8,128)(2,1)} %constant.41.clone.refs_4_) | copy-start | bytes 497668
  95.1 14.6 %collective-permute-start.8 = (bf16[2160,128]{1,0:T(8,128)(2,1)S(1)}, bf16[2160,128]{1,0:T(8,128)(2,1)S(1)}, u32[]{:S(2)}, u32[]{:S(2)}) collective-permute-start(bf16[2160,128]{1,0:T(8,128)(2,1)S(1)} %bitcast.20), channel_id=1, source_target_pairs={{0,2},{1,3},{2,0},{3,1},{4,6},{5,7},{6,4},{7,5},{8,10},{9,11},{10,... | collective-permute-start | bytes 1658888 | tf_op jit(solution)/shard_map/ppermute | solution.py:1058
  109.8 37.0 %copy-start.7 = (bf16[512,512]{1,0:T(8,128)(2,1)S(1)}, bf16[512,512]{1,0:T(8,128)(2,1)}, u32[]{:S(2)}) copy-start(bf16[512,512]{1,0:T(8,128)(2,1)} %constant.44.clone.refs_7_) | copy-start | bytes 1572868
  109.8 37.0 %copy-start.8 = (bf16[512,512]{1,0:T(8,128)(2,1)S(1)}, bf16[512,512]{1,0:T(8,128)(2,1)}, u32[]{:S(2)}) copy-start(bf16[512,512]{1,0:T(8,128)(2,1)} %constant.43.clone.refs_6_) | copy-start | bytes 1572868
  114.2 10.8 %collective-permute-start.11 = (f32[288,128]{1,0:T(8,128)S(1)}, f32[288,128]{1,0:T(8,128)S(1)}, u32[]{:S(2)}, u32[]{:S(2)}) collective-permute-start(f32[288,128]{1,0:T(8,128)S(1)} %get-tuple-element.50.refs_0_), channel_id=1, source_target_pairs={{0,12},{4,0},{8,4},{12,8},{1,13},{5,1},{9,5},{13,9},{2,14},{6,2},{... | collective-permute-start | bytes 442376 | tf_op jit(solution)/shard_map/ppermute | solution.py:1076
  114.8 10.2 %collective-permute-start.9 = (f32[288,128]{1,0:T(8,128)S(1)}, f32[288,128]{1,0:T(8,128)S(1)}, u32[]{:S(2)}, u32[]{:S(2)}) collective-permute-start(f32[288,128]{1,0:T(8,128)S(1)} %get-tuple-element.50.refs_0_), channel_id=1, source_target_pairs={{0,4},{4,8},{8,12},{12,0},{1,5},{5,9},{9,13},{13,1},{2,6},{6,10},{... | collective-permute-start | bytes 442376 | tf_op jit(solution)/shard_map/ppermute | solution.py:1076
  116.3 8.7 %collective-permute-start.10 = (bf16[288,128]{1,0:T(8,128)(2,1)S(1)}, bf16[288,128]{1,0:T(8,128)(2,1)S(1)}, u32[]{:S(2)}, u32[]{:S(2)}) collective-permute-start(bf16[288,128]{1,0:T(8,128)(2,1)S(1)} %convert_element_type.3), channel_id=1, source_target_pairs={{0,8},{4,12},{8,0},{12,4},{1,9},{5,13},{9,1},{13,5},{2,10},{6,14},... | collective-permute-start | bytes 221192 | tf_op jit(solution)/shard_map/ppermute | solution.py:1076
  129.8 17.0 %collective-permute-start.12 = (f32[864,128]{1,0:T(8,128)S(1)}, f32[864,128]{1,0:T(8,128)S(1)}, u32[]{:S(2)}, u32[]{:S(2)}) collective-permute-start(f32[864,128]{1,0:T(8,128)S(1)} %get-tuple-element.52), channel_id=1, source_target_pairs={{0,1},{1,0},{2,3},{3,2},{4,5},{5,4},{6,7},{7,6},{8,9},{9,8},{10,11... | collective-permute-start | bytes 1327112 | tf_op jit(solution)/shard_map/ppermute | solution.py:1089
  129.9 10.7 %collective-permute-start.13 = (bf16[1296,128]{1,0:T(8,128)(2,1)S(1)}, bf16[1296,128]{1,0:T(8,128)(2,1)S(1)}, u32[]{:S(2)}, u32[]{:S(2)}) collective-permute-start(bf16[1296,128]{1,0:T(8,128)(2,1)S(1)} %get-tuple-element.53), channel_id=1, source_target_pairs={{0,2},{1,3},{2,0},{3,1},{4,6},{5,7},{6,4},{7,5},{8,10},{9,11},{10,... | collective-permute-start | bytes 995336 | tf_op jit(solution)/shard_map/ppermute | solution.py:1089
  130.5 16.3 %collective-permute-start.14 = (bf16[1296,128]{1,0:T(8,128)(2,1)S(1)}, bf16[1296,128]{1,0:T(8,128)(2,1)S(1)}, u32[]{:S(2)}, u32[]{:S(2)}) collective-permute-start(bf16[1296,128]{1,0:T(8,128)(2,1)S(1)} %get-tuple-element.54), channel_id=1, source_target_pairs={{0,3},{1,2},{2,1},{3,0},{4,7},{5,6},{6,5},{7,4},{8,11},{9,10},{10,... | collective-permute-start | bytes 995336 | tf_op jit(solution)/shard_map/ppermute | solution.py:1089
  (1 other events, 0.6 us)

commit v3 on v2

--- a/solution.py
+++ b/solution.py
@@ -248,13 +248,12 @@
     unrolled(HALO + rows - 1, planes - 1, residual, 0)
 
     def plant(o, carry):
-        column = columns[o]
-        row = lax.div(column, ny)
-        y = column - row * ny
-        p = row - first_row + HALO
-
-        @pl.when((p >= 1) & (p < planes - 1))
+        column = columns[o] - (first_row - HALO) * ny
+
+        @pl.when((column >= ny) & (column < (planes - 1) * ny))
         def _():
+            p = lax.div(column, ny)
+            y = column - p * ny
             at = pl.ds(p * plane + PAD + y, 1)
             flat = pl.ds(p * ny + y, 1)
             added = residuals[pl.ds(o, 1)]
@@ -357,9 +356,9 @@
     low = edge if first > 0 else 0
     high = edge if first + size < ny else 0
     held = PAD + size + (PAD if high else 0)
-    early = min(4, length)
+    cuts = misfit_cuts(length, parts)
     sem = iter(range(sems.shape[0]))
-    waits = ([], [])
+    waits = [[] for _ in cuts[1:]]
 
     def bring(source, target, group):
         copy = pltpu.make_async_copy(source, target, sems.at[next(sem)])
@@ -386,13 +385,16 @@
             if hi > lo:
                 bring(source.at[pl.ds(lo - 1, hi - lo), ys], ref.at[pl.ds(lo, hi - lo), yt], group)
 
-    for part in range(parts):
-        bring_rows(0, part * length, part * length + early)
-    for part in range(parts):
-        end = rows + 2 if part == parts - 1 else (part + 1) * length
-        if end > part * length + early:
-            bring_rows(1, part * length + early, end)
-    block = block_rows(size)
+    def bring_group(group):
+        for part in range(parts):
+            end = cuts[group + 1]
+            if part == parts - 1 and end == length:
+                end = length + 2
+            bring_rows(group, part * length + cuts[group], part * length + end)
+
+    for group in range(min(2, len(waits))):
+        bring_group(group)
+    block = size if size % 16 == 0 else block_rows(size)
     blocks = range(0, size, block)
     first_row, well = meta[0], meta[1]
     c0, c1 = step_lengths(sums)
@@ -497,24 +499,30 @@
         step(x)
         return carry
 
-    for copy in waits[0]:
-        copy.wait()
-    for part in range(parts):
-        prepare(part, 0)
-        prepare(part, 1)
-        along(part)
-    if parts == 1 or length <= early:
-        for copy in waits[1]:
+    done = 0
+    for group in range(len(waits)):
+        for copy in waits[group]:
             copy.wait()
-        step(0)
-        lax.fori_loop(1, length, loop, 0)
-    else:
-        step(0)
-        lax.fori_loop(1, early - 2, loop, 0)
-        for copy in waits[1]:
-            copy.wait()
-        lax.fori_loop(early - 2, length, loop, 0)
+        if group + 2 < len(waits):
+            bring_group(group + 2)
+        if group == 0:
+            for part in range(parts):
+                prepare(part, 0)
+                prepare(part, 1)
+                along(part)
+            step(0)
+            done = 1
+        ready = length if group == len(waits) - 1 else cuts[group + 1] - 2
+        if ready > done:
+            lax.fori_loop(done, ready, loop, 0)
+            done = ready
     transform(length - 1, (length - 1) % 2)
+
+
+def misfit_cuts(length, parts):
+    if parts == 1 or length <= 4:
+        return [0, length]
+    return list(range(0, length - 2, 3)) + [length]
 
 
 def misfit(meta, sums, fields, w, h, ends, tables, first, size, parts, tests):
@@ -536,7 +544,7 @@
             pltpu.VMEM((parts, size, depth), F32),
             pltpu.VMEM((2, size, parts * depth), BF16),
             pltpu.VMEM((2, size, parts * depth), BF16),
-            pltpu.SemaphoreType.DMA((10 * parts + 4,)),
+            pltpu.SemaphoreType.DMA((5 * parts * (len(misfit_cuts(length, parts)) - 1) + 4,)),
         ],
         compiler_params=pltpu.CompilerParams(vmem_limit_bytes=MISFIT_LIMIT),
         cost_estimate=pl.CostEstimate(flops=8000 * cells, bytes_accessed=4 * cells, transcendentals=cells),

time: 151 us -> 146 us (0.967)
  Pallas kernels: 73.8 us -> 68.9 us
    pallas_call x2, Pallas kernels: 33.6 us -> 28.8 us  [misfit(): pl.pallas_call(functools.partial(misfit_kernel, rows, ny, first, size, pa...]
  transfers between devices with their start and end apart: 15 -> 15, of which waited for: 9 -> 9; matrix products, arithmetic and copies ran while one was open for 0% -> 0% of each run, Pallas kernels for 20% -> 19%
where the time goes in v3:
time: 146 us; the launch traced here: 145 us
  Pallas kernels  68.9 us (47%)
  waiting for transfers between devices  48.5 us (33%)
  starting transfers between devices  19.4 us (13%)
  local copies, waits for them, and re-layouts  6.8 us (5%)
    pallas_call x2, Pallas kernels, misfit(): pl.pallas_call(functools.partial(misfit_kernel, rows, ny, first, size, pa...  28.8 us
    ppermute x3, waiting for transfers between devices, on_device(): arrived.append(lax.ppermute(pieces[k], 'test', turn))  15 us
    ppermute x2, waiting for transfers between devices, on_device(): fars += [lax.ppermute(far[k], 'test', hop) for k, hop in enumerate(hops)]  14 us
    pallas_call x1, Pallas kernels, moments(): pl.pallas_call(functools.partial(moments_kernel, rows, ny, count_x), out_...  13.7 us
    pallas_call x1, Pallas kernels, interior(): pl.pallas_call(functools.partial(interior_kernel, rows, ny, pieces), out_...  12.8 us
    ppermute x3, waiting for transfers between devices, on_device(): lax.ppermute(packed if near else packed.astype(BF16), 'space', turn)  7.54 us
    ppermute x2, waiting for transfers between devices, on_device(): other = lax.ppermute(other, 'test', other_core)  7.36 us
    ppermute x3, starting transfers between devices, on_device(): sums = [sums] + [lax.ppermute(sums, 'space', turn) for turn in turns]  5.65 us
  transfers between devices with their start and end apart: 15, of which 9 were waited for; matrix products, arithmetic and copies ran while one was open for 0% of the time, Pallas kernels for 19%

profile of v3, /device:TPU:0, one launch (start us, length us, event | category | flops | bytes accessed | tf_op | source)
XLA Modules:
  0.0 145.3 jit_solution(13562104114587080310)
XLA Ops:
  0.0 0.9 slice_bitcast_fusion.2
  0.9 1.1 fusion
  2.0 1.1 slice_bitcast_fusion
  3.2 5.0 %collective-permute-start = (bf16[7,288,128]{2,1,0:T(8,128)(2,1)S(1)}, bf16[7,288,128]{2,1,0:T(8,128)(2,1)S(1)}, u32[]{:S(2)}, u32[]{:S(2)}) collective-permute-start(bf16[7,288,128]{2,1,0:T(8,128)(2,1)S(1)} %pad_maximum_fusion), channel_id=1, source_target_pairs={{0,4},{4,8},{8,12},{1,5},{5,9},{9,13},{2,6},{6,10},{10,14},{3,7},{... | collective-permute-start | bytes 1548296 | tf_op jit(solution)/shard_map/ppermute | solution.py:1011
  8.2 1.3 collective-permute-start.1
  10.7 12.8 %interior.1 = (f32[47976,128]{1,0:T(8,128)S(1)}, f32[31104,128]{1,0:T(8,128)S(1)}) custom-call(s32[4]{0:T(128)} %pad_add_fusion.meta, bf16[48,288,128]{2,1,0:T(8,128)(2,1)} %lk_in.1, bf16[48,288,128]{2,1,0:T(8,128)(2,1)} %bitcast.23), custom_call_target="tpu_custom_call" | custom-call | flops 8847360000 | bytes 7077888 | tf_op jit(solution)/shard_map/interior/pallas_call | solution.py:194
  23.6 0.8 copy-done
  24.6 13.7 %moments.1 = (f32[47976,128]{1,0:T(8,128)S(1)}, f32[31104,128]{1,0:T(8,128)S(1)}, f32[3,15984,128]{2,1,0:T(8,128)}, f32[4]{0:T(128)}) custom-call(s32[4]{0:T(128)} %pad_add_fusion.meta, s32[64]{0:T(128)} %bitcast.29, f32[64,128]{1,0:T(8,128)} %bitcast.28, bf16[7,288,128]{2,1,0:T(8,128)(2,1)} %copy-done, ...), custom_call_target="tpu_custom_call", output_to_operand_aliasing={{0}: (5, {}), {1}: (6, {})} | custom-call | flops 8847360000 | bytes 7077888 | tf_op jit(solution)/shard_map/moments/pallas_call | solution.py:320
  38.3 4.7 %collective-permute-start.4 = (f32[4]{0:T(128)}, f32[4]{0:T(128)S(1)}, u32[]{:S(2)}, u32[]{:S(2)}) collective-permute-start(f32[4]{0:T(128)} %get-tuple-element.38.refs_0_), channel_id=1, source_target_pairs={{0,12},{4,0},{8,4},{12,8},{1,13},{5,1},{9,5},{13,9},{2,14},{6,2},{... | collective-permute-start | bytes 56 | tf_op jit(solution)/shard_map/ppermute | solution.py:1029
  43.0 1.0 collective-permute-start.2
  44.5 3.1 %collective-permute-done.3.refs_2_ = f32[4]{0:T(128)S(1)} collective-permute-done((f32[4]{0:T(128)}, f32[4]{0:T(128)S(1)}, u32[]{:S(2)}, u32[]{:S(2)}) %collective-permute-start.3) | collective-permute-done | bytes 48 | tf_op jit(solution)/shard_map/ppermute | solution.py:1029
  47.6 0.9 collective-permute-done.2.refs_1_
  48.5 1.0 copy-done.1
  49.6 1.0 copy-done.3
  51.2 14.6 %misfit.2 = (f32[2,1728,128]{2,1,0:T(8,128)S(1)}, f32[2,1728,128]{2,1,0:T(8,128)S(1)}) custom-call(s32[4]{0:T(128)S(1)} %copy-done.15, f32[4]{0:T(128)S(1)} %copy-done.17, f32[4]{0:T(128)S(1)} %collective-permute-done.2.refs_1_, f32[4]{0:T(128)S(1)} %collective-permute-done.3.refs_2_, f32[4]{0:T(128)S(1)} %collective-permute-done.4.refs_3_, ...), custom_call_target="tpu_custom_call" | custom-call | flops 7077888000 | bytes 3538944 | tf_op jit(solution)/shard_map/misfit/pallas_call | solution.py:537
  65.8 3.7 %collective-permute-done.5.other = f32[2,1728,128]{2,1,0:T(8,128)S(1)} collective-permute-done((f32[2,1728,128]{2,1,0:T(8,128)S(1)}, f32[2,1728,128]{2,1,0:T(8,128)S(1)}, u32[]{:S(2)}, u32[]{:S(2)}) %collective-permute-start.5) | collective-permute-done | bytes 1769504 | tf_op jit(solution)/shard_map/ppermute | solution.py:1062
  70.0 1.5 %collective-permute-start.6 = (bf16[2160,128]{1,0:T(8,128)(2,1)S(1)}, bf16[2160,128]{1,0:T(8,128)(2,1)S(1)}, u32[]{:S(2)}, u32[]{:S(2)}) collective-permute-start(bf16[2160,128]{1,0:T(8,128)(2,1)S(1)} %bitcast.19), channel_id=1, source_target_pairs={{0,2},{1,3},{2,0},{3,1},{4,6},{5,7},{6,4},{7,5},{8,10},{9,11},{10,... | collective-permute-start | bytes 1658888 | tf_op jit(solution)/shard_map/ppermute | solution.py:1066
  71.5 14.3 %misfit.3 = (f32[2,1728,128]{2,1,0:T(8,128)S(1)}, f32[2,1728,128]{2,1,0:T(8,128)S(1)}) custom-call(s32[4]{0:T(128)S(1)} %copy-done.15, f32[4]{0:T(128)S(1)} %copy-done.17, f32[4]{0:T(128)S(1)} %collective-permute-done.2.refs_1_, f32[4]{0:T(128)S(1)} %collective-permute-done.3.refs_2_, f32[4]{0:T(128)S(1)} %collective-permute-done.4.refs_3_, ...), custom_call_target="tpu_custom_call" | custom-call | flops 7077888000 | bytes 3538944 | tf_op jit(solution)/shard_map/misfit/pallas_call | solution.py:537
  86.0 3.7 %collective-permute-done.7.other = f32[2,1728,128]{2,1,0:T(8,128)S(1)} collective-permute-done((f32[2,1728,128]{2,1,0:T(8,128)S(1)}, f32[2,1728,128]{2,1,0:T(8,128)S(1)}, u32[]{:S(2)}, u32[]{:S(2)}) %collective-permute-start.7) | collective-permute-done | bytes 1769504 | tf_op jit(solution)/shard_map/ppermute | solution.py:1062
  90.1 0.6 collective-permute-start.8
  90.7 14.0 %collective-permute-done.8.refs_3_ = bf16[2160,128]{1,0:T(8,128)(2,1)S(1)} collective-permute-done((bf16[2160,128]{1,0:T(8,128)(2,1)S(1)}, bf16[2160,128]{1,0:T(8,128)(2,1)S(1)}, u32[]{:S(2)}, u32[]{:S(2)}) %collective-permute-start.8) | collective-permute-done | bytes 552992 | tf_op jit(solution)/shard_map/ppermute | solution.py:1066
  104.8 4.4 %solve.1 = (f32[12,288,128]{2,1,0:T(8,128)S(1)}, f32[4,288,128]{2,1,0:T(8,128)S(1)}, f32[288,128]{1,0:T(8,128)S(1)}) custom-call(s32[4]{0:T(128)S(1)} %copy-done.15, f32[288,128]{1,0:T(8,128)S(1)} %copy-done.6, f32[4,128]{1,0:T(4,128)S(1)} %copy-done.16, f32[1728,128]{1,0:T(8,128)S(1)} %get-tuple-element.36.refs_0_, ...), custom_call_target="tpu_custom_call" | custom-call | flops 764411904 | bytes 7077888 | tf_op jit(solution)/shard_map/solve/pallas_call | solution.py:751
  109.2 0.7 collective-permute-start.11
  109.9 1.4 collective-permute-start.9
  111.3 1.2 collective-permute-start.10
  112.5 7.5 %collective-permute-done.10.refs_2_ = bf16[288,128]{1,0:T(8,128)(2,1)S(1)} collective-permute-done((bf16[288,128]{1,0:T(8,128)(2,1)S(1)}, bf16[288,128]{1,0:T(8,128)(2,1)S(1)}, u32[]{:S(2)}, u32[]{:S(2)}) %collective-permute-start.10) | collective-permute-done | bytes 73760 | tf_op jit(solution)/shard_map/ppermute | solution.py:1084
  120.0 4.8 %finish.1 = (f32[864,128]{1,0:T(8,128)S(1)}, f32[864,128]{1,0:T(8,128)S(1)}, bf16[1296,128]{1,0:T(8,128)(2,1)S(1)}, bf16[1296,128]{1,0:T(8,128)(2,1)S(1)}) custom-call(s32[4]{0:T(128)S(1)} %copy-done.15, f32[288,128]{1,0:T(8,128)S(1)} %copy-done.6, f32[4,128]{1,0:T(4,128)S(1)} %copy-done.16, f32[12,288,128]{2,1,0:T(8,128)S(1)} %get-tuple-element.48.local, ...), custom_call_target="tpu_custom_call" | custom-call | flops 764411904 | bytes 7077888 | tf_op jit(solution)/shard_map/finish/pallas_call | solution.py:896
  124.9 0.6 collective-permute-start.13
  125.5 1.3 collective-permute-start.14
  126.8 8.8 %collective-permute-done.13.refs_2_.refs_3_ = bf16[1296,128]{1,0:T(8,128)(2,1)S(1)} collective-permute-done((bf16[1296,128]{1,0:T(8,128)(2,1)S(1)}, bf16[1296,128]{1,0:T(8,128)(2,1)S(1)}, u32[]{:S(2)}, u32[]{:S(2)}) %collective-permute-start.13) | collective-permute-done | bytes 331808 | tf_op jit(solution)/shard_map/ppermute | solution.py:1097
  135.6 6.2 %collective-permute-done.14.refs_4_.refs_5_ = bf16[1296,128]{1,0:T(8,128)(2,1)S(1)} collective-permute-done((bf16[1296,128]{1,0:T(8,128)(2,1)S(1)}, bf16[1296,128]{1,0:T(8,128)(2,1)S(1)}, u32[]{:S(2)}, u32[]{:S(2)}) %collective-permute-start.14) | collective-permute-done | bytes 331808 | tf_op jit(solution)/shard_map/ppermute | solution.py:1097
  141.8 3.5 %depth_cells.1 = f32[4,864,128]{2,1,0:T(8,128)} custom-call(s32[4]{0:T(128)S(1)} %copy-done.15, f32[864,128]{1,0:T(8,128)S(1)} %get-tuple-element.51.refs_0_, f32[864,128]{1,0:T(8,128)S(1)} %collective-permute-done.12.refs_1_, bf16[1296,128]{1,0:T(8,128)(2,1)S(1)} %collective-permute-done.13.refs_2_.refs_3_, ...), custom_call_target="tpu_custom_call" | custom-call | flops 1358954496 | bytes 3538944 | tf_op jit(solution)/shard_map/depth_cells/pallas_call | solution.py:982
  (50 shorter events, 3.3 us)
Async XLA Ops:
  3.2 20.4 %collective-permute-start = (bf16[7,288,128]{2,1,0:T(8,128)(2,1)S(1)}, bf16[7,288,128]{2,1,0:T(8,128)(2,1)S(1)}, u32[]{:S(2)}, u32[]{:S(2)}) collective-permute-start(bf16[7,288,128]{2,1,0:T(8,128)(2,1)S(1)} %pad_maximum_fusion), channel_id=1, source_target_pairs={{0,4},{4,8},{8,12},{1,5},{5,9},{9,13},{2,6},{6,10},{10,14},{3,7},{... | collective-permute-start | bytes 1548296 | tf_op jit(solution)/shard_map/ppermute | solution.py:1011
  8.2 15.4 %collective-permute-start.1 = (bf16[7,288,128]{2,1,0:T(8,128)(2,1)S(1)}, bf16[7,288,128]{2,1,0:T(8,128)(2,1)S(1)}, u32[]{:S(2)}, u32[]{:S(2)}) collective-permute-start(bf16[7,288,128]{2,1,0:T(8,128)(2,1)S(1)} %pad_maximum_fusion.1), channel_id=1, source_target_pairs={{4,0},{8,4},{12,8},{5,1},{9,5},{13,9},{6,2},{10,6},{14,10},{7,3},{... | collective-permute-start | bytes 1548296 | tf_op jit(solution)/shard_map/ppermute | solution.py:1015
  23.6 0.8 copy-start
  23.6 1.0 copy-start.2
  24.6 23.9 %copy-start.4 = (bf16[512,512]{1,0:T(8,128)(2,1)S(1)}, bf16[512,512]{1,0:T(8,128)(2,1)}, u32[]{:S(2)}) copy-start(bf16[512,512]{1,0:T(8,128)(2,1)} %constant.34.clone.refs_10_) | copy-start | bytes 1572868
  24.6 23.9 %copy-start.5 = (bf16[512,512]{1,0:T(8,128)(2,1)S(1)}, bf16[512,512]{1,0:T(8,128)(2,1)}, u32[]{:S(2)}) copy-start(bf16[512,512]{1,0:T(8,128)(2,1)} %constant.33.clone.refs_9_) | copy-start | bytes 1572868
  24.6 23.9 %copy-start.15 = (s32[4]{0:T(128)S(1)}, s32[4]{0:T(128)}, u32[]{:S(2)}) copy-start(s32[4]{0:T(128)} %pad_add_fusion.meta) | copy-start | bytes 52
  38.3 6.2 %collective-permute-start.4 = (f32[4]{0:T(128)}, f32[4]{0:T(128)S(1)}, u32[]{:S(2)}, u32[]{:S(2)}) collective-permute-start(f32[4]{0:T(128)} %get-tuple-element.38.refs_0_), channel_id=1, source_target_pairs={{0,12},{4,0},{8,4},{12,8},{1,13},{5,1},{9,5},{13,9},{2,14},{6,2},{... | collective-permute-start | bytes 56 | tf_op jit(solution)/shard_map/ppermute | solution.py:1029
  43.0 4.7 %collective-permute-start.3 = (f32[4]{0:T(128)}, f32[4]{0:T(128)S(1)}, u32[]{:S(2)}, u32[]{:S(2)}) collective-permute-start(f32[4]{0:T(128)} %get-tuple-element.38.refs_0_), channel_id=1, source_target_pairs={{0,8},{4,12},{8,0},{12,4},{1,9},{5,13},{9,1},{13,5},{2,10},{6,14},... | collective-permute-start | bytes 56 | tf_op jit(solution)/shard_map/ppermute | solution.py:1029
  43.0 5.5 %collective-permute-start.2 = (f32[4]{0:T(128)}, f32[4]{0:T(128)S(1)}, u32[]{:S(2)}, u32[]{:S(2)}) collective-permute-start(f32[4]{0:T(128)} %get-tuple-element.38.refs_0_), channel_id=1, source_target_pairs={{0,4},{4,8},{8,12},{12,0},{1,5},{5,9},{9,13},{13,1},{2,6},{6,10},{... | collective-permute-start | bytes 56 | tf_op jit(solution)/shard_map/ppermute | solution.py:1029
  48.5 1.0 copy-start.1
  49.6 1.0 copy-start.3
  65.8 3.8 %collective-permute-start.5 = (f32[2,1728,128]{2,1,0:T(8,128)S(1)}, f32[2,1728,128]{2,1,0:T(8,128)S(1)}, u32[]{:S(2)}, u32[]{:S(2)}) collective-permute-start(f32[2,1728,128]{2,1,0:T(8,128)S(1)} %get-tuple-element.35), channel_id=1, source_target_pairs={{0,1},{1,0},{2,3},{3,2},{4,5},{5,4},{6,7},{7,6},{8,9},{9,8},{10,11... | collective-permute-start | bytes 5308424 | tf_op jit(solution)/shard_map/ppermute | solution.py:1062
  70.0 15.9 %collective-permute-start.6 = (bf16[2160,128]{1,0:T(8,128)(2,1)S(1)}, bf16[2160,128]{1,0:T(8,128)(2,1)S(1)}, u32[]{:S(2)}, u32[]{:S(2)}) collective-permute-start(bf16[2160,128]{1,0:T(8,128)(2,1)S(1)} %bitcast.19), channel_id=1, source_target_pairs={{0,2},{1,3},{2,0},{3,1},{4,6},{5,7},{6,4},{7,5},{8,10},{9,11},{10,... | collective-permute-start | bytes 1658888 | tf_op jit(solution)/shard_map/ppermute | solution.py:1066
  85.8 19.0 %copy-start.6 = (f32[288,128]{1,0:T(8,128)S(1)}, f32[288,128]{1,0:T(8,128)}, u32[]{:S(2)}) copy-start(f32[288,128]{1,0:T(8,128)} %constant.35.clone.across) | copy-start | bytes 442372
  85.8 18.9 %copy-start.11 = (bf16[288,144]{1,0:T(8,128)(2,1)S(1)}, bf16[288,144]{1,0:T(8,128)(2,1)}, u32[]{:S(2)}) copy-start(bf16[288,144]{1,0:T(8,128)(2,1)} %constant.40.clone.refs_7_) | copy-start | bytes 248836
  85.8 18.9 %copy-start.12 = (bf16[288,144]{1,0:T(8,128)(2,1)S(1)}, bf16[288,144]{1,0:T(8,128)(2,1)}, u32[]{:S(2)}) copy-start(bf16[288,144]{1,0:T(8,128)(2,1)} %constant.39.clone.refs_6_) | copy-start | bytes 248836
  85.8 18.9 %copy-start.13 = (bf16[288,144]{1,0:T(8,128)(2,1)S(1)}, bf16[288,144]{1,0:T(8,128)(2,1)}, u32[]{:S(2)}) copy-start(bf16[288,144]{1,0:T(8,128)(2,1)} %constant.38.clone.refs_5_) | copy-start | bytes 248836
  85.9 18.9 %copy-start.14 = (bf16[288,144]{1,0:T(8,128)(2,1)S(1)}, bf16[288,144]{1,0:T(8,128)(2,1)}, u32[]{:S(2)}) copy-start(bf16[288,144]{1,0:T(8,128)(2,1)} %constant.37.clone.refs_4_) | copy-start | bytes 248836
  85.9 18.9 %copy-start.16 = (f32[4,128]{1,0:T(4,128)S(1)}, f32[4,128]{1,0:T(4,128)}, u32[]{:S(2)}) copy-start(f32[4,128]{1,0:T(4,128)} %constant.36.clone.deep) | copy-start | bytes 6148
  85.9 3.8 %collective-permute-start.7 = (f32[2,1728,128]{2,1,0:T(8,128)S(1)}, f32[2,1728,128]{2,1,0:T(8,128)S(1)}, u32[]{:S(2)}, u32[]{:S(2)}) collective-permute-start(f32[2,1728,128]{2,1,0:T(8,128)S(1)} %get-tuple-element.44), channel_id=1, source_target_pairs={{0,1},{1,0},{2,3},{3,2},{4,5},{5,4},{6,7},{7,6},{8,9},{9,8},{10,11... | collective-permute-start | bytes 5308424 | tf_op jit(solution)/shard_map/ppermute | solution.py:1062
  89.7 30.4 %copy-start.9 = (bf16[288,288]{1,0:T(8,128)(2,1)S(1)}, bf16[288,288]{1,0:T(8,128)(2,1)}, u32[]{:S(2)}) copy-start(bf16[288,288]{1,0:T(8,128)(2,1)} %constant.42.clone.refs_5_) | copy-start | bytes 497668
  89.7 30.4 %copy-start.10 = (bf16[288,288]{1,0:T(8,128)(2,1)S(1)}, bf16[288,288]{1,0:T(8,128)(2,1)}, u32[]{:S(2)}) copy-start(bf16[288,288]{1,0:T(8,128)(2,1)} %constant.41.clone.refs_4_) | copy-start | bytes 497668
  90.1 14.6 %collective-permute-start.8 = (bf16[2160,128]{1,0:T(8,128)(2,1)S(1)}, bf16[2160,128]{1,0:T(8,128)(2,1)S(1)}, u32[]{:S(2)}, u32[]{:S(2)}) collective-permute-start(bf16[2160,128]{1,0:T(8,128)(2,1)S(1)} %bitcast.20), channel_id=1, source_target_pairs={{0,2},{1,3},{2,0},{3,1},{4,6},{5,7},{6,4},{7,5},{8,10},{9,11},{10,... | collective-permute-start | bytes 1658888 | tf_op jit(solution)/shard_map/ppermute | solution.py:1066
  104.8 37.0 %copy-start.7 = (bf16[512,512]{1,0:T(8,128)(2,1)S(1)}, bf16[512,512]{1,0:T(8,128)(2,1)}, u32[]{:S(2)}) copy-start(bf16[512,512]{1,0:T(8,128)(2,1)} %constant.44.clone.refs_7_) | copy-start | bytes 1572868
  104.8 37.0 %copy-start.8 = (bf16[512,512]{1,0:T(8,128)(2,1)S(1)}, bf16[512,512]{1,0:T(8,128)(2,1)}, u32[]{:S(2)}) copy-start(bf16[512,512]{1,0:T(8,128)(2,1)} %constant.43.clone.refs_6_) | copy-start | bytes 1572868
  109.2 10.8 %collective-permute-start.11 = (f32[288,128]{1,0:T(8,128)S(1)}, f32[288,128]{1,0:T(8,128)S(1)}, u32[]{:S(2)}, u32[]{:S(2)}) collective-permute-start(f32[288,128]{1,0:T(8,128)S(1)} %get-tuple-element.50.refs_0_), channel_id=1, source_target_pairs={{0,12},{4,0},{8,4},{12,8},{1,13},{5,1},{9,5},{13,9},{2,14},{6,2},{... | collective-permute-start | bytes 442376 | tf_op jit(solution)/shard_map/ppermute | solution.py:1084
  109.9 10.2 %collective-permute-start.9 = (f32[288,128]{1,0:T(8,128)S(1)}, f32[288,128]{1,0:T(8,128)S(1)}, u32[]{:S(2)}, u32[]{:S(2)}) collective-permute-start(f32[288,128]{1,0:T(8,128)S(1)} %get-tuple-element.50.refs_0_), channel_id=1, source_target_pairs={{0,4},{4,8},{8,12},{12,0},{1,5},{5,9},{9,13},{13,1},{2,6},{6,10},{... | collective-permute-start | bytes 442376 | tf_op jit(solution)/shard_map/ppermute | solution.py:1084
  111.3 8.7 %collective-permute-start.10 = (bf16[288,128]{1,0:T(8,128)(2,1)S(1)}, bf16[288,128]{1,0:T(8,128)(2,1)S(1)}, u32[]{:S(2)}, u32[]{:S(2)}) collective-permute-start(bf16[288,128]{1,0:T(8,128)(2,1)S(1)} %convert_element_type.3), channel_id=1, source_target_pairs={{0,8},{4,12},{8,0},{12,4},{1,9},{5,13},{9,1},{13,5},{2,10},{6,14},... | collective-permute-start | bytes 221192 | tf_op jit(solution)/shard_map/ppermute | solution.py:1084
  124.8 17.0 %collective-permute-start.12 = (f32[864,128]{1,0:T(8,128)S(1)}, f32[864,128]{1,0:T(8,128)S(1)}, u32[]{:S(2)}, u32[]{:S(2)}) collective-permute-start(f32[864,128]{1,0:T(8,128)S(1)} %get-tuple-element.52), channel_id=1, source_target_pairs={{0,1},{1,0},{2,3},{3,2},{4,5},{5,4},{6,7},{7,6},{8,9},{9,8},{10,11... | collective-permute-start | bytes 1327112 | tf_op jit(solution)/shard_map/ppermute | solution.py:1097
  124.9 10.7 %collective-permute-start.13 = (bf16[1296,128]{1,0:T(8,128)(2,1)S(1)}, bf16[1296,128]{1,0:T(8,128)(2,1)S(1)}, u32[]{:S(2)}, u32[]{:S(2)}) collective-permute-start(bf16[1296,128]{1,0:T(8,128)(2,1)S(1)} %get-tuple-element.53), channel_id=1, source_target_pairs={{0,2},{1,3},{2,0},{3,1},{4,6},{5,7},{6,4},{7,5},{8,10},{9,11},{10,... | collective-permute-start | bytes 995336 | tf_op jit(solution)/shard_map/ppermute | solution.py:1097
  125.5 16.3 %collective-permute-start.14 = (bf16[1296,128]{1,0:T(8,128)(2,1)S(1)}, bf16[1296,128]{1,0:T(8,128)(2,1)S(1)}, u32[]{:S(2)}, u32[]{:S(2)}) collective-permute-start(bf16[1296,128]{1,0:T(8,128)(2,1)S(1)} %get-tuple-element.54), channel_id=1, source_target_pairs={{0,3},{1,2},{2,1},{3,0},{4,7},{5,6},{6,5},{7,4},{8,11},{9,10},{10,... | collective-permute-start | bytes 995336 | tf_op jit(solution)/shard_map/ppermute | solution.py:1097
  (1 other events, 0.6 us)

commit v4 on v3

--- a/solution.py
+++ b/solution.py
@@ -549,7 +549,7 @@
         compiler_params=pltpu.CompilerParams(vmem_limit_bytes=MISFIT_LIMIT),
         cost_estimate=pl.CostEstimate(flops=8000 * cells, bytes_accessed=4 * cells, transcendentals=cells),
         name="misfit",
-    )(meta, *sums, in_hbm(fields), in_hbm(w), in_hbm(h), *ends, *tables)
+    )(meta, *sums, in_hbm(fields), in_hbm(w), in_hbm(h), *(in_hbm(end) for end in ends), *tables)
 
 
 def pack_rest(rests, width, kept):

time: 146 us -> 143 us (0.979)
  local copies, waits for them, and re-layouts: 6.8 us -> 4.74 us
    unnamed x36 -> x32, local copies, waits for them, and re-layouts: 3.72 us -> 1.67 us
where the time goes in v4:
time: 143 us
  Pallas kernels  68.7 us (48%)
  waiting for transfers between devices  48.6 us (34%)
  starting transfers between devices  19.4 us (14%)
  local copies, waits for them, and re-layouts  4.74 us (3%)
    pallas_call x2, Pallas kernels, misfit(): pl.pallas_call(functools.partial(misfit_kernel, rows, ny, first, size, pa...  28.6 us
    ppermute x3, waiting for transfers between devices, on_device(): arrived.append(lax.ppermute(pieces[k], 'test', turn))  15 us
    ppermute x2, waiting for transfers between devices, on_device(): fars += [lax.ppermute(far[k], 'test', hop) for k, hop in enumerate(hops)]  14.1 us
    pallas_call x1, Pallas kernels, moments(): pl.pallas_call(functools.partial(moments_kernel, rows, ny, count_x), out_...  13.6 us
    pallas_call x1, Pallas kernels, interior(): pl.pallas_call(functools.partial(interior_kernel, rows, ny, pieces), out_...  12.8 us
    ppermute x3, waiting for transfers between devices, on_device(): lax.ppermute(packed if near else packed.astype(BF16), 'space', turn)  7.54 us
    ppermute x2, waiting for transfers between devices, on_device(): other = lax.ppermute(other, 'test', other_core)  7.36 us
    ppermute x3, starting transfers between devices, on_device(): sums = [sums] + [lax.ppermute(sums, 'space', turn) for turn in turns]  5.7 us
  transfers between devices with their start and end apart: 15, of which 9 were waited for; matrix products, arithmetic and copies ran while one was open for 0% of the time, Pallas kernels for 19%

profile of v4, /device:TPU:0, one launch (start us, length us, event | category | flops | bytes accessed | tf_op | source)
XLA Modules:
  0.0 143.1 jit_solution(2246736378652864832)
XLA Ops:
  0.0 0.9 slice_bitcast_fusion.2
  0.9 1.1 fusion
  2.0 1.1 slice_bitcast_fusion
  3.2 5.0 %collective-permute-start = (bf16[7,288,128]{2,1,0:T(8,128)(2,1)S(1)}, bf16[7,288,128]{2,1,0:T(8,128)(2,1)S(1)}, u32[]{:S(2)}, u32[]{:S(2)}) collective-permute-start(bf16[7,288,128]{2,1,0:T(8,128)(2,1)S(1)} %pad_maximum_fusion), channel_id=1, source_target_pairs={{0,4},{4,8},{8,12},{1,5},{5,9},{9,13},{2,6},{6,10},{10,14},{3,7},{... | collective-permute-start | bytes 1548296 | tf_op jit(solution)/shard_map/ppermute | solution.py:1011
  8.2 1.3 collective-permute-start.1
  10.2 0.6 pad_add_fusion.meta
  10.8 12.8 %interior.1 = (f32[47976,128]{1,0:T(8,128)S(1)}, f32[31104,128]{1,0:T(8,128)S(1)}) custom-call(s32[4]{0:T(128)} %pad_add_fusion.meta, bf16[48,288,128]{2,1,0:T(8,128)(2,1)} %lk_in.1, bf16[48,288,128]{2,1,0:T(8,128)(2,1)} %bitcast.23), custom_call_target="tpu_custom_call" | custom-call | flops 8847360000 | bytes 7077888 | tf_op jit(solution)/shard_map/interior/pallas_call | solution.py:194
  23.6 0.8 copy-done.14
  24.6 13.6 %moments.1 = (f32[47976,128]{1,0:T(8,128)S(1)}, f32[31104,128]{1,0:T(8,128)S(1)}, f32[3,15984,128]{2,1,0:T(8,128)}, f32[4]{0:T(128)}) custom-call(s32[4]{0:T(128)} %pad_add_fusion.meta, s32[64]{0:T(128)} %bitcast.29, f32[64,128]{1,0:T(8,128)} %bitcast.28, bf16[7,288,128]{2,1,0:T(8,128)(2,1)} %copy-done.14, ...), custom_call_target="tpu_custom_call", output_to_operand_aliasing={{0}: (5, {}), {1}: (6, {})} | custom-call | flops 8847360000 | bytes 7077888 | tf_op jit(solution)/shard_map/moments/pallas_call | solution.py:320
  38.3 4.7 %collective-permute-start.4 = (f32[4]{0:T(128)}, f32[4]{0:T(128)S(1)}, u32[]{:S(2)}, u32[]{:S(2)}) collective-permute-start(f32[4]{0:T(128)} %get-tuple-element.38.refs_0_), channel_id=1, source_target_pairs={{0,12},{4,0},{8,4},{12,8},{1,13},{5,1},{9,5},{13,9},{2,14},{6,2},{... | collective-permute-start | bytes 56 | tf_op jit(solution)/shard_map/ppermute | solution.py:1029
  43.0 1.0 collective-permute-start.2
  44.5 3.1 %collective-permute-done.3.refs_2_ = f32[4]{0:T(128)S(1)} collective-permute-done((f32[4]{0:T(128)}, f32[4]{0:T(128)S(1)}, u32[]{:S(2)}, u32[]{:S(2)}) %collective-permute-start.3) | collective-permute-done | bytes 48 | tf_op jit(solution)/shard_map/ppermute | solution.py:1029
  47.6 0.9 collective-permute-done.2.refs_1_
  48.5 0.6 copy-done.13
  49.1 14.4 %misfit.2 = (f32[2,1728,128]{2,1,0:T(8,128)S(1)}, f32[2,1728,128]{2,1,0:T(8,128)S(1)}) custom-call(s32[4]{0:T(128)S(1)} %copy-done.11, f32[4]{0:T(128)S(1)} %copy-done.13, f32[4]{0:T(128)S(1)} %collective-permute-done.2.refs_1_, f32[4]{0:T(128)S(1)} %collective-permute-done.3.refs_2_, f32[4]{0:T(128)S(1)} %collective-permute-done.4.refs_3_, ...), custom_call_target="tpu_custom_call" | custom-call | flops 7077888000 | bytes 3538944 | tf_op jit(solution)/shard_map/misfit/pallas_call | solution.py:537
  63.7 3.7 %collective-permute-done.5.other = f32[2,1728,128]{2,1,0:T(8,128)S(1)} collective-permute-done((f32[2,1728,128]{2,1,0:T(8,128)S(1)}, f32[2,1728,128]{2,1,0:T(8,128)S(1)}, u32[]{:S(2)}, u32[]{:S(2)}) %collective-permute-start.5) | collective-permute-done | bytes 1769504 | tf_op jit(solution)/shard_map/ppermute | solution.py:1062
  67.8 1.6 %collective-permute-start.6 = (bf16[2160,128]{1,0:T(8,128)(2,1)S(1)}, bf16[2160,128]{1,0:T(8,128)(2,1)S(1)}, u32[]{:S(2)}, u32[]{:S(2)}) collective-permute-start(bf16[2160,128]{1,0:T(8,128)(2,1)S(1)} %bitcast.19), channel_id=1, source_target_pairs={{0,2},{1,3},{2,0},{3,1},{4,6},{5,7},{6,4},{7,5},{8,10},{9,11},{10,... | collective-permute-start | bytes 1658888 | tf_op jit(solution)/shard_map/ppermute | solution.py:1066
  69.4 14.2 %misfit.3 = (f32[2,1728,128]{2,1,0:T(8,128)S(1)}, f32[2,1728,128]{2,1,0:T(8,128)S(1)}) custom-call(s32[4]{0:T(128)S(1)} %copy-done.11, f32[4]{0:T(128)S(1)} %copy-done.13, f32[4]{0:T(128)S(1)} %collective-permute-done.2.refs_1_, f32[4]{0:T(128)S(1)} %collective-permute-done.3.refs_2_, f32[4]{0:T(128)S(1)} %collective-permute-done.4.refs_3_, ...), custom_call_target="tpu_custom_call" | custom-call | flops 7077888000 | bytes 3538944 | tf_op jit(solution)/shard_map/misfit/pallas_call | solution.py:537
  83.7 3.7 %collective-permute-done.7.other = f32[2,1728,128]{2,1,0:T(8,128)S(1)} collective-permute-done((f32[2,1728,128]{2,1,0:T(8,128)S(1)}, f32[2,1728,128]{2,1,0:T(8,128)S(1)}, u32[]{:S(2)}, u32[]{:S(2)}) %collective-permute-start.7) | collective-permute-done | bytes 1769504 | tf_op jit(solution)/shard_map/ppermute | solution.py:1062
  87.9 0.6 collective-permute-start.8
  88.4 14.1 %collective-permute-done.8.refs_3_ = bf16[2160,128]{1,0:T(8,128)(2,1)S(1)} collective-permute-done((bf16[2160,128]{1,0:T(8,128)(2,1)S(1)}, bf16[2160,128]{1,0:T(8,128)(2,1)S(1)}, u32[]{:S(2)}, u32[]{:S(2)}) %collective-permute-start.8) | collective-permute-done | bytes 552992 | tf_op jit(solution)/shard_map/ppermute | solution.py:1066
  102.6 4.4 %solve.1 = (f32[12,288,128]{2,1,0:T(8,128)S(1)}, f32[4,288,128]{2,1,0:T(8,128)S(1)}, f32[288,128]{1,0:T(8,128)S(1)}) custom-call(s32[4]{0:T(128)S(1)} %copy-done.11, f32[288,128]{1,0:T(8,128)S(1)} %copy-done.2, f32[4,128]{1,0:T(4,128)S(1)} %copy-done.12, f32[1728,128]{1,0:T(8,128)S(1)} %get-tuple-element.36.refs_0_, ...), custom_call_target="tpu_custom_call" | custom-call | flops 764411904 | bytes 7077888 | tf_op jit(solution)/shard_map/solve/pallas_call | solution.py:751
  107.0 0.7 collective-permute-start.11
  107.6 1.4 collective-permute-start.9
  109.1 1.2 collective-permute-start.10
  110.3 7.5 %collective-permute-done.10.refs_2_ = bf16[288,128]{1,0:T(8,128)(2,1)S(1)} collective-permute-done((bf16[288,128]{1,0:T(8,128)(2,1)S(1)}, bf16[288,128]{1,0:T(8,128)(2,1)S(1)}, u32[]{:S(2)}, u32[]{:S(2)}) %collective-permute-start.10) | collective-permute-done | bytes 73760 | tf_op jit(solution)/shard_map/ppermute | solution.py:1084
  117.8 4.8 %finish.1 = (f32[864,128]{1,0:T(8,128)S(1)}, f32[864,128]{1,0:T(8,128)S(1)}, bf16[1296,128]{1,0:T(8,128)(2,1)S(1)}, bf16[1296,128]{1,0:T(8,128)(2,1)S(1)}) custom-call(s32[4]{0:T(128)S(1)} %copy-done.11, f32[288,128]{1,0:T(8,128)S(1)} %copy-done.2, f32[4,128]{1,0:T(4,128)S(1)} %copy-done.12, f32[12,288,128]{2,1,0:T(8,128)S(1)} %get-tuple-element.48.local, ...), custom_call_target="tpu_custom_call" | custom-call | flops 764411904 | bytes 7077888 | tf_op jit(solution)/shard_map/finish/pallas_call | solution.py:896
  122.7 0.6 collective-permute-start.13
  123.3 1.3 collective-permute-start.14
  124.6 8.8 %collective-permute-done.13.refs_2_.refs_3_ = bf16[1296,128]{1,0:T(8,128)(2,1)S(1)} collective-permute-done((bf16[1296,128]{1,0:T(8,128)(2,1)S(1)}, bf16[1296,128]{1,0:T(8,128)(2,1)S(1)}, u32[]{:S(2)}, u32[]{:S(2)}) %collective-permute-start.13) | collective-permute-done | bytes 331808 | tf_op jit(solution)/shard_map/ppermute | solution.py:1097
  133.4 6.2 %collective-permute-done.14.refs_4_.refs_5_ = bf16[1296,128]{1,0:T(8,128)(2,1)S(1)} collective-permute-done((bf16[1296,128]{1,0:T(8,128)(2,1)S(1)}, bf16[1296,128]{1,0:T(8,128)(2,1)S(1)}, u32[]{:S(2)}, u32[]{:S(2)}) %collective-permute-start.14) | collective-permute-done | bytes 331808 | tf_op jit(solution)/shard_map/ppermute | solution.py:1097
  139.6 3.5 %depth_cells.1 = f32[4,864,128]{2,1,0:T(8,128)} custom-call(s32[4]{0:T(128)S(1)} %copy-done.11, f32[864,128]{1,0:T(8,128)S(1)} %get-tuple-element.51.refs_0_, f32[864,128]{1,0:T(8,128)S(1)} %collective-permute-done.12.refs_1_, bf16[1296,128]{1,0:T(8,128)(2,1)S(1)} %collective-permute-done.13.refs_2_.refs_3_, ...), custom_call_target="tpu_custom_call" | custom-call | flops 1358954496 | bytes 3538944 | tf_op jit(solution)/shard_map/depth_cells/pallas_call | solution.py:982
  (46 shorter events, 2.1 us)
Async XLA Ops:
  3.2 20.4 %collective-permute-start = (bf16[7,288,128]{2,1,0:T(8,128)(2,1)S(1)}, bf16[7,288,128]{2,1,0:T(8,128)(2,1)S(1)}, u32[]{:S(2)}, u32[]{:S(2)}) collective-permute-start(bf16[7,288,128]{2,1,0:T(8,128)(2,1)S(1)} %pad_maximum_fusion), channel_id=1, source_target_pairs={{0,4},{4,8},{8,12},{1,5},{5,9},{9,13},{2,6},{6,10},{10,14},{3,7},{... | collective-permute-start | bytes 1548296 | tf_op jit(solution)/shard_map/ppermute | solution.py:1011
  8.2 15.4 %collective-permute-start.1 = (bf16[7,288,128]{2,1,0:T(8,128)(2,1)S(1)}, bf16[7,288,128]{2,1,0:T(8,128)(2,1)S(1)}, u32[]{:S(2)}, u32[]{:S(2)}) collective-permute-start(bf16[7,288,128]{2,1,0:T(8,128)(2,1)S(1)} %pad_maximum_fusion.1), channel_id=1, source_target_pairs={{4,0},{8,4},{12,8},{5,1},{9,5},{13,9},{6,2},{10,6},{14,10},{7,3},{... | collective-permute-start | bytes 1548296 | tf_op jit(solution)/shard_map/ppermute | solution.py:1015
  23.6 0.8 copy-start.14
  23.6 1.0 copy-start.15
  24.6 23.9 %copy-start = (bf16[512,512]{1,0:T(8,128)(2,1)S(1)}, bf16[512,512]{1,0:T(8,128)(2,1)}, u32[]{:S(2)}) copy-start(bf16[512,512]{1,0:T(8,128)(2,1)} %constant.34.clone.refs_10_) | copy-start | bytes 1572868
  24.6 23.9 %copy-start.1 = (bf16[512,512]{1,0:T(8,128)(2,1)S(1)}, bf16[512,512]{1,0:T(8,128)(2,1)}, u32[]{:S(2)}) copy-start(bf16[512,512]{1,0:T(8,128)(2,1)} %constant.33.clone.refs_9_) | copy-start | bytes 1572868
  24.6 23.9 %copy-start.11 = (s32[4]{0:T(128)S(1)}, s32[4]{0:T(128)}, u32[]{:S(2)}) copy-start(s32[4]{0:T(128)} %pad_add_fusion.meta) | copy-start | bytes 52
  38.3 6.2 %collective-permute-start.4 = (f32[4]{0:T(128)}, f32[4]{0:T(128)S(1)}, u32[]{:S(2)}, u32[]{:S(2)}) collective-permute-start(f32[4]{0:T(128)} %get-tuple-element.38.refs_0_), channel_id=1, source_target_pairs={{0,12},{4,0},{8,4},{12,8},{1,13},{5,1},{9,5},{13,9},{2,14},{6,2},{... | collective-permute-start | bytes 56 | tf_op jit(solution)/shard_map/ppermute | solution.py:1029
  43.0 4.7 %collective-permute-start.3 = (f32[4]{0:T(128)}, f32[4]{0:T(128)S(1)}, u32[]{:S(2)}, u32[]{:S(2)}) collective-permute-start(f32[4]{0:T(128)} %get-tuple-element.38.refs_0_), channel_id=1, source_target_pairs={{0,8},{4,12},{8,0},{12,4},{1,9},{5,13},{9,1},{13,5},{2,10},{6,14},... | collective-permute-start | bytes 56 | tf_op jit(solution)/shard_map/ppermute | solution.py:1029
  43.0 5.5 %collective-permute-start.2 = (f32[4]{0:T(128)}, f32[4]{0:T(128)S(1)}, u32[]{:S(2)}, u32[]{:S(2)}) collective-permute-start(f32[4]{0:T(128)} %get-tuple-element.38.refs_0_), channel_id=1, source_target_pairs={{0,4},{4,8},{8,12},{12,0},{1,5},{5,9},{9,13},{13,1},{2,6},{6,10},{... | collective-permute-start | bytes 56 | tf_op jit(solution)/shard_map/ppermute | solution.py:1029
  48.5 0.6 copy-start.13
  63.6 3.8 %collective-permute-start.5 = (f32[2,1728,128]{2,1,0:T(8,128)S(1)}, f32[2,1728,128]{2,1,0:T(8,128)S(1)}, u32[]{:S(2)}, u32[]{:S(2)}) collective-permute-start(f32[2,1728,128]{2,1,0:T(8,128)S(1)} %get-tuple-element.35), channel_id=1, source_target_pairs={{0,1},{1,0},{2,3},{3,2},{4,5},{5,4},{6,7},{7,6},{8,9},{9,8},{10,11... | collective-permute-start | bytes 5308424 | tf_op jit(solution)/shard_map/ppermute | solution.py:1062
  67.8 15.8 %collective-permute-start.6 = (bf16[2160,128]{1,0:T(8,128)(2,1)S(1)}, bf16[2160,128]{1,0:T(8,128)(2,1)S(1)}, u32[]{:S(2)}, u32[]{:S(2)}) collective-permute-start(bf16[2160,128]{1,0:T(8,128)(2,1)S(1)} %bitcast.19), channel_id=1, source_target_pairs={{0,2},{1,3},{2,0},{3,1},{4,6},{5,7},{6,4},{7,5},{8,10},{9,11},{10,... | collective-permute-start | bytes 1658888 | tf_op jit(solution)/shard_map/ppermute | solution.py:1066
  83.6 19.0 %copy-start.2 = (f32[288,128]{1,0:T(8,128)S(1)}, f32[288,128]{1,0:T(8,128)}, u32[]{:S(2)}) copy-start(f32[288,128]{1,0:T(8,128)} %constant.35.clone.across) | copy-start | bytes 442372
  83.6 18.9 %copy-start.7 = (bf16[288,144]{1,0:T(8,128)(2,1)S(1)}, bf16[288,144]{1,0:T(8,128)(2,1)}, u32[]{:S(2)}) copy-start(bf16[288,144]{1,0:T(8,128)(2,1)} %constant.40.clone.refs_7_) | copy-start | bytes 248836
  83.6 18.9 %copy-start.8 = (bf16[288,144]{1,0:T(8,128)(2,1)S(1)}, bf16[288,144]{1,0:T(8,128)(2,1)}, u32[]{:S(2)}) copy-start(bf16[288,144]{1,0:T(8,128)(2,1)} %constant.39.clone.refs_6_) | copy-start | bytes 248836
  83.6 18.9 %copy-start.9 = (bf16[288,144]{1,0:T(8,128)(2,1)S(1)}, bf16[288,144]{1,0:T(8,128)(2,1)}, u32[]{:S(2)}) copy-start(bf16[288,144]{1,0:T(8,128)(2,1)} %constant.38.clone.refs_5_) | copy-start | bytes 248836
  83.6 18.9 %copy-start.10 = (bf16[288,144]{1,0:T(8,128)(2,1)S(1)}, bf16[288,144]{1,0:T(8,128)(2,1)}, u32[]{:S(2)}) copy-start(bf16[288,144]{1,0:T(8,128)(2,1)} %constant.37.clone.refs_4_) | copy-start | bytes 248836
  83.6 18.9 %copy-start.12 = (f32[4,128]{1,0:T(4,128)S(1)}, f32[4,128]{1,0:T(4,128)}, u32[]{:S(2)}) copy-start(f32[4,128]{1,0:T(4,128)} %constant.36.clone.deep) | copy-start | bytes 6148
  83.7 3.8 %collective-permute-start.7 = (f32[2,1728,128]{2,1,0:T(8,128)S(1)}, f32[2,1728,128]{2,1,0:T(8,128)S(1)}, u32[]{:S(2)}, u32[]{:S(2)}) collective-permute-start(f32[2,1728,128]{2,1,0:T(8,128)S(1)} %get-tuple-element.44), channel_id=1, source_target_pairs={{0,1},{1,0},{2,3},{3,2},{4,5},{5,4},{6,7},{7,6},{8,9},{9,8},{10,11... | collective-permute-start | bytes 5308424 | tf_op jit(solution)/shard_map/ppermute | solution.py:1062
  87.4 30.4 %copy-start.5 = (bf16[288,288]{1,0:T(8,128)(2,1)S(1)}, bf16[288,288]{1,0:T(8,128)(2,1)}, u32[]{:S(2)}) copy-start(bf16[288,288]{1,0:T(8,128)(2,1)} %constant.42.clone.refs_5_) | copy-start | bytes 497668
  87.4 30.4 %copy-start.6 = (bf16[288,288]{1,0:T(8,128)(2,1)S(1)}, bf16[288,288]{1,0:T(8,128)(2,1)}, u32[]{:S(2)}) copy-start(bf16[288,288]{1,0:T(8,128)(2,1)} %constant.41.clone.refs_4_) | copy-start | bytes 497668
  87.9 14.6 %collective-permute-start.8 = (bf16[2160,128]{1,0:T(8,128)(2,1)S(1)}, bf16[2160,128]{1,0:T(8,128)(2,1)S(1)}, u32[]{:S(2)}, u32[]{:S(2)}) collective-permute-start(bf16[2160,128]{1,0:T(8,128)(2,1)S(1)} %bitcast.20), channel_id=1, source_target_pairs={{0,2},{1,3},{2,0},{3,1},{4,6},{5,7},{6,4},{7,5},{8,10},{9,11},{10,... | collective-permute-start | bytes 1658888 | tf_op jit(solution)/shard_map/ppermute | solution.py:1066
  102.6 37.0 %copy-start.3 = (bf16[512,512]{1,0:T(8,128)(2,1)S(1)}, bf16[512,512]{1,0:T(8,128)(2,1)}, u32[]{:S(2)}) copy-start(bf16[512,512]{1,0:T(8,128)(2,1)} %constant.44.clone.refs_7_) | copy-start | bytes 1572868
  102.6 37.0 %copy-start.4 = (bf16[512,512]{1,0:T(8,128)(2,1)S(1)}, bf16[512,512]{1,0:T(8,128)(2,1)}, u32[]{:S(2)}) copy-start(bf16[512,512]{1,0:T(8,128)(2,1)} %constant.43.clone.refs_6_) | copy-start | bytes 1572868
  107.0 10.8 %collective-permute-start.11 = (f32[288,128]{1,0:T(8,128)S(1)}, f32[288,128]{1,0:T(8,128)S(1)}, u32[]{:S(2)}, u32[]{:S(2)}) collective-permute-start(f32[288,128]{1,0:T(8,128)S(1)} %get-tuple-element.50.refs_0_), channel_id=1, source_target_pairs={{0,12},{4,0},{8,4},{12,8},{1,13},{5,1},{9,5},{13,9},{2,14},{6,2},{... | collective-permute-start | bytes 442376 | tf_op jit(solution)/shard_map/ppermute | solution.py:1084
  107.6 10.2 %collective-permute-start.9 = (f32[288,128]{1,0:T(8,128)S(1)}, f32[288,128]{1,0:T(8,128)S(1)}, u32[]{:S(2)}, u32[]{:S(2)}) collective-permute-start(f32[288,128]{1,0:T(8,128)S(1)} %get-tuple-element.50.refs_0_), channel_id=1, source_target_pairs={{0,4},{4,8},{8,12},{12,0},{1,5},{5,9},{9,13},{13,1},{2,6},{6,10},{... | collective-permute-start | bytes 442376 | tf_op jit(solution)/shard_map/ppermute | solution.py:1084
  109.1 8.7 %collective-permute-start.10 = (bf16[288,128]{1,0:T(8,128)(2,1)S(1)}, bf16[288,128]{1,0:T(8,128)(2,1)S(1)}, u32[]{:S(2)}, u32[]{:S(2)}) collective-permute-start(bf16[288,128]{1,0:T(8,128)(2,1)S(1)} %convert_element_type.3), channel_id=1, source_target_pairs={{0,8},{4,12},{8,0},{12,4},{1,9},{5,13},{9,1},{13,5},{2,10},{6,14},... | collective-permute-start | bytes 221192 | tf_op jit(solution)/shard_map/ppermute | solution.py:1084
  122.6 17.0 %collective-permute-start.12 = (f32[864,128]{1,0:T(8,128)S(1)}, f32[864,128]{1,0:T(8,128)S(1)}, u32[]{:S(2)}, u32[]{:S(2)}) collective-permute-start(f32[864,128]{1,0:T(8,128)S(1)} %get-tuple-element.52), channel_id=1, source_target_pairs={{0,1},{1,0},{2,3},{3,2},{4,5},{5,4},{6,7},{7,6},{8,9},{9,8},{10,11... | collective-permute-start | bytes 1327112 | tf_op jit(solution)/shard_map/ppermute | solution.py:1097
  122.7 10.7 %collective-permute-start.13 = (bf16[1296,128]{1,0:T(8,128)(2,1)S(1)}, bf16[1296,128]{1,0:T(8,128)(2,1)S(1)}, u32[]{:S(2)}, u32[]{:S(2)}) collective-permute-start(bf16[1296,128]{1,0:T(8,128)(2,1)S(1)} %get-tuple-element.53), channel_id=1, source_target_pairs={{0,2},{1,3},{2,0},{3,1},{4,6},{5,7},{6,4},{7,5},{8,10},{9,11},{10,... | collective-permute-start | bytes 995336 | tf_op jit(solution)/shard_map/ppermute | solution.py:1097
  123.3 16.3 %collective-permute-start.14 = (bf16[1296,128]{1,0:T(8,128)(2,1)S(1)}, bf16[1296,128]{1,0:T(8,128)(2,1)S(1)}, u32[]{:S(2)}, u32[]{:S(2)}) collective-permute-start(bf16[1296,128]{1,0:T(8,128)(2,1)S(1)} %get-tuple-element.54), channel_id=1, source_target_pairs={{0,3},{1,2},{2,1},{3,0},{4,7},{5,6},{6,5},{7,4},{8,11},{9,10},{10,... | collective-permute-start | bytes 995336 | tf_op jit(solution)/shard_map/ppermute | solution.py:1097

commit v5 on v4

--- a/solution.py
+++ b/solution.py
@@ -71,10 +71,13 @@
     return count
 
 
-def unrolled(start, stop, body, carry, most=4):
-    count = stop - start
-    factor = next(f for f in range(most, 0, -1) if count % f == 0)
-    return lax.fori_loop(start, stop, body, carry, unroll=factor)
+def unrolled(start, stop, body, carry, most=6):
+    factor = min(most, stop - start)
+    middle = start + (stop - start) // factor * factor
+    carry = lax.fori_loop(start, middle, body, carry, unroll=factor)
+    if middle < stop:
+        carry = lax.fori_loop(middle, stop, body, carry, unroll=stop - middle)
+    return carry
 
 
 def lane_index(shape):

time: 143 us -> 142 us (level)
  Pallas kernels: 68.7 us -> 66.9 us
  transfers between devices with their start and end apart: 15 -> 15, of which waited for: 9 -> 10; matrix products, arithmetic and copies ran while one was open for 0% -> 0% of each run, Pallas kernels for 19% -> 18%
where the time goes in v5:
time: 142 us; the launch traced here: 141 us
  Pallas kernels  66.9 us (47%)
  waiting for transfers between devices  49.3 us (35%)
  starting transfers between devices  18.8 us (13%)
  local copies, waits for them, and re-layouts  4.6 us (3%)
    pallas_call x2, Pallas kernels, misfit(): pl.pallas_call(functools.partial(misfit_kernel, rows, ny, first, size, pa...  28.6 us
    ppermute x3, waiting for transfers between devices, on_device(): arrived.append(lax.ppermute(pieces[k], 'test', turn))  15 us
    ppermute x2, waiting for transfers between devices, on_device(): fars += [lax.ppermute(far[k], 'test', hop) for k, hop in enumerate(hops)]  14.1 us
    pallas_call x1, Pallas kernels, moments(): pl.pallas_call(functools.partial(moments_kernel, rows, ny, count_x), out_...  13 us
    pallas_call x1, Pallas kernels, interior(): pl.pallas_call(functools.partial(interior_kernel, rows, ny, pieces), out_...  11.7 us
    ppermute x3, waiting for transfers between devices, on_device(): lax.ppermute(packed if near else packed.astype(BF16), 'space', turn)  7.54 us
    ppermute x2, waiting for transfers between devices, on_device(): other = lax.ppermute(other, 'test', other_core)  7.36 us
    ppermute x3, starting transfers between devices, on_device(): sums = [sums] + [lax.ppermute(sums, 'space', turn) for turn in turns]  5.08 us
  transfers between devices with their start and end apart: 15, of which 10 were waited for; matrix products, arithmetic and copies ran while one was open for 0% of the time, Pallas kernels for 18%

profile of v5, /device:TPU:0, one launch (start us, length us, event | category | flops | bytes accessed | tf_op | source)
XLA Modules:
  0.0 141.4 jit_solution(16238127416048563491)
XLA Ops:
  0.0 0.9 slice_bitcast_fusion.2
  0.9 1.1 fusion
  2.0 1.1 slice_bitcast_fusion
  3.2 5.0 %collective-permute-start = (bf16[7,288,128]{2,1,0:T(8,128)(2,1)S(1)}, bf16[7,288,128]{2,1,0:T(8,128)(2,1)S(1)}, u32[]{:S(2)}, u32[]{:S(2)}) collective-permute-start(bf16[7,288,128]{2,1,0:T(8,128)(2,1)S(1)} %pad_maximum_fusion), channel_id=1, source_target_pairs={{0,4},{4,8},{8,12},{1,5},{5,9},{9,13},{2,6},{6,10},{10,14},{3,7},{... | collective-permute-start | bytes 1548296 | tf_op jit(solution)/shard_map/ppermute | solution.py:1014
  8.2 1.3 collective-permute-start.1
  10.2 0.6 pad_add_fusion.meta
  10.8 11.7 %interior.1 = (f32[47976,128]{1,0:T(8,128)S(1)}, f32[31104,128]{1,0:T(8,128)S(1)}) custom-call(s32[4]{0:T(128)} %pad_add_fusion.meta, bf16[48,288,128]{2,1,0:T(8,128)(2,1)} %lk_in.1, bf16[48,288,128]{2,1,0:T(8,128)(2,1)} %bitcast.23), custom_call_target="tpu_custom_call" | custom-call | flops 8847360000 | bytes 7077888 | tf_op jit(solution)/shard_map/interior/pallas_call | solution.py:197
  22.5 0.8 collective-permute-done.1.ends_high.refs_8_
  23.3 0.8 copy-done.15
  24.1 13.0 %moments.1 = (f32[47976,128]{1,0:T(8,128)S(1)}, f32[31104,128]{1,0:T(8,128)S(1)}, f32[3,15984,128]{2,1,0:T(8,128)}, f32[4]{0:T(128)}) custom-call(s32[4]{0:T(128)} %pad_add_fusion.meta, s32[64]{0:T(128)} %bitcast.29, f32[64,128]{1,0:T(8,128)} %bitcast.28, bf16[7,288,128]{2,1,0:T(8,128)(2,1)} %copy-done.14, ...), custom_call_target="tpu_custom_call", output_to_operand_aliasing={{0}: (5, {}), {1}: (6, {})} | custom-call | flops 8847360000 | bytes 7077888 | tf_op jit(solution)/shard_map/moments/pallas_call | solution.py:323
  37.2 4.0 %collective-permute-start.4 = (f32[4]{0:T(128)}, f32[4]{0:T(128)S(1)}, u32[]{:S(2)}, u32[]{:S(2)}) collective-permute-start(f32[4]{0:T(128)} %get-tuple-element.38.refs_0_), channel_id=1, source_target_pairs={{0,12},{4,0},{8,4},{12,8},{1,13},{5,1},{9,5},{13,9},{2,14},{6,2},{... | collective-permute-start | bytes 56 | tf_op jit(solution)/shard_map/ppermute | solution.py:1032
  41.2 1.0 collective-permute-start.2
  42.7 3.1 %collective-permute-done.3.refs_2_ = f32[4]{0:T(128)S(1)} collective-permute-done((f32[4]{0:T(128)}, f32[4]{0:T(128)S(1)}, u32[]{:S(2)}, u32[]{:S(2)}) %collective-permute-start.3) | collective-permute-done | bytes 48 | tf_op jit(solution)/shard_map/ppermute | solution.py:1032
  45.9 0.9 collective-permute-done.2.refs_1_
  46.8 0.6 copy-done.13
  47.4 14.4 %misfit.2 = (f32[2,1728,128]{2,1,0:T(8,128)S(1)}, f32[2,1728,128]{2,1,0:T(8,128)S(1)}) custom-call(s32[4]{0:T(128)S(1)} %copy-done.11, f32[4]{0:T(128)S(1)} %copy-done.13, f32[4]{0:T(128)S(1)} %collective-permute-done.2.refs_1_, f32[4]{0:T(128)S(1)} %collective-permute-done.3.refs_2_, f32[4]{0:T(128)S(1)} %collective-permute-done.4.refs_3_, ...), custom_call_target="tpu_custom_call" | custom-call | flops 7077888000 | bytes 3538944 | tf_op jit(solution)/shard_map/misfit/pallas_call | solution.py:540
  61.9 3.7 %collective-permute-done.5.other = f32[2,1728,128]{2,1,0:T(8,128)S(1)} collective-permute-done((f32[2,1728,128]{2,1,0:T(8,128)S(1)}, f32[2,1728,128]{2,1,0:T(8,128)S(1)}, u32[]{:S(2)}, u32[]{:S(2)}) %collective-permute-start.5) | collective-permute-done | bytes 1769504 | tf_op jit(solution)/shard_map/ppermute | solution.py:1065
  66.1 1.6 %collective-permute-start.6 = (bf16[2160,128]{1,0:T(8,128)(2,1)S(1)}, bf16[2160,128]{1,0:T(8,128)(2,1)S(1)}, u32[]{:S(2)}, u32[]{:S(2)}) collective-permute-start(bf16[2160,128]{1,0:T(8,128)(2,1)S(1)} %bitcast.19), channel_id=1, source_target_pairs={{0,2},{1,3},{2,0},{3,1},{4,6},{5,7},{6,4},{7,5},{8,10},{9,11},{10,... | collective-permute-start | bytes 1658888 | tf_op jit(solution)/shard_map/ppermute | solution.py:1069
  67.7 14.2 %misfit.3 = (f32[2,1728,128]{2,1,0:T(8,128)S(1)}, f32[2,1728,128]{2,1,0:T(8,128)S(1)}) custom-call(s32[4]{0:T(128)S(1)} %copy-done.11, f32[4]{0:T(128)S(1)} %copy-done.13, f32[4]{0:T(128)S(1)} %collective-permute-done.2.refs_1_, f32[4]{0:T(128)S(1)} %collective-permute-done.3.refs_2_, f32[4]{0:T(128)S(1)} %collective-permute-done.4.refs_3_, ...), custom_call_target="tpu_custom_call" | custom-call | flops 7077888000 | bytes 3538944 | tf_op jit(solution)/shard_map/misfit/pallas_call | solution.py:540
  82.0 3.7 %collective-permute-done.7.other = f32[2,1728,128]{2,1,0:T(8,128)S(1)} collective-permute-done((f32[2,1728,128]{2,1,0:T(8,128)S(1)}, f32[2,1728,128]{2,1,0:T(8,128)S(1)}, u32[]{:S(2)}, u32[]{:S(2)}) %collective-permute-start.7) | collective-permute-done | bytes 1769504 | tf_op jit(solution)/shard_map/ppermute | solution.py:1065
  86.1 0.6 collective-permute-start.8
  86.7 14.1 %collective-permute-done.8.refs_3_ = bf16[2160,128]{1,0:T(8,128)(2,1)S(1)} collective-permute-done((bf16[2160,128]{1,0:T(8,128)(2,1)S(1)}, bf16[2160,128]{1,0:T(8,128)(2,1)S(1)}, u32[]{:S(2)}, u32[]{:S(2)}) %collective-permute-start.8) | collective-permute-done | bytes 552992 | tf_op jit(solution)/shard_map/ppermute | solution.py:1069
  100.8 4.4 %solve.1 = (f32[12,288,128]{2,1,0:T(8,128)S(1)}, f32[4,288,128]{2,1,0:T(8,128)S(1)}, f32[288,128]{1,0:T(8,128)S(1)}) custom-call(s32[4]{0:T(128)S(1)} %copy-done.11, f32[288,128]{1,0:T(8,128)S(1)} %copy-done.2, f32[4,128]{1,0:T(4,128)S(1)} %copy-done.12, f32[1728,128]{1,0:T(8,128)S(1)} %get-tuple-element.36.refs_0_, ...), custom_call_target="tpu_custom_call" | custom-call | flops 764411904 | bytes 7077888 | tf_op jit(solution)/shard_map/solve/pallas_call | solution.py:754
  105.2 0.7 collective-permute-start.11
  105.9 1.4 %collective-permute-start.9 = (f32[288,128]{1,0:T(8,128)S(1)}, f32[288,128]{1,0:T(8,128)S(1)}, u32[]{:S(2)}, u32[]{:S(2)}) collective-permute-start(f32[288,128]{1,0:T(8,128)S(1)} %get-tuple-element.50.refs_0_), channel_id=1, source_target_pairs={{0,4},{4,8},{8,12},{12,0},{1,5},{5,9},{9,13},{13,1},{2,6},{6,10},{... | collective-permute-start | bytes 442376 | tf_op jit(solution)/shard_map/ppermute | solution.py:1087
  107.3 1.2 collective-permute-start.10
  108.5 7.5 %collective-permute-done.10.refs_2_ = bf16[288,128]{1,0:T(8,128)(2,1)S(1)} collective-permute-done((bf16[288,128]{1,0:T(8,128)(2,1)S(1)}, bf16[288,128]{1,0:T(8,128)(2,1)S(1)}, u32[]{:S(2)}, u32[]{:S(2)}) %collective-permute-start.10) | collective-permute-done | bytes 73760 | tf_op jit(solution)/shard_map/ppermute | solution.py:1087
  116.1 4.8 %finish.1 = (f32[864,128]{1,0:T(8,128)S(1)}, f32[864,128]{1,0:T(8,128)S(1)}, bf16[1296,128]{1,0:T(8,128)(2,1)S(1)}, bf16[1296,128]{1,0:T(8,128)(2,1)S(1)}) custom-call(s32[4]{0:T(128)S(1)} %copy-done.11, f32[288,128]{1,0:T(8,128)S(1)} %copy-done.2, f32[4,128]{1,0:T(4,128)S(1)} %copy-done.12, f32[12,288,128]{2,1,0:T(8,128)S(1)} %get-tuple-element.48.local, ...), custom_call_target="tpu_custom_call" | custom-call | flops 764411904 | bytes 7077888 | tf_op jit(solution)/shard_map/finish/pallas_call | solution.py:899
  121.5 1.3 collective-permute-start.14
  122.8 8.8 %collective-permute-done.13.refs_2_.refs_3_ = bf16[1296,128]{1,0:T(8,128)(2,1)S(1)} collective-permute-done((bf16[1296,128]{1,0:T(8,128)(2,1)S(1)}, bf16[1296,128]{1,0:T(8,128)(2,1)S(1)}, u32[]{:S(2)}, u32[]{:S(2)}) %collective-permute-start.13) | collective-permute-done | bytes 331808 | tf_op jit(solution)/shard_map/ppermute | solution.py:1100
  131.6 6.2 %collective-permute-done.14.refs_4_.refs_5_ = bf16[1296,128]{1,0:T(8,128)(2,1)S(1)} collective-permute-done((bf16[1296,128]{1,0:T(8,128)(2,1)S(1)}, bf16[1296,128]{1,0:T(8,128)(2,1)S(1)}, u32[]{:S(2)}, u32[]{:S(2)}) %collective-permute-start.14) | collective-permute-done | bytes 331808 | tf_op jit(solution)/shard_map/ppermute | solution.py:1100
  137.8 3.5 %depth_cells.1 = f32[4,864,128]{2,1,0:T(8,128)} custom-call(s32[4]{0:T(128)S(1)} %copy-done.11, f32[864,128]{1,0:T(8,128)S(1)} %get-tuple-element.51.refs_0_, f32[864,128]{1,0:T(8,128)S(1)} %collective-permute-done.12.refs_1_, bf16[1296,128]{1,0:T(8,128)(2,1)S(1)} %collective-permute-done.13.refs_2_.refs_3_, ...), custom_call_target="tpu_custom_call" | custom-call | flops 1358954496 | bytes 3538944 | tf_op jit(solution)/shard_map/depth_cells/pallas_call | solution.py:985
  (46 shorter events, 2.4 us)
Async XLA Ops:
  3.2 19.3 %collective-permute-start = (bf16[7,288,128]{2,1,0:T(8,128)(2,1)S(1)}, bf16[7,288,128]{2,1,0:T(8,128)(2,1)S(1)}, u32[]{:S(2)}, u32[]{:S(2)}) collective-permute-start(bf16[7,288,128]{2,1,0:T(8,128)(2,1)S(1)} %pad_maximum_fusion), channel_id=1, source_target_pairs={{0,4},{4,8},{8,12},{1,5},{5,9},{9,13},{2,6},{6,10},{10,14},{3,7},{... | collective-permute-start | bytes 1548296 | tf_op jit(solution)/shard_map/ppermute | solution.py:1014
  8.2 15.1 %collective-permute-start.1 = (bf16[7,288,128]{2,1,0:T(8,128)(2,1)S(1)}, bf16[7,288,128]{2,1,0:T(8,128)(2,1)S(1)}, u32[]{:S(2)}, u32[]{:S(2)}) collective-permute-start(bf16[7,288,128]{2,1,0:T(8,128)(2,1)S(1)} %pad_maximum_fusion.1), channel_id=1, source_target_pairs={{4,0},{8,4},{12,8},{5,1},{9,5},{13,9},{6,2},{10,6},{14,10},{7,3},{... | collective-permute-start | bytes 1548296 | tf_op jit(solution)/shard_map/ppermute | solution.py:1018
  22.5 0.8 copy-start.14
  23.3 0.8 copy-start.15
  24.1 22.6 %copy-start = (bf16[512,512]{1,0:T(8,128)(2,1)S(1)}, bf16[512,512]{1,0:T(8,128)(2,1)}, u32[]{:S(2)}) copy-start(bf16[512,512]{1,0:T(8,128)(2,1)} %constant.34.clone.refs_10_) | copy-start | bytes 1572868
  24.1 22.6 %copy-start.1 = (bf16[512,512]{1,0:T(8,128)(2,1)S(1)}, bf16[512,512]{1,0:T(8,128)(2,1)}, u32[]{:S(2)}) copy-start(bf16[512,512]{1,0:T(8,128)(2,1)} %constant.33.clone.refs_9_) | copy-start | bytes 1572868
  24.1 22.6 %copy-start.11 = (s32[4]{0:T(128)S(1)}, s32[4]{0:T(128)}, u32[]{:S(2)}) copy-start(s32[4]{0:T(128)} %pad_add_fusion.meta) | copy-start | bytes 52
  37.2 5.6 %collective-permute-start.4 = (f32[4]{0:T(128)}, f32[4]{0:T(128)S(1)}, u32[]{:S(2)}, u32[]{:S(2)}) collective-permute-start(f32[4]{0:T(128)} %get-tuple-element.38.refs_0_), channel_id=1, source_target_pairs={{0,12},{4,0},{8,4},{12,8},{1,13},{5,1},{9,5},{13,9},{2,14},{6,2},{... | collective-permute-start | bytes 56 | tf_op jit(solution)/shard_map/ppermute | solution.py:1032
  41.2 4.7 %collective-permute-start.3 = (f32[4]{0:T(128)}, f32[4]{0:T(128)S(1)}, u32[]{:S(2)}, u32[]{:S(2)}) collective-permute-start(f32[4]{0:T(128)} %get-tuple-element.38.refs_0_), channel_id=1, source_target_pairs={{0,8},{4,12},{8,0},{12,4},{1,9},{5,13},{9,1},{13,5},{2,10},{6,14},... | collective-permute-start | bytes 56 | tf_op jit(solution)/shard_map/ppermute | solution.py:1032
  41.2 5.5 %collective-permute-start.2 = (f32[4]{0:T(128)}, f32[4]{0:T(128)S(1)}, u32[]{:S(2)}, u32[]{:S(2)}) collective-permute-start(f32[4]{0:T(128)} %get-tuple-element.38.refs_0_), channel_id=1, source_target_pairs={{0,4},{4,8},{8,12},{12,0},{1,5},{5,9},{9,13},{13,1},{2,6},{6,10},{... | collective-permute-start | bytes 56 | tf_op jit(solution)/shard_map/ppermute | solution.py:1032
  46.8 0.6 copy-start.13
  61.8 3.8 %collective-permute-start.5 = (f32[2,1728,128]{2,1,0:T(8,128)S(1)}, f32[2,1728,128]{2,1,0:T(8,128)S(1)}, u32[]{:S(2)}, u32[]{:S(2)}) collective-permute-start(f32[2,1728,128]{2,1,0:T(8,128)S(1)} %get-tuple-element.35), channel_id=1, source_target_pairs={{0,1},{1,0},{2,3},{3,2},{4,5},{5,4},{6,7},{7,6},{8,9},{9,8},{10,11... | collective-permute-start | bytes 5308424 | tf_op jit(solution)/shard_map/ppermute | solution.py:1065
  66.1 15.8 %collective-permute-start.6 = (bf16[2160,128]{1,0:T(8,128)(2,1)S(1)}, bf16[2160,128]{1,0:T(8,128)(2,1)S(1)}, u32[]{:S(2)}, u32[]{:S(2)}) collective-permute-start(bf16[2160,128]{1,0:T(8,128)(2,1)S(1)} %bitcast.19), channel_id=1, source_target_pairs={{0,2},{1,3},{2,0},{3,1},{4,6},{5,7},{6,4},{7,5},{8,10},{9,11},{10,... | collective-permute-start | bytes 1658888 | tf_op jit(solution)/shard_map/ppermute | solution.py:1069
  81.8 19.0 %copy-start.2 = (f32[288,128]{1,0:T(8,128)S(1)}, f32[288,128]{1,0:T(8,128)}, u32[]{:S(2)}) copy-start(f32[288,128]{1,0:T(8,128)} %constant.35.clone.across) | copy-start | bytes 442372
  81.8 18.9 %copy-start.7 = (bf16[288,144]{1,0:T(8,128)(2,1)S(1)}, bf16[288,144]{1,0:T(8,128)(2,1)}, u32[]{:S(2)}) copy-start(bf16[288,144]{1,0:T(8,128)(2,1)} %constant.40.clone.refs_7_) | copy-start | bytes 248836
  81.8 18.9 %copy-start.8 = (bf16[288,144]{1,0:T(8,128)(2,1)S(1)}, bf16[288,144]{1,0:T(8,128)(2,1)}, u32[]{:S(2)}) copy-start(bf16[288,144]{1,0:T(8,128)(2,1)} %constant.39.clone.refs_6_) | copy-start | bytes 248836
  81.9 18.9 %copy-start.9 = (bf16[288,144]{1,0:T(8,128)(2,1)S(1)}, bf16[288,144]{1,0:T(8,128)(2,1)}, u32[]{:S(2)}) copy-start(bf16[288,144]{1,0:T(8,128)(2,1)} %constant.38.clone.refs_5_) | copy-start | bytes 248836
  81.9 18.9 %copy-start.10 = (bf16[288,144]{1,0:T(8,128)(2,1)S(1)}, bf16[288,144]{1,0:T(8,128)(2,1)}, u32[]{:S(2)}) copy-start(bf16[288,144]{1,0:T(8,128)(2,1)} %constant.37.clone.refs_4_) | copy-start | bytes 248836
  81.9 18.9 %copy-start.12 = (f32[4,128]{1,0:T(4,128)S(1)}, f32[4,128]{1,0:T(4,128)}, u32[]{:S(2)}) copy-start(f32[4,128]{1,0:T(4,128)} %constant.36.clone.deep) | copy-start | bytes 6148
  81.9 3.8 %collective-permute-start.7 = (f32[2,1728,128]{2,1,0:T(8,128)S(1)}, f32[2,1728,128]{2,1,0:T(8,128)S(1)}, u32[]{:S(2)}, u32[]{:S(2)}) collective-permute-start(f32[2,1728,128]{2,1,0:T(8,128)S(1)} %get-tuple-element.44), channel_id=1, source_target_pairs={{0,1},{1,0},{2,3},{3,2},{4,5},{5,4},{6,7},{7,6},{8,9},{9,8},{10,11... | collective-permute-start | bytes 5308424 | tf_op jit(solution)/shard_map/ppermute | solution.py:1065
  85.7 30.4 %copy-start.5 = (bf16[288,288]{1,0:T(8,128)(2,1)S(1)}, bf16[288,288]{1,0:T(8,128)(2,1)}, u32[]{:S(2)}) copy-start(bf16[288,288]{1,0:T(8,128)(2,1)} %constant.42.clone.refs_5_) | copy-start | bytes 497668
  85.7 30.4 %copy-start.6 = (bf16[288,288]{1,0:T(8,128)(2,1)S(1)}, bf16[288,288]{1,0:T(8,128)(2,1)}, u32[]{:S(2)}) copy-start(bf16[288,288]{1,0:T(8,128)(2,1)} %constant.41.clone.refs_4_) | copy-start | bytes 497668
  86.1 14.6 %collective-permute-start.8 = (bf16[2160,128]{1,0:T(8,128)(2,1)S(1)}, bf16[2160,128]{1,0:T(8,128)(2,1)S(1)}, u32[]{:S(2)}, u32[]{:S(2)}) collective-permute-start(bf16[2160,128]{1,0:T(8,128)(2,1)S(1)} %bitcast.20), channel_id=1, source_target_pairs={{0,2},{1,3},{2,0},{3,1},{4,6},{5,7},{6,4},{7,5},{8,10},{9,11},{10,... | collective-permute-start | bytes 1658888 | tf_op jit(solution)/shard_map/ppermute | solution.py:1069
  100.8 37.0 %copy-start.3 = (bf16[512,512]{1,0:T(8,128)(2,1)S(1)}, bf16[512,512]{1,0:T(8,128)(2,1)}, u32[]{:S(2)}) copy-start(bf16[512,512]{1,0:T(8,128)(2,1)} %constant.44.clone.refs_7_) | copy-start | bytes 1572868
  100.8 37.0 %copy-start.4 = (bf16[512,512]{1,0:T(8,128)(2,1)S(1)}, bf16[512,512]{1,0:T(8,128)(2,1)}, u32[]{:S(2)}) copy-start(bf16[512,512]{1,0:T(8,128)(2,1)} %constant.43.clone.refs_6_) | copy-start | bytes 1572868
  105.2 10.8 %collective-permute-start.11 = (f32[288,128]{1,0:T(8,128)S(1)}, f32[288,128]{1,0:T(8,128)S(1)}, u32[]{:S(2)}, u32[]{:S(2)}) collective-permute-start(f32[288,128]{1,0:T(8,128)S(1)} %get-tuple-element.50.refs_0_), channel_id=1, source_target_pairs={{0,12},{4,0},{8,4},{12,8},{1,13},{5,1},{9,5},{13,9},{2,14},{6,2},{... | collective-permute-start | bytes 442376 | tf_op jit(solution)/shard_map/ppermute | solution.py:1087
  105.9 10.2 %collective-permute-start.9 = (f32[288,128]{1,0:T(8,128)S(1)}, f32[288,128]{1,0:T(8,128)S(1)}, u32[]{:S(2)}, u32[]{:S(2)}) collective-permute-start(f32[288,128]{1,0:T(8,128)S(1)} %get-tuple-element.50.refs_0_), channel_id=1, source_target_pairs={{0,4},{4,8},{8,12},{12,0},{1,5},{5,9},{9,13},{13,1},{2,6},{6,10},{... | collective-permute-start | bytes 442376 | tf_op jit(solution)/shard_map/ppermute | solution.py:1087
  107.3 8.7 %collective-permute-start.10 = (bf16[288,128]{1,0:T(8,128)(2,1)S(1)}, bf16[288,128]{1,0:T(8,128)(2,1)S(1)}, u32[]{:S(2)}, u32[]{:S(2)}) collective-permute-start(bf16[288,128]{1,0:T(8,128)(2,1)S(1)} %convert_element_type.3), channel_id=1, source_target_pairs={{0,8},{4,12},{8,0},{12,4},{1,9},{5,13},{9,1},{13,5},{2,10},{6,14},... | collective-permute-start | bytes 221192 | tf_op jit(solution)/shard_map/ppermute | solution.py:1087
  120.9 17.0 %collective-permute-start.12 = (f32[864,128]{1,0:T(8,128)S(1)}, f32[864,128]{1,0:T(8,128)S(1)}, u32[]{:S(2)}, u32[]{:S(2)}) collective-permute-start(f32[864,128]{1,0:T(8,128)S(1)} %get-tuple-element.52), channel_id=1, source_target_pairs={{0,1},{1,0},{2,3},{3,2},{4,5},{5,4},{6,7},{7,6},{8,9},{9,8},{10,11... | collective-permute-start | bytes 1327112 | tf_op jit(solution)/shard_map/ppermute | solution.py:1100
  121.0 10.7 %collective-permute-start.13 = (bf16[1296,128]{1,0:T(8,128)(2,1)S(1)}, bf16[1296,128]{1,0:T(8,128)(2,1)S(1)}, u32[]{:S(2)}, u32[]{:S(2)}) collective-permute-start(bf16[1296,128]{1,0:T(8,128)(2,1)S(1)} %get-tuple-element.53), channel_id=1, source_target_pairs={{0,2},{1,3},{2,0},{3,1},{4,6},{5,7},{6,4},{7,5},{8,10},{9,11},{10,... | collective-permute-start | bytes 995336 | tf_op jit(solution)/shard_map/ppermute | solution.py:1100
  121.5 16.3 %collective-permute-start.14 = (bf16[1296,128]{1,0:T(8,128)(2,1)S(1)}, bf16[1296,128]{1,0:T(8,128)(2,1)S(1)}, u32[]{:S(2)}, u32[]{:S(2)}) collective-permute-start(bf16[1296,128]{1,0:T(8,128)(2,1)S(1)} %get-tuple-element.54), channel_id=1, source_target_pairs={{0,3},{1,2},{2,1},{3,0},{4,7},{5,6},{6,5},{7,4},{8,11},{9,10},{10,... | collective-permute-start | bytes 995336 | tf_op jit(solution)/shard_map/ppermute | solution.py:1100
